TPU v7x, 32 devices: a whole 2x2x4 slice. The times are simulated.
32 devices in a mesh: group: 2 (over y), expert: 4 (over z), dp: 4 (over x, core).
Axes of the slice: x: 2, y: 2, z: 4, core: 2. Of those that a mesh axis runs over, the one named last changes fastest.
Arguments:
- tokens: bfloat16 [256, 4096], P(('group', 'expert', 'dp')), parts along dimension 0, may hold values from -6 to 6
- routing: int32 [256, 8], P(('group', 'expert', 'dp')), parts along dimension 0, may hold values from 0 to 127, as said below
- gate_quantized: int32 [256, 8], P(('group', 'expert', 'dp')), parts along dimension 0, may hold values from 1 to 32767
- tenant: int32 [256], P(('group', 'expert', 'dp')), parts along dimension 0, may hold values from 0 to 23
- tenant_page_lookup: int32 [4, 24], replicated, may hold values from 0 to 23, each once within a row
- gate_weight: bfloat16 [4, 4096, 1024], P('expert', None, 'dp'), may hold values from -0.09375 to 0.09375
- up_projection: bfloat16 [4, 4096, 1024], P('expert', None, 'dp'), may hold values from -0.09375 to 0.09375
- down_weight: bfloat16 [4, 1024, 4096], P('expert', None, 'dp'), may hold values from -0.1875 to 0.1875
- adapter_shrink: bfloat16 [4, 24, 16, 4096], P('expert', 'dp'), may hold values from -0.09375 to 0.09375
- adapter_expand: bfloat16 [4, 24, 16, 1024], P('expert', 'dp'), may hold values from -1.5 to 1.5
Outputs:
- mixed_out: bfloat16 [256, 4096], P(('group', 'expert', 'dp')), parts along dimension 0
There are 2 independent parts, one for each index of `group`. A program takes and returns all parts, laid end to end along the dimension named above; an argument that names none is the same for every part. Nothing has to cross between parts.
Inputs may be any that keep to these rules, and one draw needn't show every extreme that they name: `routing`: each row names 8 different experts. Among the 8 tokens of one device no expert is named more than 2 times, and in every draw some expert below 4 is named exactly 2 times by the tokens of every device. `tenant_page_lookup`: row e gives every tenant a different page of expert e's pool.
All inputs are finite; a program needn't handle non-finite values.
Results may differ from a plain program's by a relative error of at most 0.0061.
Values may be sent and summed in bfloat16 or wider, within the bound.
No kernel may reach another device: no remote copies, remote signals or barrier semaphores. Data moves between devices by JAX's collectives and lax.ppermute only.
A program may use at most 64 MiB of HBM per device.

v0:
```python
import jax
import jax.numpy as jnp
from jax import lax
from jax.sharding import PartitionSpec as P


def slot_tables(routing, experts, capacity):
    expert_ids = jnp.arange(experts, dtype=jnp.int32)
    matches = routing[:, :, None] == expert_ids[None, None, :]
    assign = jnp.sum(matches.astype(jnp.int32), axis=1)
    slot_rank = jnp.cumsum(assign, axis=0) - assign
    scale_levels = jnp.arange(capacity, dtype=jnp.int32)
    placing = (assign.T[:, None, :] == 1) & (slot_rank.T[:, None, :] == scale_levels[None, :, None])
    return (matches, slot_rank, placing)


def per_device(
    tokens,
    routing,
    gate_quantized,
    tenant,
    tenant_page_lookup,
    gate_weight,
    up_projection,
    down_weight,
    adapter_shrink,
    adapter_expand,
):
    tok_count, model_width = tokens.shape
    experts, tenants = tenant_page_lookup.shape
    capacity = tok_count // 4
    rank_extent = adapter_shrink.shape[2]
    part_width = down_weight.shape[2]
    my_expert = lax.axis_index("expert")
    matches, slot_rank, placing = slot_tables(routing, experts, capacity)
    send_rows = jnp.einsum(
        "ect,td->ecd", placing.astype(jnp.bfloat16), tokens, preferred_element_type=jnp.float32
    ).astype(jnp.bfloat16)
    send_ten = jnp.sum(placing.astype(jnp.int32) * (tenant[None, None, :] + 1), axis=2)
    got_rows, got_ten = (
        lax.all_to_all(send_rows, "expert", split_axis=0, concat_axis=0, tiled=True),
        lax.all_to_all(send_ten, "expert", split_axis=0, concat_axis=0, tiled=True),
    )
    slot_rows, slot_ten = (
        lax.all_gather(got_rows[None], "dp", axis=0, tiled=True),
        lax.all_gather(got_ten[None], "dp", axis=0, tiled=True),
    )
    block_shape = slot_rows.shape[:3]
    slot_count = block_shape[0] * block_shape[1] * block_shape[2]
    slot_input = slot_rows.reshape(slot_count, model_width)
    slot_tenant = slot_ten.reshape(slot_count)
    page_row = lax.dynamic_index_in_dim(tenant_page_lookup, my_expert, 0, keepdims=False)
    tenant_ids = jnp.arange(tenants, dtype=jnp.int32)
    tenant_hot = slot_tenant[:, None] == tenant_ids[None, :] + 1
    slot_page = jnp.sum(jnp.where(tenant_hot, page_row[None, :], 0), axis=1)
    occupied = slot_tenant > 0
    page_pick = ((slot_page[:, None] == tenant_ids[None, :]) & occupied[:, None]).astype(
        jnp.float32
    )
    partial_terms = lax.all_gather(adapter_shrink, "dp", axis=1, tiled=True)
    page_count = partial_terms.shape[1]
    flat_pages = partial_terms.reshape(page_count * rank_extent, model_width)
    products = lax.dot_general(
        slot_input, flat_pages, (((1,), (1,)), ((), ())), preferred_element_type=jnp.float32
    )
    shrink_result = jnp.sum(
        page_pick[:, :, None] * products.reshape(slot_count, page_count, rank_extent), axis=1
    )
    shrink_low = shrink_result.astype(jnp.bfloat16)
    expand_every_page = lax.all_to_all(
        adapter_expand, "dp", split_axis=3, concat_axis=1, tiled=True
    )[0]
    hidden_part = expand_every_page.shape[2]
    expand_matrix = expand_every_page.reshape(tenants * rank_extent, hidden_part)
    spread_rows = (page_pick[:, :, None] * shrink_low.astype(jnp.float32)[:, None, :]).astype(
        jnp.bfloat16
    )
    spread_rows = spread_rows.reshape(slot_count, tenants * rank_extent)
    adapter_update = jnp.dot(spread_rows, expand_matrix, preferred_element_type=jnp.float32)
    gate_act = jnp.dot(slot_input, gate_weight[0], preferred_element_type=jnp.float32)
    up_activation = (
        jnp.dot(slot_input, up_projection[0], preferred_element_type=jnp.float32) + adapter_update
    )
    hidden = (jax.nn.silu(gate_act) * up_activation).astype(jnp.bfloat16)
    weights = down_weight[0]
    expert_out = jnp.dot(
        lax.all_gather(hidden, "dp", axis=1, tiled=True),
        weights,
        preferred_element_type=jnp.float32,
    )
    expert_out = expert_out.astype(jnp.bfloat16).reshape(block_shape + (part_width,))
    home_rows = lax.all_to_all(expert_out, "dp", split_axis=0, concat_axis=3, tiled=True)
    back_rows = lax.all_to_all(home_rows, "expert", split_axis=1, concat_axis=0, tiled=True)
    back_rows = back_rows.reshape(experts * capacity, model_width)
    chosen_rank = jnp.sum(jnp.where(matches, slot_rank[:, None, :], 0), axis=2)
    inside = routing < experts
    flat_index = routing * capacity + chosen_rank
    slot_ids = jnp.arange(experts * capacity, dtype=jnp.int32)
    row_picks = ((flat_index[:, :, None] == slot_ids[None, None, :]) & inside[:, :, None]).astype(
        jnp.bfloat16
    )
    picked = jnp.einsum("tkm,md->tkd", row_picks, back_rows, preferred_element_type=jnp.float32)
    mix_coef = jnp.where(inside, gate_quantized.astype(jnp.float32) / 32768.0, jnp.float32(0.0))
    mixed_out = jnp.sum(mix_coef[:, :, None] * picked, axis=1)
    return mixed_out.astype(jnp.bfloat16)


def solution(mesh):
    return jax.shard_map(
        per_device,
        mesh=mesh,
        in_specs=(
            P(("group", "expert", "dp"), None),
            P(("group", "expert", "dp"), None),
            P(("group", "expert", "dp"), None),
            P(("group", "expert", "dp")),
            P(),
            P("expert", None, "dp"),
            P("expert", None, "dp"),
            P("expert", None, "dp"),
            P("expert", "dp", None, None),
            P("expert", "dp", None, None),
        ),
        out_specs=P(("group", "expert", "dp"), None),
        check_vma=False,
    )
```

profile of v0, /device:TPU:0, one launch (start us, length us, event | category | flops | bytes accessed | tf_op | source)
XLA Modules:
  0.0 94.0 jit_solution(14872100671156031645)
XLA Ops:
  6.5 0.7 all-gather.4.cloned.1.call-update
  7.3 0.8 convert_reduce_fusion
  8.1 0.2 reduce_window_sum.11
  8.3 0.7 broadcast_add_fusion
  9.1 0.7 copy.39
  9.8 6.3 %all-to-all-start.1 = ((s32[4,1,2]{2,1,0:T(1,128)}), s32[4,1,2]{2,1,0:T(1,128)S(1)}, u32[]{:S(2)}, u32[]{:S(2)}) async-start(s32[4,1,2]{2,1,0:T(1,128)} %copy.39), calls=%async_computation.1 | async-start | bytes 4096 | tf_op jit(solution)/shard_map/all_to_all | solution.py:42
  16.1 1.0 %convolution_convert_fusion = bf16[4,2,4096]{2,0,1:T(4,128)(2,1)S(1)} fusion(bf16[8,4096]{1,0:T(8,128)(2,1)} %param.10, s32[4,8]{1,0:T(4,128)S(1)} %bitcast.58, pred[4,8]{1,0:T(4,128)(4,1)S(1)} %compare_bitcast_fusion), kind=kOutput, calls=%fused_computation.1 | convolution fusion | flops 557184 | bytes 131232 | tf_op jit(solution)/shard_map/ect,td->ecd/dot_general | solution.py:36
  17.1 0.7 copy.38
  17.8 3.3 %copy.43 = bf16[1,6,16,1024]{2,1,0,3:T(8,128)(2,1)} copy(bf16[1,6,16,1024]{3,2,1,0:T(8,128)(2,1)} %param.19) | data formatting | bytes 393216 | tf_op args[9]
  21.1 3.5 %reshape.122 = bf16[4,2,12288]{2,1,0:T(2,128)(2,1)} reshape(bf16[1024,1,6,16]{3,2,1,0:T(8,128)(2,1)} %bitcast.51) | data formatting | bytes 393216
  24.7 0.7 dynamic-slice_bitcast_fusion
  25.4 5.1 %all-to-all-start = ((bf16[4,2,4096]{2,1,0:T(2,128)(2,1)}), bf16[4,2,4096]{2,1,0:T(2,128)(2,1)S(1)}, u32[]{:S(2)}, u32[]{:S(2)}) async-start(bf16[4,2,4096]{2,1,0:T(2,128)(2,1)} %copy.38), calls=%async_computation | async-start | bytes 131072 | tf_op jit(solution)/shard_map/all_to_all | solution.py:41
  30.5 5.2 %all-gather.1 = s32[16,1,2]{2,1,0:T(1,128)S(1)} all-gather(s32[4,1,2]{2,1,0:T(1,128)S(1)} %all-to-all-done.1), channel_id=3, replica_groups=mesh['group'=2,'expert'=4,'dp'=4] {'dp'}, dimensions={0}, use_global_device_ids=true | all-gather | bytes 160 | tf_op jit(solution)/shard_map/all_gather | solution.py:46
  35.6 0.5 broadcast.74
  36.1 0.6 reduce.3
  36.9 3.4 %all-to-all-start.2 = ((bf16[4,2,12288]{2,1,0:T(2,128)(2,1)}), bf16[4,2,12288]{2,1,0:T(2,128)(2,1)S(1)}, u32[]{:S(2)}, u32[]{:S(2)}) async-start(bf16[4,2,12288]{2,1,0:T(2,128)(2,1)} %reshape.122), calls=%async_computation.2 | async-start | bytes 393216 | tf_op jit(solution)/shard_map/all_to_all | solution.py:70
  40.3 7.5 %all-gather = bf16[16,2,4096]{2,1,0:T(2,128)(2,1)S(1)} all-gather(bf16[4,2,4096]{2,1,0:T(2,128)(2,1)S(1)} %all-to-all-done), channel_id=2, replica_groups=mesh['group'=2,'expert'=4,'dp'=4] {'dp'}, dimensions={0}, use_global_device_ids=true | all-gather | bytes 327680 | tf_op jit(solution)/shard_map/all_gather | solution.py:45
  48.1 2.2 %fusion.5 = f32[32,256]{1,0:T(8,128)S(1)} fusion(bf16[32,4096]{1,0:T(8,128)(2,1)S(1)} %reshape.101, bf16[1,4096,256]{2,1,0:T(8,128)(2,1)} %param.16), kind=kOutput, calls=%fused_computation.7 | convolution fusion | flops 67108864 | bytes 2392064 | tf_op jit(solution)/shard_map/dot_general | solution.py:82
  50.3 0.5 fusion.7
  50.8 2.9 %reshape.123 = bf16[1024,1,6,16]{3,2,1,0:T(8,128)(2,1)} reshape(bf16[4,2,12288]{2,1,0:T(2,128)(2,1)S(1)} %all-to-all-done.2) | data formatting | bytes 393216
  53.7 2.5 %copy.48 = bf16[1,6,16,4,256]{4,3,2,1,0:T(4,128)(2,1)S(1)} copy(bf16[1,6,16,4,256]{2,1,4,3,0:T(8,128)(2,1)} %bitcast.50) | data formatting | bytes 393216 | tf_op jit(solution)/shard_map/all_to_all | solution.py:70
  56.2 4.2 %fusion.16 = bf16[32,16]{0,1:T(8,128)(2,1)S(1)} fusion(bf16[32,4096,1]{1,0,2:T(8,128)(2,1)S(1)} %reshape.109, bf16[1,24,16,4096]{3,2,0,1:T(8,128)(2,1)} %all-gather.4.cloned.1.call-done, f32[32,24]{0,1:T(8,128)S(1)} %fusion.27), kind=kOutput, calls=%fused_computation.14 | convolution fusion | flops 100687360 | bytes 3411968 | tf_op jit(solution)/shard_map/dot_general | solution.py:63
  60.5 0.2 fusion.20
  60.7 5.3 %all_gather.15 = bf16[32,1024]{1,0:T(8,128)(2,1)S(1)} all-gather(bf16[32,256]{1,0:T(8,128)(2,1)S(1)} %fusion.20), channel_id=1, replica_groups=mesh['group'=2,'expert'=4,'dp'=4] {'dp'}, dimensions={1}, use_global_device_ids=true | all-gather | bytes 81920 | tf_op jit(solution)/shard_map/all_gather | solution.py:87
  66.0 0.5 fusion.13
  66.5 0.7 reshape.102
  67.1 3.3 %all-to-all-start.3 = ((bf16[4,4,2,1024]{3,2,1,0:T(2,128)(2,1)}), bf16[4,4,2,1024]{3,2,1,0:T(2,128)(2,1)S(1)}, u32[]{:S(2)}, u32[]{:S(2)}) async-start(bf16[4,4,2,1024]{3,2,1,0:T(2,128)(2,1)} %reshape.102), calls=%async_computation.3 | async-start | bytes 131072 | tf_op jit(solution)/shard_map/all_to_all | solution.py:92
  70.5 4.0 %all-to-all-done.3 = bf16[4,4,2,1024]{3,2,1,0:T(2,128)(2,1)S(1)} async-done(((bf16[4,4,2,1024]{3,2,1,0:T(2,128)(2,1)}), bf16[4,4,2,1024]{3,2,1,0:T(2,128)(2,1)S(1)}, u32[]{:S(2)}, u32[]{:S(2)}) %all-to-all-start.3) | async-done | bytes 65568 | tf_op jit(solution)/shard_map/all_to_all | solution.py:92
  74.5 0.7 copy.49
  75.2 5.1 %all-to-all-start.4 = ((bf16[1,4,2,4096]{3,2,0,1:T(2,128)(2,1)}), bf16[1,4,2,4096]{3,2,0,1:T(2,128)(2,1)S(1)}, u32[]{:S(2)}, u32[]{:S(2)}) async-start(bf16[1,4,2,4096]{3,2,0,1:T(2,128)(2,1)} %bitcast.16), calls=%async_computation.4 | async-start | bytes 131072 | tf_op jit(solution)/shard_map/all_to_all | solution.py:93
  80.3 5.7 %all-to-all-done.4 = bf16[1,4,2,4096]{3,2,0,1:T(2,128)(2,1)S(1)} async-done(((bf16[1,4,2,4096]{3,2,0,1:T(2,128)(2,1)}), bf16[1,4,2,4096]{3,2,0,1:T(2,128)(2,1)S(1)}, u32[]{:S(2)}, u32[]{:S(2)}) %all-to-all-start.4) | async-done | bytes 65568 | tf_op jit(solution)/shard_map/all_to_all | solution.py:93
  86.1 1.1 %fusion.9 = bf16[8,4096]{1,0:T(8,128)(2,1)} fusion(bf16[8,4096,1]{1,0,2:T(8,128)(2,1)S(1)} %reshape.110, f32[8,8]{1,0:T(8,128)S(1)} %get-tuple-element.5, s32[8,8]{1,0:T(8,128)S(1)} %multiply_add_fusion, pred[8,8]{1,0:T(8,128)(4,1)S(1)} %get-tuple-element.6), kind=kOutput, calls=%fused_computation.11 | convolution fusion | flops 4686848 | bytes 131648 | tf_op jit(solution)/shard_map/tkm,md->tkd/dot_general | solution.py:102
  (31 shorter events, 0.8 us)
Async XLA Ops:
  6.5 59.5 %copy-start = (bf16[1,1024,1024]{2,1,0:T(8,128)(2,1)S(1)}, bf16[1,1024,1024]{2,1,0:T(8,128)(2,1)}, u32[]{:S(2)}) copy-start(bf16[1,1024,1024]{2,1,0:T(8,128)(2,1)} %param.17) | copy-start | bytes 6291460
  6.5 49.7 %all-gather.4.cloned.1.call-start = ((), (), s32[]{:S(2)}) async-start(), calls=%async_computation.5 | async-start | bytes 3932160 | tf_op jit(solution)/shard_map/all_gather | solution.py:60
  9.8 15.6 %all-to-all-start.1 = ((s32[4,1,2]{2,1,0:T(1,128)}), s32[4,1,2]{2,1,0:T(1,128)S(1)}, u32[]{:S(2)}, u32[]{:S(2)}) async-start(s32[4,1,2]{2,1,0:T(1,128)} %copy.39), calls=%async_computation.1 | async-start | bytes 4096 | tf_op jit(solution)/shard_map/all_to_all | solution.py:42
  17.8 7.6 %copy-start.2 = (s32[8,8]{1,0:T(8,128)S(1)}, s32[8,8]{1,0:T(8,128)}, u32[]{:S(2)}) copy-start(s32[8,8]{1,0:T(8,128)} %param.11) | copy-start | bytes 772
  17.8 7.6 %copy-start.3 = (s32[8,8]{1,0:T(8,128)S(1)}, s32[8,8]{1,0:T(8,128)}, u32[]{:S(2)}) copy-start(s32[8,8]{1,0:T(8,128)} %param.12) | copy-start | bytes 772
  25.4 11.5 %all-to-all-start = ((bf16[4,2,4096]{2,1,0:T(2,128)(2,1)}), bf16[4,2,4096]{2,1,0:T(2,128)(2,1)S(1)}, u32[]{:S(2)}, u32[]{:S(2)}) async-start(bf16[4,2,4096]{2,1,0:T(2,128)(2,1)} %copy.38), calls=%async_computation | async-start | bytes 131072 | tf_op jit(solution)/shard_map/all_to_all | solution.py:41
  36.9 13.9 %all-to-all-start.2 = ((bf16[4,2,12288]{2,1,0:T(2,128)(2,1)}), bf16[4,2,12288]{2,1,0:T(2,128)(2,1)S(1)}, u32[]{:S(2)}, u32[]{:S(2)}) async-start(bf16[4,2,12288]{2,1,0:T(2,128)(2,1)} %reshape.122), calls=%async_computation.2 | async-start | bytes 393216 | tf_op jit(solution)/shard_map/all_to_all | solution.py:70
  48.0 2.2 %copy-start.1 = (bf16[1,4096,256]{2,1,0:T(8,128)(2,1)S(1)}, bf16[1,4096,256]{2,1,0:T(8,128)(2,1)}, u32[]{:S(2)}) copy-start(bf16[1,4096,256]{2,1,0:T(8,128)(2,1)} %param.15) | copy-start | bytes 6291460
  67.1 7.4 %all-to-all-start.3 = ((bf16[4,4,2,1024]{3,2,1,0:T(2,128)(2,1)}), bf16[4,4,2,1024]{3,2,1,0:T(2,128)(2,1)S(1)}, u32[]{:S(2)}, u32[]{:S(2)}) async-start(bf16[4,4,2,1024]{3,2,1,0:T(2,128)(2,1)} %reshape.102), calls=%async_computation.3 | async-start | bytes 131072 | tf_op jit(solution)/shard_map/all_to_all | solution.py:92
  75.2 10.8 %all-to-all-start.4 = ((bf16[1,4,2,4096]{3,2,0,1:T(2,128)(2,1)}), bf16[1,4,2,4096]{3,2,0,1:T(2,128)(2,1)S(1)}, u32[]{:S(2)}, u32[]{:S(2)}) async-start(bf16[1,4,2,4096]{3,2,0,1:T(2,128)(2,1)} %bitcast.16), calls=%async_computation.4 | async-start | bytes 131072 | tf_op jit(solution)/shard_map/all_to_all | solution.py:93
Sparse Core Ops, SparseCore 0:
  8.9 31.2 all-gather.3
where the time goes:
time: 94.8 us; the launch traced here: 94 us
  starting transfers between devices  23.2 us (24%)
  blocking collectives  18 us (19%)
  local copies, waits for them, and re-layouts  16.5 us (17%)
  between operations  13.6 us (14%)
  waiting for transfers between devices  10.5 us (11%)
  matrix products  9.7 us (10%)
  other arithmetic  2.63 us (3%)
    unnamed x11, local copies, waits for them, and re-layouts  9.81 us
    all_gather x1, blocking collectives, per_device(): lax.all_gather(got_rows[None], 'dp', axis=0, tiled=True)  7.55 us
    all_to_all x1, starting transfers between devices, per_device(): lax.all_to_all(send_ten, 'expert', split_axis=0, concat_axis=0, tiled=True)  6.32 us
    all_to_all x1, waiting for transfers between devices, per_device(): lax.all_to_all(home_rows, 'expert', split_axis=1, concat_axis=0, tiled=True)  5.74 us
    all_gather x1, blocking collectives, per_device(): lax.all_gather(hidden, 'dp', axis=1, tiled=True)  5.25 us
    all_gather x1, blocking collectives, per_device(): lax.all_gather(got_ten[None], 'dp', axis=0, tiled=True)  5.16 us
    all_to_all x1, starting transfers between devices, per_device(): lax.all_to_all(send_rows, 'expert', split_axis=0, concat_axis=0, tiled=True)  5.1 us
    all_to_all x1, starting transfers between devices, per_device(): lax.all_to_all(home_rows, 'expert', split_axis=1, concat_axis=0, tiled=True)  5.09 us
  transfers between devices with their start and end apart: 6, of which 2 were waited for; matrix products, arithmetic and copies ran while one was open for 23% of the time, Pallas kernels for 0%

commit v1 on v0

v1 whole, which is shorter than its diff:
```python
import jax
import jax.numpy as jnp
from jax import lax
from jax.sharding import PartitionSpec as P

BF = jnp.bfloat16
F32 = jnp.float32


def swap(x, axis, size, mask):
    return lax.ppermute(x, axis, [(i, i ^ mask) for i in range(size)])


def bits_of(size):
    return [1 << b for b in range(size.bit_length() - 1)]


def gather_order(size):
    order = [0]
    for mask in reversed(bits_of(size)):
        order = order + [q ^ mask for q in order]
    return order


def gather_rows(x, axis, size):
    x = x[None]
    for mask in reversed(bits_of(size)):
        x = jnp.concatenate([x, swap(x, axis, size, mask)], axis=0)
    return x


def exchange(x, axis, size, dim, order):
    for mask in bits_of(size):
        keep = [i for i in range(size) if not order[i] & mask]
        send = [order.index(order[i] ^ mask) for i in keep]
        kept = jnp.stack([lax.index_in_dim(x, i, dim, False) for i in keep], dim)
        sent = jnp.stack([lax.index_in_dim(x, i, dim, False) for i in send], dim)
        came = swap(sent, axis, size, mask)
        parts = [None] * size
        for j in range(size // 2):
            parts[keep[j]] = lax.index_in_dim(kept, j, dim, False)
            parts[send[j]] = lax.index_in_dim(came, j, dim, False)
        x = jnp.stack(parts, dim)
    return x


def build(mesh):
    n_exp, n_dp = mesh.shape["expert"], mesh.shape["dp"]
    order_e = list(range(n_exp))
    order_d = gather_order(n_dp)

    def per_device(
        tokens,
        routing,
        gate_quantized,
        tenant,
        tenant_page_lookup,
        gate_weight,
        up_projection,
        down_weight,
        adapter_shrink,
        adapter_expand,
    ):
        tok_count, width = tokens.shape
        experts, tenants = tenant_page_lookup.shape
        cap = tok_count // 4
        pages, rank = adapter_shrink.shape[1:3]
        hid = gate_weight.shape[2]
        part = down_weight.shape[2]
        mine = lax.axis_index("expert")
        col = lax.axis_index("dp")

        expand = gather_rows(
            adapter_expand.reshape(pages * rank, adapter_expand.shape[3]), "dp", n_dp
        ).reshape(n_dp * pages * rank, adapter_expand.shape[3])

        ids = jnp.arange(experts, dtype=jnp.int32) ^ mine
        matches = routing[:, :, None] == ids[None, None, :]
        assign = jnp.any(matches, axis=1)
        toks = jnp.arange(tok_count, dtype=jnp.int32)
        earlier = toks[:, None] > toks[None, :]
        slot_rank = jnp.sum((earlier[:, :, None] & assign[None, :, :]).astype(jnp.int32), axis=1)
        caps = jnp.arange(cap, dtype=jnp.int32)
        placing = assign[:, :, None] & (slot_rank[:, :, None] == caps[None, None, :])
        coef = jnp.sum(jnp.where(matches, gate_quantized[:, :, None].astype(F32) / 32768.0, 0.0), axis=1)
        mix = jnp.where(placing, coef[:, :, None], 0.0).reshape(tok_count, experts * cap)
        place = placing.reshape(tok_count, experts * cap)
        rows = lax.dot_general(
            place.astype(BF), tokens, (((0,), (0,)), ((), ())), preferred_element_type=F32
        ).astype(BF)
        hot = tenant[:, None] == jnp.arange(tenants, dtype=jnp.int32)[None, :]
        looked = jnp.sum(
            jnp.where(hot[:, None, :], tenant_page_lookup[None, :, :], 0), axis=2
        )
        looked = jnp.sum(
            jnp.where(
                jnp.arange(experts)[None, None, :] == ids[None, :, None], looked[:, None, :], 0
            ),
            axis=2,
        )
        slot_page = jnp.sum(jnp.where(placing, looked[:, :, None], 0), axis=0).reshape(-1)
        tail = jnp.broadcast_to(slot_page[:, None].astype(BF), (experts * cap, 128))
        sent = jnp.concatenate([rows, tail], axis=1).reshape(experts, cap, width + 128)

        got = exchange(sent, "expert", n_exp, 0, order_e)
        got = gather_rows(got, "dp", n_dp).reshape(-1, width + 128)
        slots = got[:, :width]
        page = got[:, width].astype(jnp.int32)

        gate = jnp.dot(slots, gate_weight[0], preferred_element_type=F32)
        up = jnp.dot(slots, up_projection[0], preferred_element_type=F32)
        prod = lax.dot_general(
            slots,
            adapter_shrink.reshape(pages * rank, width),
            (((1,), (1,)), ((), ())),
            preferred_element_type=F32,
        )
        page_of = col * pages + jnp.arange(pages * rank, dtype=jnp.int32) // rank
        masked = jnp.where(page[:, None] == page_of[None, :], prod, 0.0)
        packed = jnp.concatenate(
            [jax.nn.silu(gate).astype(BF), up.astype(BF), masked.astype(BF)], axis=1
        )
        block = experts * cap
        every = [packed]
        for mask in reversed(bits_of(n_dp)):
            flat = jnp.concatenate(every, axis=1) if len(every) > 1 else every[0]
            came = swap(flat, "dp", n_dp, mask)
            came = came.reshape(n_dp, block, -1)
            came = jnp.stack([came[order_d.index(q ^ mask)] for q in order_d])
            came = came.reshape(n_dp * block, -1)
            every = every + jnp.split(came, len(every), axis=1)
        wide = pages * rank
        silus = jnp.stack([y[:, :hid] for y in every])
        ups = jnp.stack([y[:, hid : 2 * hid] for y in every])
        low = jnp.concatenate([y[:, 2 * hid :] for y in every], axis=1)

        def absolute(x):
            x = jnp.stack([x[order_d.index(j)] for j in range(n_dp)])
            for mask in bits_of(n_dp):
                turned = jnp.stack([x[j ^ mask] for j in range(n_dp)])
                x = jnp.where((col & mask) != 0, turned, x)
            return x

        silus, ups = absolute(silus), absolute(ups)
        silus = jnp.moveaxis(silus, 0, 1).reshape(n_dp * block, n_dp * hid)
        ups = jnp.moveaxis(ups, 0, 1).reshape(n_dp * block, n_dp * hid)
        add = jnp.dot(low, expand, preferred_element_type=F32)
        hidden = (silus.astype(F32) * (ups.astype(F32) + add)).astype(BF)
        out = jnp.dot(hidden, down_weight[0], preferred_element_type=F32).astype(BF)
        out = out.reshape(n_dp, experts, cap, part)
        out = exchange(out, "dp", n_dp, 0, order_d)
        out = exchange(out, "expert", n_exp, 1, order_e)
        out = out.reshape(n_dp, block, part).astype(F32)
        mixed = jnp.sum(mix[None, :, :, None] * out[:, None, :, :], axis=2).astype(BF)
        mixed = absolute(mixed)
        return jnp.moveaxis(mixed, 0, 1).reshape(tok_count, n_dp * part)

    return per_device


def solution(mesh):
    row = ("group", "expert", "dp")
    return jax.shard_map(
        build(mesh),
        mesh=mesh,
        in_specs=(
            P(row, None),
            P(row, None),
            P(row, None),
            P(row),
            P(),
            P("expert", None, "dp"),
            P("expert", None, "dp"),
            P("expert", None, "dp"),
            P("expert", "dp", None, None),
            P("expert", "dp", None, None),
        ),
        out_specs=P(row, None),
        check_vma=False,
    )
```

time: 94.8 us -> 52.3 us (0.55)
  blocking collectives: 18 us -> 0 us
  local copies, waits for them, and re-layouts: 16.5 us -> 1.8 us
  between operations: 13.6 us -> 0.39 us
  waiting for transfers between devices: 10.5 us -> 18.3 us
  other arithmetic: 2.63 us -> 8.75 us
  starting transfers between devices: 23.2 us -> 17.4 us
  matrix products: 9.7 us -> 5.4 us
    all_to_all x5 -> x0, starting transfers between devices: 23.2 us -> none  [the longest x1 6.32 us: per_device(): lax.all_to_all(send_ten, 'expert', split_axis=0, concat_axis=0, tiled=True)]
    ppermute x0 -> x12, waiting for transfers between devices: none -> 18.3 us  [swap(): return lax.ppermute(x, axis, [(i, i ^ mask) for i in range(size)])]
    all_gather x3 -> x0, blocking collectives: 18 us -> none  [the longest x1 7.55 us: per_device(): lax.all_gather(got_rows[None], 'dp', axis=0, tiled=True)]
    ppermute x0 -> x12, starting transfers between devices: none -> 17.4 us  [swap(): return lax.ppermute(x, axis, [(i, i ^ mask) for i in range(size)])]
    all_to_all x5 -> x0, waiting for transfers between devices: 9.76 us -> none  [the longest x1 5.74 us: per_device(): lax.all_to_all(home_rows, 'expert', split_axis=1, concat_axis=0, tiled=True)]
    unnamed x11, local copies, waits for them, and re-layouts: 9.81 us -> 0.12 us
    dot_general x7 -> x5, matrix products: 9.7 us -> 5.4 us  [the longest x1 2.2 us: per_device(): up = jnp.dot(slots, up_projection[0], preferred_element_type=F32)]
    all_to_all x4 -> x0, local copies, waits for them, and re-layouts: 3.85 us -> none  [the longest x2 2.5 us: per_device(): lax.all_to_all(adapter_expand, 'dp', split_axis=3, concat_axis=1, tiled=T...]
  transfers between devices with their start and end apart: 6 -> 12, of which waited for: 2 -> 10; matrix products, arithmetic and copies ran while one was open for 23% -> 9% of each run, Pallas kernels for 0% -> 0%
where the time goes in v1:
time: 52.3 us; the launch traced here: 52 us
  waiting for transfers between devices  18.3 us (35%)
  starting transfers between devices  17.4 us (33%)
  other arithmetic  8.75 us (17%)
  matrix products  5.4 us (10%)
  local copies, waits for them, and re-layouts  1.8 us (3%)
    ppermute x12, waiting for transfers between devices, swap(): return lax.ppermute(x, axis, [(i, i ^ mask) for i in range(size)])  18.3 us
    ppermute x12, starting transfers between devices, swap(): return lax.ppermute(x, axis, [(i, i ^ mask) for i in range(size)])  17.4 us
    dot_general x1, matrix products, per_device(): up = jnp.dot(slots, up_projection[0], preferred_element_type=F32)  2.2 us
    concatenate x4, other arithmetic, gather_rows(): x = jnp.concatenate([x, swap(x, axis, size, mask)], axis=0)  1.69 us
    dot_general x1, matrix products, per_device(): out = jnp.dot(hidden, down_weight[0], preferred_element_type=F32).astype(BF)  1.37 us
  transfers between devices with their start and end apart: 12, of which 10 were waited for; matrix products, arithmetic and copies ran while one was open for 9% of the time, Pallas kernels for 0%

profile of v1, /device:TPU:0, one launch (start us, length us, event | category | flops | bytes accessed | tf_op | source)
XLA Modules:
  0.0 52.0 jit_solution(12283103761455719006)
XLA Ops:
  0.1 1.0 %compare_reduce_fusion = pred[8,4]{0,1:T(4,128)(4,1)S(1)} fusion(s32[8,8]{1,0:T(8,128)} %param.11, s32[4]{0:T(128)S(1)} %iota_xor_fusion), kind=kLoop, calls=%fused_computation.57 | loop fusion | flops 480 | bytes 304 | tf_op jit(solution)/shard_map/reduce_or | solution.py:79
  1.1 0.7 %iota_compare_fusion = pred[8,24]{1,0:T(8,128)(4,1)S(1)} fusion(s32[8]{0:T(128)} %param.13), kind=kLoop, calls=%fused_computation.86 | loop fusion | flops 192 | bytes 224 | tf_op jit(solution)/shard_map/eq | solution.py:91
  1.9 0.8 %select_reduce_fusion = s32[8,4]{0,1:T(4,128)S(1)} fusion(s32[4,24]{1,0:T(4,128)} %param.14, pred[8,24]{1,0:T(8,128)(4,1)S(1)} %iota_compare_fusion), kind=kLoop, calls=%fused_computation.77 | loop fusion | flops 1504 | bytes 704 | tf_op jit(solution)/shard_map/reduce_sum | solution.py:92
  3.3 0.7 %convert_multiply_fusion = f32[8,8]{1,0:T(8,128)S(1)} fusion(s32[8,8]{1,0:T(8,128)} %param.12), kind=kLoop, calls=%fused_computation.87 | loop fusion | flops 128 | bytes 512 | tf_op jit(solution)/shard_map/div | solution.py:85
  4.0 0.8 %fusion.43 = f32[8,4]{0,1:T(4,128)S(1)} fusion(f32[8,8]{1,0:T(8,128)S(1)} %convert_multiply_fusion, s32[8,8]{1,0:T(8,128)} %param.11, s32[4]{0:T(128)S(1)} %iota_xor_fusion), kind=kLoop, calls=%fused_computation.70 | loop fusion | flops 736 | bytes 656 | tf_op jit(solution)/shard_map/reduce_sum | solution.py:85
  4.8 0.6 %broadcast_select_fusion = (f32[8,8]{0,1:T(8,128)}, pred[8,8]{0,1:T(8,128)(4,1)S(1)}) fusion(f32[8,8]{0,1:T(8,128)S(1)} %bitcast.94, pred[8,8]{0,1:T(8,128)(4,1)S(1)} %and.58, s32[8,8]{0,1:T(8,128)S(1)} %bitcast.93, s32[8]{0:T(128)S(1)} %eq.100), kind=kLoop, calls=%fused_computation.91 | loop fusion | flops 192 | bytes 928 | tf_op jit(solution)/shard_map/jit(_where)/select_n | solution.py:86
  5.5 1.0 %convolution_convert_fusion = bf16[8,4096]{1,0:T(8,128)(2,1)S(1)} fusion(pred[8,8]{0,1:T(8,128)(4,1)S(1)} %get-tuple-element.6, bf16[8,4096]{1,0:T(8,128)(2,1)} %param.10), kind=kOutput, calls=%fused_computation | convolution fusion | flops 557056 | bytes 131136 | tf_op jit(solution)/shard_map/dot_general | solution.py:88
  6.7 3.1 %collective-permute-start = (bf16[2,2,4224]{2,1,0:T(2,128)(2,1)S(1)}, bf16[2,2,4224]{2,1,0:T(2,128)(2,1)S(1)}, u32[]{:S(2)}, u32[]{:S(2)}) collective-permute-start(bf16[2,2,4224]{2,1,0:T(2,128)(2,1)S(1)} %pad_maximum_fusion.6), channel_id=1, source_target_pairs={{0,4},{4,0},{8,12},{12,8},{1,5},{5,1},{9,13},{13,9},{2,6},{6,2},{1... | collective-permute-start | bytes 101384 | tf_op jit(solution)/shard_map/ppermute | solution.py:11
  9.8 1.9 %collective-permute-done = bf16[2,2,4224]{2,1,0:T(2,128)(2,1)S(1)} collective-permute-done((bf16[2,2,4224]{2,1,0:T(2,128)(2,1)S(1)}, bf16[2,2,4224]{2,1,0:T(2,128)(2,1)S(1)}, u32[]{:S(2)}, u32[]{:S(2)}) %collective-permute-start) | collective-permute-done | bytes 33824 | tf_op jit(solution)/shard_map/ppermute | solution.py:11
  11.8 3.1 %collective-permute-start.1 = (bf16[2,2,4224]{2,1,0:T(2,128)(2,1)S(1)}, bf16[2,2,4224]{2,1,0:T(2,128)(2,1)S(1)}, u32[]{:S(2)}, u32[]{:S(2)}) collective-permute-start(bf16[2,2,4224]{2,1,0:T(2,128)(2,1)S(1)} %pad_maximum_fusion.7), channel_id=1, source_target_pairs={{0,8},{4,12},{8,0},{12,4},{1,9},{5,13},{9,1},{13,5},{2,10},{6,14},... | collective-permute-start | bytes 101384 | tf_op jit(solution)/shard_map/ppermute | solution.py:11
  14.9 1.9 %collective-permute-done.1 = bf16[2,2,4224]{2,1,0:T(2,128)(2,1)S(1)} collective-permute-done((bf16[2,2,4224]{2,1,0:T(2,128)(2,1)S(1)}, bf16[2,2,4224]{2,1,0:T(2,128)(2,1)S(1)}, u32[]{:S(2)}, u32[]{:S(2)}) %collective-permute-start.1) | collective-permute-done | bytes 33824 | tf_op jit(solution)/shard_map/ppermute | solution.py:11
  16.9 1.9 %collective-permute-start.2 = (bf16[1,4,2,4224]{3,2,1,0:T(2,128)(2,1)S(1)}, bf16[1,4,2,4224]{3,2,1,0:T(2,128)(2,1)S(1)}, u32[]{:S(2)}, u32[]{:S(2)}) collective-permute-start(bf16[1,4,2,4224]{3,2,1,0:T(2,128)(2,1)S(1)} %maximum_bitcast_fusion.1), channel_id=1, source_target_pairs={{0,2},{1,3},{2,0},{3,1},{4,6},{5,7},{6,4},{7,5},{8,10},{9,11},{10,... | collective-permute-start | bytes 202760 | tf_op jit(solution)/shard_map/ppermute | solution.py:11
  18.7 2.5 %collective-permute-done.2 = bf16[1,4,2,4224]{3,2,1,0:T(2,128)(2,1)S(1)} collective-permute-done((bf16[1,4,2,4224]{3,2,1,0:T(2,128)(2,1)S(1)}, bf16[1,4,2,4224]{3,2,1,0:T(2,128)(2,1)S(1)}, u32[]{:S(2)}, u32[]{:S(2)}) %collective-permute-start.2) | collective-permute-done | bytes 67616 | tf_op jit(solution)/shard_map/ppermute | solution.py:11
  21.5 1.9 %collective-permute-start.6 = (bf16[1,96,1024]{2,1,0:T(8,128)(2,1)}, bf16[1,96,1024]{2,1,0:T(8,128)(2,1)S(1)}, u32[]{:S(2)}, u32[]{:S(2)}) collective-permute-start(bf16[1,96,1024]{2,1,0:T(8,128)(2,1)} %bitcast.86), channel_id=1, source_target_pairs={{0,2},{1,3},{2,0},{3,1},{4,6},{5,7},{6,4},{7,5},{8,10},{9,11},{10,... | collective-permute-start | bytes 589832 | tf_op jit(solution)/shard_map/ppermute | solution.py:11
  23.4 0.4 pad_maximum_fusion.2
  24.0 2.2 %fusion.11 = bf16[32,256]{1,0:T(8,128)(2,1)S(1)} fusion(bf16[1,4096,256]{2,1,0:T(8,128)(2,1)} %param.16, bf16[32,4224]{1,0:T(8,128)(2,1)S(1)} %reshape.179), kind=kOutput, calls=%fused_computation.11 | convolution fusion | flops 67117056 | bytes 2375680 | tf_op jit(solution)/shard_map/dot_general | solution.py:111
  26.2 0.5 multiply_convert_fusion
  27.1 1.3 %collective-permute-start.4 = (bf16[32,608]{1,0:T(8,128)(2,1)S(1)}, bf16[32,608]{1,0:T(8,128)(2,1)S(1)}, u32[]{:S(2)}, u32[]{:S(2)}) collective-permute-start(bf16[32,608]{1,0:T(8,128)(2,1)S(1)} %pad_maximum_fusion.5), channel_id=1, source_target_pairs={{0,2},{1,3},{2,0},{3,1},{4,6},{5,7},{6,4},{7,5},{8,10},{9,11},{10,... | collective-permute-start | bytes 116744 | tf_op jit(solution)/shard_map/ppermute | solution.py:11
  28.5 0.6 %collective-permute-done.6 = bf16[1,96,1024]{2,1,0:T(8,128)(2,1)S(1)} collective-permute-done((bf16[1,96,1024]{2,1,0:T(8,128)(2,1)}, bf16[1,96,1024]{2,1,0:T(8,128)(2,1)S(1)}, u32[]{:S(2)}, u32[]{:S(2)}) %collective-permute-start.6) | collective-permute-done | bytes 196640 | tf_op jit(solution)/shard_map/ppermute | solution.py:11
  29.2 2.0 %collective-permute-done.4 = bf16[32,608]{1,0:T(8,128)(2,1)S(1)} collective-permute-done((bf16[32,608]{1,0:T(8,128)(2,1)S(1)}, bf16[32,608]{1,0:T(8,128)(2,1)S(1)}, u32[]{:S(2)}, u32[]{:S(2)}) %collective-permute-start.4) | collective-permute-done | bytes 38944 | tf_op jit(solution)/shard_map/ppermute | solution.py:11
  31.4 1.2 %collective-permute-done.5 = bf16[32,1216]{1,0:T(8,128)(2,1)S(1)} collective-permute-done((bf16[32,1216]{1,0:T(8,128)(2,1)S(1)}, bf16[32,1216]{1,0:T(8,128)(2,1)S(1)}, u32[]{:S(2)}, u32[]{:S(2)}) %collective-permute-start.5) | collective-permute-done | bytes 77856 | tf_op jit(solution)/shard_map/ppermute | solution.py:11
  32.9 0.7 %fusion.48 = (bf16[32,96]{1,0:T(8,128)(2,1)}, bf16[32,96]{1,0:T(8,128)(2,1)}) fusion(bf16[32,1216]{1,0:T(8,128)(2,1)S(1)} %maximum_bitcast_fusion), kind=kLoop, calls=%fused_computation.100 | loop fusion | bytes 24576 | tf_op jit(solution)/shard_map/slice | solution.py:135
  33.6 1.1 %pad_maximum_fusion = bf16[4,96,1024]{2,1,0:T(8,128)(2,1)S(1)} fusion(bf16[2,96,1024]{2,1,0:T(8,128)(2,1)} %collective-permute-done.7, bf16[1,96,1024]{2,1,0:T(8,128)(2,1)S(1)} %collective-permute-done.6, bf16[1,96,1024]{2,1,0:T(8,128)(2,1)S(1)} %bitcast.88), kind=kLoop, calls=%fused_computation.15 | loop fusion | flops 786432 | bytes 1572864 | tf_op jit(solution)/shard_map/concatenate | solution.py:28
  34.7 1.4 %fusion.8 = bf16[32,1024]{1,0:T(8,128)(2,1)S(1)} fusion(bf16[1,1024,1024]{2,1,0:T(8,128)(2,1)S(1)} %copy-done, f32[32,1024]{1,0:T(8,128)S(1)} %bitcast.89, f32[32,1024]{1,0:T(8,128)S(1)} %bitcast.90, bf16[384,1024]{1,0:T(8,128)(2,1)S(1)} %bitcast.84, bf16[32,96]{1,0:T(8,128)(2,1)} %get-tuple-element.8, bf16[32,96]{1,0:T(8,128)(2,1)} %get-tuple-element.7, ...), kind=kOutput, calls=%fused_computation.10 | convolution fusion | flops 92504064 | bytes 3235840 | tf_op jit(solution)/shard_map/dot_general | solution.py:149
  36.4 1.0 %collective-permute-done.8 = bf16[2,4,2,1024]{3,2,1,0:T(2,128)(2,1)S(1)} collective-permute-done((bf16[2,4,2,1024]{3,2,1,0:T(2,128)(2,1)S(1)}, bf16[2,4,2,1024]{3,2,1,0:T(2,128)(2,1)S(1)}, u32[]{:S(2)}, u32[]{:S(2)}) %collective-permute-start.8) | collective-permute-done | bytes 32800 | tf_op jit(solution)/shard_map/ppermute | solution.py:11
  37.5 1.3 %collective-permute-start.9 = (bf16[2,4,2,1024]{3,2,1,0:T(2,128)(2,1)S(1)}, bf16[2,4,2,1024]{3,2,1,0:T(2,128)(2,1)S(1)}, u32[]{:S(2)}, u32[]{:S(2)}) collective-permute-start(bf16[2,4,2,1024]{3,2,1,0:T(2,128)(2,1)S(1)} %pad_maximum_fusion.9), channel_id=1, source_target_pairs={{0,2},{1,3},{2,0},{3,1},{4,6},{5,7},{6,4},{7,5},{8,10},{9,11},{10,... | collective-permute-start | bytes 98312 | tf_op jit(solution)/shard_map/ppermute | solution.py:11
  38.9 2.6 %collective-permute-done.9 = bf16[2,4,2,1024]{3,2,1,0:T(2,128)(2,1)S(1)} collective-permute-done((bf16[2,4,2,1024]{3,2,1,0:T(2,128)(2,1)S(1)}, bf16[2,4,2,1024]{3,2,1,0:T(2,128)(2,1)S(1)}, u32[]{:S(2)}, u32[]{:S(2)}) %collective-permute-start.9) | collective-permute-done | bytes 32800 | tf_op jit(solution)/shard_map/ppermute | solution.py:11
  41.8 1.6 %collective-permute-start.10 = (bf16[4,2,2,1024]{3,2,1,0:T(2,128)(2,1)S(1)}, bf16[4,2,2,1024]{3,2,1,0:T(2,128)(2,1)S(1)}, u32[]{:S(2)}, u32[]{:S(2)}) collective-permute-start(bf16[4,2,2,1024]{3,2,1,0:T(2,128)(2,1)S(1)} %pad_maximum_fusion.10), channel_id=1, source_target_pairs={{0,4},{4,0},{8,12},{12,8},{1,5},{5,1},{9,13},{13,9},{2,6},{6,2},{1... | collective-permute-start | bytes 98312 | tf_op jit(solution)/shard_map/ppermute | solution.py:11
  43.4 2.3 %collective-permute-done.10 = bf16[4,2,2,1024]{3,2,1,0:T(2,128)(2,1)S(1)} collective-permute-done((bf16[4,2,2,1024]{3,2,1,0:T(2,128)(2,1)S(1)}, bf16[4,2,2,1024]{3,2,1,0:T(2,128)(2,1)S(1)}, u32[]{:S(2)}, u32[]{:S(2)}) %collective-permute-start.10) | collective-permute-done | bytes 32800 | tf_op jit(solution)/shard_map/ppermute | solution.py:11
  45.9 2.7 %collective-permute-start.11 = (bf16[4,2,2,1024]{3,2,1,0:T(2,128)(2,1)S(1)}, bf16[4,2,2,1024]{3,2,1,0:T(2,128)(2,1)S(1)}, u32[]{:S(2)}, u32[]{:S(2)}) collective-permute-start(bf16[4,2,2,1024]{3,2,1,0:T(2,128)(2,1)S(1)} %pad_maximum_fusion.11), channel_id=1, source_target_pairs={{0,8},{4,12},{8,0},{12,4},{1,9},{5,13},{9,1},{13,5},{2,10},{6,14},... | collective-permute-start | bytes 98312 | tf_op jit(solution)/shard_map/ppermute | solution.py:11
  48.6 2.1 %collective-permute-done.11 = bf16[4,2,2,1024]{3,2,1,0:T(2,128)(2,1)S(1)} collective-permute-done((bf16[4,2,2,1024]{3,2,1,0:T(2,128)(2,1)S(1)}, bf16[4,2,2,1024]{3,2,1,0:T(2,128)(2,1)S(1)}, u32[]{:S(2)}, u32[]{:S(2)}) %collective-permute-start.11) | collective-permute-done | bytes 32800 | tf_op jit(solution)/shard_map/ppermute | solution.py:11
  51.3 0.7 %maximum_select_fusion.5 = bf16[4,8,1024]{2,1,0:T(8,128)(2,1)} fusion(bf16[2,8,1024]{2,1,0:T(8,128)(2,1)S(1)} %get-tuple-element.22, bf16[2,8,1024]{2,1,0:T(8,128)(2,1)S(1)} %get-tuple-element.21, pred[]{:T(512)S(6)} %ne.34, bf16[1,8,1024]{2,1,0:T(8,128)(2,1)S(1)} %get-tuple-element.24, bf16[1,8,1024]{2,1,0:T(8,128)(2,1)S(1)} %get-tuple-element.26, ...), kind=kLoop, calls=%fused_computation.36 | loop fusion | flops 294912 | bytes 196610 | tf_op jit(solution)/shard_map/jit(_where)/select_n | solution.py:141
  (81 shorter events, 3.8 us)
Async XLA Ops:
  0.0 34.7 %copy-start = (bf16[1,1024,1024]{2,1,0:T(8,128)(2,1)S(1)}, bf16[1,1024,1024]{2,1,0:T(8,128)(2,1)}, u32[]{:S(2)}) copy-start(bf16[1,1024,1024]{2,1,0:T(8,128)(2,1)} %param.17) | copy-start | bytes 6291460
  6.7 5.0 %collective-permute-start = (bf16[2,2,4224]{2,1,0:T(2,128)(2,1)S(1)}, bf16[2,2,4224]{2,1,0:T(2,128)(2,1)S(1)}, u32[]{:S(2)}, u32[]{:S(2)}) collective-permute-start(bf16[2,2,4224]{2,1,0:T(2,128)(2,1)S(1)} %pad_maximum_fusion.6), channel_id=1, source_target_pairs={{0,4},{4,0},{8,12},{12,8},{1,5},{5,1},{9,13},{13,9},{2,6},{6,2},{1... | collective-permute-start | bytes 101384 | tf_op jit(solution)/shard_map/ppermute | solution.py:11
  11.8 5.0 %collective-permute-start.1 = (bf16[2,2,4224]{2,1,0:T(2,128)(2,1)S(1)}, bf16[2,2,4224]{2,1,0:T(2,128)(2,1)S(1)}, u32[]{:S(2)}, u32[]{:S(2)}) collective-permute-start(bf16[2,2,4224]{2,1,0:T(2,128)(2,1)S(1)} %pad_maximum_fusion.7), channel_id=1, source_target_pairs={{0,8},{4,12},{8,0},{12,4},{1,9},{5,13},{9,1},{13,5},{2,10},{6,14},... | collective-permute-start | bytes 101384 | tf_op jit(solution)/shard_map/ppermute | solution.py:11
  16.9 4.4 %collective-permute-start.2 = (bf16[1,4,2,4224]{3,2,1,0:T(2,128)(2,1)S(1)}, bf16[1,4,2,4224]{3,2,1,0:T(2,128)(2,1)S(1)}, u32[]{:S(2)}, u32[]{:S(2)}) collective-permute-start(bf16[1,4,2,4224]{3,2,1,0:T(2,128)(2,1)S(1)} %maximum_bitcast_fusion.1), channel_id=1, source_target_pairs={{0,2},{1,3},{2,0},{3,1},{4,6},{5,7},{6,4},{7,5},{8,10},{9,11},{10,... | collective-permute-start | bytes 202760 | tf_op jit(solution)/shard_map/ppermute | solution.py:11
  21.4 2.0 %collective-permute-start.3 = (bf16[2,4,2,4224]{3,2,1,0:T(2,128)(2,1)S(1)}, bf16[2,4,2,4224]{3,2,1,0:T(2,128)(2,1)S(1)}, u32[]{:S(2)}, u32[]{:S(2)}) collective-permute-start(bf16[2,4,2,4224]{3,2,1,0:T(2,128)(2,1)S(1)} %pad_maximum_fusion.3), channel_id=1, source_target_pairs={{0,1},{1,0},{2,3},{3,2},{4,5},{5,4},{6,7},{7,6},{8,9},{9,8},{10,11... | collective-permute-start | bytes 405512 | tf_op jit(solution)/shard_map/ppermute | solution.py:11
  21.5 7.6 %collective-permute-start.6 = (bf16[1,96,1024]{2,1,0:T(8,128)(2,1)}, bf16[1,96,1024]{2,1,0:T(8,128)(2,1)S(1)}, u32[]{:S(2)}, u32[]{:S(2)}) collective-permute-start(bf16[1,96,1024]{2,1,0:T(8,128)(2,1)} %bitcast.86), channel_id=1, source_target_pairs={{0,2},{1,3},{2,0},{3,1},{4,6},{5,7},{6,4},{7,5},{8,10},{9,11},{10,... | collective-permute-start | bytes 589832 | tf_op jit(solution)/shard_map/ppermute | solution.py:11
  24.0 2.2 %copy-start.1 = (bf16[1,4096,256]{2,1,0:T(8,128)(2,1)S(1)}, bf16[1,4096,256]{2,1,0:T(8,128)(2,1)}, u32[]{:S(2)}) copy-start(bf16[1,4096,256]{2,1,0:T(8,128)(2,1)} %param.15) | copy-start | bytes 6291460
  24.0 2.7 %copy-start.2 = (bf16[1,6,16,4096]{3,2,1,0:T(8,128)(2,1)S(1)}, bf16[1,6,16,4096]{3,2,1,0:T(8,128)(2,1)}, u32[]{:S(2)}) copy-start(bf16[1,6,16,4096]{3,2,1,0:T(8,128)(2,1)} %param.18) | copy-start | bytes 2359300
  26.2 2.9 %copy-start.3 = (bf16[1,6,16,1024]{3,2,1,0:T(8,128)(2,1)S(1)}, bf16[1,6,16,1024]{3,2,1,0:T(8,128)(2,1)}, u32[]{:S(2)}) copy-start(bf16[1,6,16,1024]{3,2,1,0:T(8,128)(2,1)} %param.19) | copy-start | bytes 589828
  27.1 4.1 %collective-permute-start.4 = (bf16[32,608]{1,0:T(8,128)(2,1)S(1)}, bf16[32,608]{1,0:T(8,128)(2,1)S(1)}, u32[]{:S(2)}, u32[]{:S(2)}) collective-permute-start(bf16[32,608]{1,0:T(8,128)(2,1)S(1)} %pad_maximum_fusion.5), channel_id=1, source_target_pairs={{0,2},{1,3},{2,0},{3,1},{4,6},{5,7},{6,4},{7,5},{8,10},{9,11},{10,... | collective-permute-start | bytes 116744 | tf_op jit(solution)/shard_map/ppermute | solution.py:11
  29.1 4.5 %collective-permute-start.7 = (bf16[2,96,1024]{2,1,0:T(8,128)(2,1)S(1)}, bf16[2,96,1024]{2,1,0:T(8,128)(2,1)}, u32[]{:S(2)}, u32[]{:S(2)}) collective-permute-start(bf16[2,96,1024]{2,1,0:T(8,128)(2,1)S(1)} %pad_maximum_fusion.1), channel_id=1, source_target_pairs={{0,1},{1,0},{2,3},{3,2},{4,5},{5,4},{6,7},{7,6},{8,9},{9,8},{10,11... | collective-permute-start | bytes 1179656 | tf_op jit(solution)/shard_map/ppermute | solution.py:11
  31.3 1.3 %collective-permute-start.5 = (bf16[32,1216]{1,0:T(8,128)(2,1)S(1)}, bf16[32,1216]{1,0:T(8,128)(2,1)S(1)}, u32[]{:S(2)}, u32[]{:S(2)}) collective-permute-start(bf16[32,1216]{1,0:T(8,128)(2,1)S(1)} %concatenate.31), channel_id=1, source_target_pairs={{0,1},{1,0},{2,3},{3,2},{4,5},{5,4},{6,7},{7,6},{8,9},{9,8},{10,11... | collective-permute-start | bytes 233480 | tf_op jit(solution)/shard_map/ppermute | solution.py:11
  34.7 13.8 %copy-start.4 = (f32[8,8]{0,1:T(8,128)S(1)}, f32[8,8]{0,1:T(8,128)}, u32[]{:S(2)}) copy-start(f32[8,8]{0,1:T(8,128)} %get-tuple-element.5) | copy-start | bytes 772
  36.2 1.3 %collective-permute-start.8 = (bf16[2,4,2,1024]{3,2,1,0:T(2,128)(2,1)S(1)}, bf16[2,4,2,1024]{3,2,1,0:T(2,128)(2,1)S(1)}, u32[]{:S(2)}, u32[]{:S(2)}) collective-permute-start(bf16[2,4,2,1024]{3,2,1,0:T(2,128)(2,1)S(1)} %pad_maximum_fusion.8), channel_id=1, source_target_pairs={{0,1},{1,0},{2,3},{3,2},{4,5},{5,4},{6,7},{7,6},{8,9},{9,8},{10,11... | collective-permute-start | bytes 98312 | tf_op jit(solution)/shard_map/ppermute | solution.py:11
  37.5 4.0 %collective-permute-start.9 = (bf16[2,4,2,1024]{3,2,1,0:T(2,128)(2,1)S(1)}, bf16[2,4,2,1024]{3,2,1,0:T(2,128)(2,1)S(1)}, u32[]{:S(2)}, u32[]{:S(2)}) collective-permute-start(bf16[2,4,2,1024]{3,2,1,0:T(2,128)(2,1)S(1)} %pad_maximum_fusion.9), channel_id=1, source_target_pairs={{0,2},{1,3},{2,0},{3,1},{4,6},{5,7},{6,4},{7,5},{8,10},{9,11},{10,... | collective-permute-start | bytes 98312 | tf_op jit(solution)/shard_map/ppermute | solution.py:11
  41.8 4.0 %collective-permute-start.10 = (bf16[4,2,2,1024]{3,2,1,0:T(2,128)(2,1)S(1)}, bf16[4,2,2,1024]{3,2,1,0:T(2,128)(2,1)S(1)}, u32[]{:S(2)}, u32[]{:S(2)}) collective-permute-start(bf16[4,2,2,1024]{3,2,1,0:T(2,128)(2,1)S(1)} %pad_maximum_fusion.10), channel_id=1, source_target_pairs={{0,4},{4,0},{8,12},{12,8},{1,5},{5,1},{9,13},{13,9},{2,6},{6,2},{1... | collective-permute-start | bytes 98312 | tf_op jit(solution)/shard_map/ppermute | solution.py:11
  45.9 4.9 %collective-permute-start.11 = (bf16[4,2,2,1024]{3,2,1,0:T(2,128)(2,1)S(1)}, bf16[4,2,2,1024]{3,2,1,0:T(2,128)(2,1)S(1)}, u32[]{:S(2)}, u32[]{:S(2)}) collective-permute-start(bf16[4,2,2,1024]{3,2,1,0:T(2,128)(2,1)S(1)} %pad_maximum_fusion.11), channel_id=1, source_target_pairs={{0,8},{4,12},{8,0},{12,4},{1,9},{5,13},{9,1},{13,5},{2,10},{6,14},... | collective-permute-start | bytes 98312 | tf_op jit(solution)/shard_map/ppermute | solution.py:11

commit v2 on v1

v2 whole, which is shorter than its diff:
```python
import jax
import jax.numpy as jnp
from jax import lax
from jax.experimental import pallas as pl
from jax.experimental.pallas import tpu as pltpu
from jax.sharding import PartitionSpec as P

BF = jnp.bfloat16
F32 = jnp.float32
I32 = jnp.int32
TAIL = 128
VM = pl.BlockSpec(memory_space=pltpu.VMEM)
HB = pl.BlockSpec(memory_space=pl.ANY)


def swap(x, axis, size, mask):
    return lax.ppermute(x, axis, [(i, i ^ mask) for i in range(size)])


def bits_of(size):
    return [1 << b for b in range(size.bit_length() - 1)]


def gather_order(size):
    order = [0]
    for mask in reversed(bits_of(size)):
        order = order + [q ^ mask for q in order]
    return order


def turned(x, col, size, names_in, names_out):
    rows = x.shape[0] // size
    block = {q: x[i * rows : (i + 1) * rows] for i, q in enumerate(names_in)}
    for mask in bits_of(size):
        here = (col & mask) != 0
        block = {q: jnp.where(here, block[q ^ mask], block[q]) for q in range(size)}
    return jnp.concatenate([block[q] for q in names_out], axis=0)


def slot_kernel(topk, tok_ref, meta_ref, sent_ref, mix_ref):
    tok_count, width = tok_ref.shape
    experts, lanes = meta_ref.shape[0] - 3 * tok_count, meta_ref.shape[1]
    slots = sent_ref.shape[0]
    cap = slots // experts
    mine = lax.axis_index("expert")
    lane = lax.broadcasted_iota(I32, (tok_count, slots), 1)
    expert_of = (lane // cap) ^ mine
    routing = meta_ref[:tok_count]
    quant = meta_ref[tok_count : 2 * tok_count].astype(F32) * (1.0 / 32768.0)
    assign = jnp.zeros((tok_count, slots), F32)
    coef = jnp.zeros((tok_count, slots), F32)
    for k in range(topk):
        match = routing[:, k : k + 1] == expert_of
        assign = jnp.where(match, 1.0, assign)
        coef = jnp.where(match, quant[:, k : k + 1], coef)
    below = lax.broadcasted_iota(I32, (tok_count, tok_count), 0) > lax.broadcasted_iota(
        I32, (tok_count, tok_count), 1
    )
    slot_rank = jnp.dot(
        jnp.where(below, 1.0, 0.0).astype(BF), assign.astype(BF), preferred_element_type=F32
    )
    place = jnp.where(slot_rank == (lane % cap).astype(F32), assign, 0.0)
    mix_ref[...] = place * coef
    who = meta_ref[2 * tok_count : 2 * tok_count + 1][:, :tok_count]
    hot = jnp.where(lax.broadcasted_iota(I32, (lanes, tok_count), 0) == who, 1.0, 0.0)
    pages = lax.dot_general(
        hot.astype(BF),
        meta_ref[3 * tok_count :].astype(F32).astype(BF),
        (((0,), (1,)), ((), ())),
        preferred_element_type=F32,
    )
    pick = jnp.where(
        lax.broadcasted_iota(I32, (experts, slots), 0)
        == (lax.broadcasted_iota(I32, (experts, slots), 1) // cap) ^ mine,
        1.0,
        0.0,
    )
    page = place * jnp.dot(pages.astype(BF), pick.astype(BF), preferred_element_type=F32)
    by_token = (((0,), (0,)), ((), ()))
    sent_ref[:, :width] = lax.dot_general(
        place.astype(BF), tok_ref[...], by_token, preferred_element_type=F32
    ).astype(BF)
    sent_ref[:, width:] = lax.dot_general(
        page.astype(BF), jnp.ones((tok_count, TAIL), BF), by_token, preferred_element_type=F32
    ).astype(BF)


def expert_kernel(n_dp, rank, own_ref, came_ref, gate_ref, up_ref, shrink_ref, expand_ref, out_ref):
    width = gate_ref.shape[0]
    hid = gate_ref.shape[1]
    wide = shrink_ref.shape[0]
    col = lax.axis_index("dp")
    x = jnp.concatenate([own_ref[:, :width], came_ref[:, :width]], axis=0)
    page = jnp.concatenate([own_ref[:, width:], came_ref[:, width:]], axis=0).astype(F32)[:, :1]
    rows = x.shape[0]
    order = gather_order(n_dp)
    prod = lax.dot_general(
        x, shrink_ref[...], (((1,), (1,)), ((), ())), preferred_element_type=F32
    )
    page_of = col * (wide // rank) + lax.broadcasted_iota(I32, (rows, wide), 1) // rank
    masked = jnp.where(page == page_of.astype(F32), prod, 0.0).astype(BF)
    grown = jnp.dot(masked, expand_ref[...], preferred_element_type=F32)
    gate = jnp.dot(x, gate_ref[...], preferred_element_type=F32)
    up = jnp.dot(x, up_ref[...], preferred_element_type=F32)
    act = gate / (1.0 + jnp.exp(-gate))

    def put(at, y):
        y = turned(y, col, n_dp, order, list(range(n_dp)))
        out_ref[:, at : at + y.shape[1]] = y.astype(BF)

    put(0, act)
    put(hid, act * up)
    put(2 * hid, grown)


def down_kernel(n_dp, hid, own_ref, came_ref, down_ref, keep_ref, send_ref, add_ref):
    col = lax.axis_index("dp")
    order = gather_order(n_dp)
    half = n_dp // 2
    split = 2 * hid * half
    rows = own_ref.shape[0]
    block = rows // n_dp
    part = down_ref.shape[1]
    add_ref[...] = own_ref[:, split:].astype(F32) + came_ref[:, split:].astype(F32)
    total = jnp.zeros((2 * rows, part), F32)
    for i, p in enumerate(order):
        ref = own_ref if i < half else came_ref
        at = (i % half) * 2 * hid
        start = pl.multiple_of((p ^ col) * hid, hid)
        act = ref[:, at : at + hid]
        first = ref[:, at + hid : at + 2 * hid]
        second = (act.astype(F32) * add_ref[:, pl.ds(start, hid)]).astype(BF)
        both = jnp.concatenate([first, second], axis=0)
        total += jnp.dot(both, down_ref[pl.ds(start, hid), :], preferred_element_type=F32)
    out = total[:rows] + total[rows:]
    out = turned(out, col, n_dp, list(range(n_dp)), order)
    for i in range(n_dp):
        ref = keep_ref if i < half else send_ref
        at = (i % half) * part
        ref[:, at : at + part] = out[i * block : (i + 1) * block].astype(BF)


def mix_kernel(n_dp, part, mix_ref, kept_ref, came_ref, out_ref):
    col = lax.axis_index("dp")
    mix = mix_ref[...]
    blocks, cap = kept_ref.shape[:2]
    for p in range(n_dp):
        lanes = slice(p * part, (p + 1) * part)
        total = jnp.zeros((mix.shape[0], part), F32)
        for i, ref in enumerate((kept_ref, came_ref)):
            for r in range(blocks):
                x = ref[r, :, lanes].astype(F32)
                for c in range(cap):
                    at = (i * blocks + r) * cap + c
                    total += mix[:, at : at + 1] * x[c : c + 1]
        out_ref[:, pl.ds(pl.multiple_of((p ^ col) * part, part), part)] = total.astype(BF)


def hold_kernel(x_ref, *refs):
    refs[-1][...] = x_ref[...]


def hold(x, *arrays):
    return call(
        hold_kernel,
        jax.ShapeDtypeStruct(x.shape, x.dtype),
        0,
        in_specs=[VM] + [HB] * len(arrays),
    )(x, *arrays)


def call(kernel, out_shape, n_in, limit=4 << 20, **kw):
    specs = kw.pop("in_specs", [VM] * n_in)
    outs = jax.tree.map(lambda _: VM, out_shape)
    return pl.pallas_call(
        kernel,
        out_shape=out_shape,
        in_specs=specs,
        out_specs=outs,
        compiler_params=pltpu.CompilerParams(vmem_limit_bytes=limit),
        **kw,
    )


def build(mesh):
    n_exp, n_dp = mesh.shape["expert"], mesh.shape["dp"]

    def stage(blocks, axis, size, mask, dim, early=()):
        labels = sorted(blocks)
        sent = [q for q in labels if q & mask]
        x = jnp.concatenate([blocks[q] for q in sent], axis=dim)
        came = jnp.split(swap(x, axis, size, mask), len(sent), axis=dim)
        if early:
            stay = [q for q in labels if not q & mask]
            x = hold(jnp.concatenate([blocks[q] for q in stay], axis=dim), *early)
            blocks = {**blocks, **dict(zip(stay, jnp.split(x, len(stay), axis=dim)))}
        return {**blocks, **dict(zip(sent, came))}

    def per_device(
        tokens,
        routing,
        gate_quantized,
        tenant,
        tenant_page_lookup,
        gate_weight,
        up_projection,
        down_weight,
        adapter_shrink,
        adapter_expand,
    ):
        tok_count, width = tokens.shape
        experts = tenant_page_lookup.shape[0]
        cap = tok_count // 4
        pages, rank = adapter_shrink.shape[1:3]
        hid = gate_weight.shape[2]
        hidden_all = adapter_expand.shape[3]
        part = down_weight.shape[2]
        block = experts * cap
        rows = n_dp * block
        half = n_dp // 2
        shape = jax.ShapeDtypeStruct
        topk = routing.shape[1]
        lanes = max(tenant_page_lookup.shape[1], topk, tok_count)

        def wide(x, rows):
            return jnp.pad(x, ((0, rows - x.shape[0]), (0, lanes - x.shape[1])))

        meta = jnp.concatenate(
            [
                wide(routing, tok_count),
                wide(gate_quantized, tok_count),
                wide(tenant[None], tok_count),
                wide(tenant_page_lookup, experts),
            ],
            axis=0,
        )
        sent, mix = call(
            lambda *refs: slot_kernel(topk, *refs),
            (shape((block, width + TAIL), BF), shape((tok_count, block), F32)),
            2,
        )(tokens, meta)

        state = sent.reshape(n_exp, cap, width + TAIL)
        state = {r: state[r : r + 1] for r in range(n_exp)}
        gate_w = gate_weight.reshape(width, hid)
        up_w = up_projection.reshape(width, hid)
        shrink_w = adapter_shrink.reshape(pages * rank, width)
        expand_w = adapter_expand.reshape(pages * rank, hidden_all)
        early = [(gate_w,), (gate_w, up_w)]
        for mask in bits_of(n_exp):
            state = stage(state, "expert", n_exp, mask, 0, early.pop(0) if early else ())
        own = jnp.concatenate([state[r] for r in range(n_exp)], axis=0)
        own = own.reshape(block, width + TAIL)
        masks = list(reversed(bits_of(n_dp)))
        for mask in masks[:-1]:
            other = swap(own, "dp", n_dp, mask)
            own = jnp.concatenate([hold(own, gate_w, up_w, shrink_w, expand_w), other], axis=0)
        came = swap(own, "dp", n_dp, masks[-1])
        packed = call(
            lambda *refs: expert_kernel(n_dp, rank, *refs),
            shape((rows, 2 * hid + hidden_all), BF),
            6,
        )(
            own,
            came,
            gate_w,
            up_w,
            shrink_w,
            expand_w,
        )

        for mask in masks[:-1]:
            other = swap(packed, "dp", n_dp, mask)
            at = packed.shape[1] - hidden_all
            packed = jnp.concatenate(
                [packed[:, :at], other[:, :at], packed[:, at:] + other[:, at:]], axis=1
            )
        other = swap(packed, "dp", n_dp, masks[-1])
        keep, send = call(
            lambda *refs: down_kernel(n_dp, hid, *refs),
            (shape((block, half * part), BF),) * 2,
            3,
            scratch_shapes=[pltpu.VMEM((rows, hidden_all), F32)],
        )(packed, other, down_weight.reshape(-1, part))

        back = swap(send, "dp", n_dp, 1)
        order = gather_order(n_dp)
        state = {}
        for i, q in enumerate(order[:half]):
            state[q] = keep[:, i * part : (i + 1) * part]
            state[q ^ 1] = back[:, i * part : (i + 1) * part]
        for mask in bits_of(n_dp)[1:]:
            state = stage(state, "dp", n_dp, mask, 1)
        home = jnp.concatenate([state[q] for q in range(n_dp)], axis=1)
        home = home.reshape(n_exp, cap, n_dp * part)
        state = {r: home[r : r + 1] for r in range(n_exp)}
        for mask in bits_of(n_exp)[:-1]:
            state = stage(state, "expert", n_exp, mask, 0)
        middle = n_exp // 2
        kept = jnp.concatenate([state[r] for r in range(middle)], axis=0)
        sent = jnp.concatenate([state[r] for r in range(middle, n_exp)], axis=0)
        came = swap(sent, "expert", n_exp, middle)
        return call(
            lambda *refs: mix_kernel(n_dp, part, *refs),
            shape((tok_count, n_dp * part), BF),
            3,
        )(mix, kept, came)

    return per_device


def solution(mesh):
    row = ("group", "expert", "dp")
    return jax.shard_map(
        build(mesh),
        mesh=mesh,
        in_specs=(
            P(row, None),
            P(row, None),
            P(row, None),
            P(row),
            P(),
            P("expert", None, "dp"),
            P("expert", None, "dp"),
            P("expert", None, "dp"),
            P("expert", "dp", None, None),
            P("expert", "dp", None, None),
        ),
        out_specs=P(row, None),
        check_vma=False,
    )
```

time: 52.3 us -> 42 us (0.80)
  other arithmetic: 8.75 us -> 1.22 us
  matrix products: 5.4 us -> 0 us
  local copies, waits for them, and re-layouts: 1.8 us -> 5.85 us
  waiting for transfers between devices: 18.3 us -> 14.3 us
  Pallas kernels: 0 us -> 3.19 us
    unnamed x11 -> x18, local copies, waits for them, and re-layouts: 0.12 us -> 5.62 us
    dot_general x5 -> x0, matrix products: 5.4 us -> none  [the longest x1 2.2 us: per_device(): up = jnp.dot(slots, up_projection[0], preferred_element_type=F32)]
    ppermute x12 -> x10, waiting for transfers between devices: 18.3 us -> 14.3 us  [swap(): return lax.ppermute(x, axis, [(i, i ^ mask) for i in range(size)])]
    pallas_call x0 -> x7, Pallas kernels: none -> 3.19 us  [the longest x1 1.42 us: per_device(): call(lambda *refs: expert_kernel(n_dp, rank, *refs), shape((rows, 2 * hid...]
    reduce_sum x6 -> x0, other arithmetic: 2.43 us -> none  [the longest x1 0.84 us: per_device(): jnp.sum(jnp.where(matches, gate_quantized[:, :, None].astype(F32) / 32768...]
    select_n x4 -> x0, other arithmetic: 1.33 us -> none  [the longest x3 0.69 us: absolute(): x = jnp.where(col & mask != 0, turned, x)]
    reduce_or x1 -> x0, other arithmetic: 1.03 us -> none  [per_device(): assign = jnp.any(matches, axis=1)]
    eq x3 -> x0, other arithmetic: 0.82 us -> none  [the longest x1 0.73 us: per_device(): hot = tenant[:, None] == jnp.arange(tenants, dtype=jnp.int32)[None, :]]
  transfers between devices with their start and end apart: 12 -> 10, of which waited for: 10 -> 10; matrix products, arithmetic and copies ran while one was open for 9% -> 0% of each run, Pallas kernels for 0% -> 0%
where the time goes in v2:
time: 42 us; the launch traced here: 41.7 us
  starting transfers between devices  16.9 us (40%)
  waiting for transfers between devices  14.3 us (34%)
  local copies, waits for them, and re-layouts  5.85 us (14%)
  Pallas kernels  3.19 us (8%)
  other arithmetic  1.22 us (3%)
    ppermute x10, starting transfers between devices, swap(): return lax.ppermute(x, axis, [(i, i ^ mask) for i in range(size)])  16.9 us
    ppermute x10, waiting for transfers between devices, swap(): return lax.ppermute(x, axis, [(i, i ^ mask) for i in range(size)])  14.3 us
    unnamed x18, local copies, waits for them, and re-layouts  5.62 us
    pallas_call x1, Pallas kernels, per_device(): call(lambda *refs: expert_kernel(n_dp, rank, *refs), shape((rows, 2 * hid...  1.42 us
  transfers between devices with their start and end apart: 10, of which 10 were waited for; matrix products, arithmetic and copies ran while one was open for 0% of the time, Pallas kernels for 0%

profile of v2, /device:TPU:0, one launch (start us, length us, event | category | flops | bytes accessed | tf_op | source)
XLA Modules:
  0.0 41.7 jit_solution(13808269734814198648)
XLA Ops:
  0.0 0.7 %fusion.refs_1_ = s32[28,24]{1,0:T(8,128)S(1)} fusion(s32[1,8]{1,0:T(1,128)} %bitcast.34, s32[8,8]{1,0:T(8,128)} %param.12, s32[8,8]{1,0:T(8,128)} %param.11, s32[4,24]{1,0:T(4,128)} %param.14), kind=kLoop, calls=%fused_computation.22 | loop fusion | flops 2016 | bytes 3616 | tf_op jit(solution)/shard_map/concatenate | solution.py:228
  0.7 0.8 %copy-done.8 = bf16[8,4096]{1,0:T(8,128)(2,1)S(1)} copy-done((bf16[8,4096]{1,0:T(8,128)(2,1)S(1)}, bf16[8,4096]{1,0:T(8,128)(2,1)}, u32[]{:S(2)}) %copy-start.8) | copy-done | bytes 65560
  1.6 0.5 %shard_map.100 = (bf16[8,4224]{1,0:T(8,128)(2,1)S(1)}, f32[8,8]{1,0:T(8,128)S(1)}) custom-call(bf16[8,4096]{1,0:T(8,128)(2,1)S(1)} %copy-done.8, s32[28,24]{1,0:T(8,128)S(1)} %fusion.refs_1_), custom_call_target="tpu_custom_call" | custom-call | tf_op jit(solution)/shard_map/pallas_call | solution.py:237
  2.0 0.1 slice_bitcast_fusion.3
  2.1 0.1 pad_maximum_fusion.5
  2.2 3.1 %collective-permute-start = (bf16[2,2,4224]{2,1,0:T(2,128)(2,1)S(1)}, bf16[2,2,4224]{2,1,0:T(2,128)(2,1)S(1)}, u32[]{:S(2)}, u32[]{:S(2)}) collective-permute-start(bf16[2,2,4224]{2,1,0:T(2,128)(2,1)S(1)} %pad_maximum_fusion.5), channel_id=1, source_target_pairs={{0,4},{4,0},{8,12},{12,8},{1,5},{5,1},{9,13},{13,9},{2,6},{6,2},{1... | collective-permute-start | bytes 101384 | tf_op jit(solution)/shard_map/ppermute | solution.py:17
  5.3 1.6 %copy-done = bf16[1,4096,256]{2,1,0:T(8,128)(2,1)S(1)} copy-done((bf16[1,4096,256]{2,1,0:T(8,128)(2,1)S(1)}, bf16[1,4096,256]{2,1,0:T(8,128)(2,1)}, u32[]{:S(2)}) %copy-start) | copy-done | bytes 2097176
  6.9 0.2 collective-permute-done
  7.2 3.1 %collective-permute-start.1 = (bf16[2,2,4224]{2,1,0:T(2,128)(2,1)S(1)}, bf16[2,2,4224]{2,1,0:T(2,128)(2,1)S(1)}, u32[]{:S(2)}, u32[]{:S(2)}) collective-permute-start(bf16[2,2,4224]{2,1,0:T(2,128)(2,1)S(1)} %pad_maximum_fusion.7), channel_id=1, source_target_pairs={{0,8},{4,12},{8,0},{12,4},{1,9},{5,13},{9,1},{13,5},{2,10},{6,14},... | collective-permute-start | bytes 101384 | tf_op jit(solution)/shard_map/ppermute | solution.py:17
  10.4 1.6 %copy-done.2 = bf16[1,4096,256]{2,1,0:T(8,128)(2,1)S(1)} copy-done((bf16[1,4096,256]{2,1,0:T(8,128)(2,1)S(1)}, bf16[1,4096,256]{2,1,0:T(8,128)(2,1)}, u32[]{:S(2)}) %copy-start.2) | copy-done | bytes 2097176
  12.0 0.2 collective-permute-done.1
  12.2 0.1 pad_maximum_fusion.2
  12.4 1.9 %collective-permute-start.2 = (bf16[8,4224]{1,0:T(8,128)(2,1)S(1)}, bf16[8,4224]{1,0:T(8,128)(2,1)S(1)}, u32[]{:S(2)}, u32[]{:S(2)}) collective-permute-start(bf16[8,4224]{1,0:T(8,128)(2,1)S(1)} %reshape.30.x_ref), channel_id=1, source_target_pairs={{0,2},{1,3},{2,0},{3,1},{4,6},{5,7},{6,4},{7,5},{8,10},{9,11},{10,... | collective-permute-start | bytes 202760 | tf_op jit(solution)/shard_map/ppermute | solution.py:17
  14.3 1.6 %copy-done.3 = bf16[1,4096,256]{2,1,0:T(8,128)(2,1)S(1)} copy-done((bf16[1,4096,256]{2,1,0:T(8,128)(2,1)S(1)}, bf16[1,4096,256]{2,1,0:T(8,128)(2,1)}, u32[]{:S(2)}) %copy-start.3) | copy-done | bytes 2097176
  15.9 0.9 %collective-permute-done.2 = bf16[8,4224]{1,0:T(8,128)(2,1)S(1)} collective-permute-done((bf16[8,4224]{1,0:T(8,128)(2,1)S(1)}, bf16[8,4224]{1,0:T(8,128)(2,1)S(1)}, u32[]{:S(2)}, u32[]{:S(2)}) %collective-permute-start.2) | collective-permute-done | bytes 67616 | tf_op jit(solution)/shard_map/ppermute | solution.py:17
  16.8 0.1 collective-permute-start.3
  16.8 1.3 %collective-permute-done.3.refs_1_ = bf16[16,4224]{1,0:T(8,128)(2,1)S(1)} collective-permute-done((bf16[16,4224]{1,0:T(8,128)(2,1)S(1)}, bf16[16,4224]{1,0:T(8,128)(2,1)S(1)}, u32[]{:S(2)}, u32[]{:S(2)}) %collective-permute-start.3) | collective-permute-done | bytes 135200 | tf_op jit(solution)/shard_map/ppermute | solution.py:17
  18.2 1.4 %shard_map.104 = bf16[32,1536]{1,0:T(8,128)(2,1)S(1)} custom-call(bf16[16,4224]{1,0:T(8,128)(2,1)S(1)} %pad_maximum_fusion.refs_0_, bf16[16,4224]{1,0:T(8,128)(2,1)S(1)} %collective-permute-done.3.refs_1_, bf16[4096,256]{1,0:T(8,128)(2,1)S(1)} %bitcast.25, bf16[4096,256]{1,0:T(8,128)(2,1)S(1)} %bitcast.28, bf16[96,4096]{1,0:T(8,128)(2,1)S(1)} %bitcast.30, ...), custom_call_target="tpu_custom_call" | custom-call | tf_op jit(solution)/shard_map/pallas_call | solution.py:259
  19.6 1.9 %collective-permute-start.4 = (bf16[32,1536]{1,0:T(8,128)(2,1)S(1)}, bf16[32,1536]{1,0:T(8,128)(2,1)S(1)}, u32[]{:S(2)}, u32[]{:S(2)}) collective-permute-start(bf16[32,1536]{1,0:T(8,128)(2,1)S(1)} %shard_map.104), channel_id=1, source_target_pairs={{0,2},{1,3},{2,0},{3,1},{4,6},{5,7},{6,4},{7,5},{8,10},{9,11},{10,... | collective-permute-start | bytes 294920 | tf_op jit(solution)/shard_map/ppermute | solution.py:17
  21.5 3.1 %collective-permute-done.4 = bf16[32,1536]{1,0:T(8,128)(2,1)S(1)} collective-permute-done((bf16[32,1536]{1,0:T(8,128)(2,1)S(1)}, bf16[32,1536]{1,0:T(8,128)(2,1)S(1)}, u32[]{:S(2)}, u32[]{:S(2)}) %collective-permute-start.4) | collective-permute-done | bytes 98336 | tf_op jit(solution)/shard_map/ppermute | solution.py:17
  24.6 0.1 collective-permute-start.5
  24.7 1.3 %collective-permute-done.5.refs_1_ = bf16[32,2048]{1,0:T(8,128)(2,1)S(1)} collective-permute-done((bf16[32,2048]{1,0:T(8,128)(2,1)S(1)}, bf16[32,2048]{1,0:T(8,128)(2,1)S(1)}, u32[]{:S(2)}, u32[]{:S(2)}) %collective-permute-start.5) | collective-permute-done | bytes 131104 | tf_op jit(solution)/shard_map/ppermute | solution.py:17
  26.1 0.5 %shard_map.105 = (bf16[8,2048]{1,0:T(8,128)(2,1)S(1)}, bf16[8,2048]{1,0:T(8,128)(2,1)S(1)}) custom-call(bf16[32,2048]{1,0:T(8,128)(2,1)S(1)} %pad_maximum_fusion.1.refs_0_, bf16[32,2048]{1,0:T(8,128)(2,1)S(1)} %collective-permute-done.5.refs_1_, bf16[1024,1024]{1,0:T(8,128)(2,1)S(1)} %bitcast.31), custom_call_target="tpu_custom_call" | custom-call | tf_op jit(solution)/shard_map/pallas_call | solution.py:279
  26.6 0.2 collective-permute-start.6
  26.8 1.1 %collective-permute-done.6 = bf16[8,2048]{1,0:T(8,128)(2,1)S(1)} collective-permute-done((bf16[8,2048]{1,0:T(8,128)(2,1)S(1)}, bf16[8,2048]{1,0:T(8,128)(2,1)S(1)}, u32[]{:S(2)}, u32[]{:S(2)}) %collective-permute-start.6) | collective-permute-done | bytes 32800 | tf_op jit(solution)/shard_map/ppermute | solution.py:17
  27.8 1.8 %collective-permute-start.7 = (bf16[8,2048]{1,0:T(8,128)(2,1)S(1)}, bf16[8,2048]{1,0:T(8,128)(2,1)S(1)}, u32[]{:S(2)}, u32[]{:S(2)}) collective-permute-start(bf16[8,2048]{1,0:T(8,128)(2,1)S(1)} %pad_maximum_fusion.8), channel_id=1, source_target_pairs={{0,2},{1,3},{2,0},{3,1},{4,6},{5,7},{6,4},{7,5},{8,10},{9,11},{10,... | collective-permute-start | bytes 98312 | tf_op jit(solution)/shard_map/ppermute | solution.py:17
  29.6 2.2 %collective-permute-done.7 = bf16[8,2048]{1,0:T(8,128)(2,1)S(1)} collective-permute-done((bf16[8,2048]{1,0:T(8,128)(2,1)S(1)}, bf16[8,2048]{1,0:T(8,128)(2,1)S(1)}, u32[]{:S(2)}, u32[]{:S(2)}) %collective-permute-start.7) | collective-permute-done | bytes 32800 | tf_op jit(solution)/shard_map/ppermute | solution.py:17
  31.9 1.9 %collective-permute-start.8 = (bf16[2,2,4096]{2,1,0:T(2,128)(2,1)S(1)}, bf16[2,2,4096]{2,1,0:T(2,128)(2,1)S(1)}, u32[]{:S(2)}, u32[]{:S(2)}) collective-permute-start(bf16[2,2,4096]{2,1,0:T(2,128)(2,1)S(1)} %pad_maximum_fusion.9), channel_id=1, source_target_pairs={{0,4},{4,0},{8,12},{12,8},{1,5},{5,1},{9,13},{13,9},{2,6},{6,2},{1... | collective-permute-start | bytes 98312 | tf_op jit(solution)/shard_map/ppermute | solution.py:17
  33.8 2.1 %collective-permute-done.8 = bf16[2,2,4096]{2,1,0:T(2,128)(2,1)S(1)} collective-permute-done((bf16[2,2,4096]{2,1,0:T(2,128)(2,1)S(1)}, bf16[2,2,4096]{2,1,0:T(2,128)(2,1)S(1)}, u32[]{:S(2)}, u32[]{:S(2)}) %collective-permute-start.8) | collective-permute-done | bytes 32800 | tf_op jit(solution)/shard_map/ppermute | solution.py:17
  36.0 2.9 %collective-permute-start.9 = (bf16[2,2,4096]{2,1,0:T(2,128)(2,1)S(1)}, bf16[2,2,4096]{2,1,0:T(2,128)(2,1)S(1)}, u32[]{:S(2)}, u32[]{:S(2)}) collective-permute-start(bf16[2,2,4096]{2,1,0:T(2,128)(2,1)S(1)} %pad_maximum_fusion.11), channel_id=1, source_target_pairs={{0,8},{4,12},{8,0},{12,4},{1,9},{5,13},{9,1},{13,5},{2,10},{6,14},... | collective-permute-start | bytes 98312 | tf_op jit(solution)/shard_map/ppermute | solution.py:17
  39.0 1.9 %collective-permute-done.9.refs_2_ = bf16[2,2,4096]{2,1,0:T(2,128)(2,1)S(1)} collective-permute-done((bf16[2,2,4096]{2,1,0:T(2,128)(2,1)S(1)}, bf16[2,2,4096]{2,1,0:T(2,128)(2,1)S(1)}, u32[]{:S(2)}, u32[]{:S(2)}) %collective-permute-start.9) | collective-permute-done | bytes 32800 | tf_op jit(solution)/shard_map/ppermute | solution.py:17
  40.9 0.8 %shard_map.106 = bf16[8,4096]{1,0:T(8,128)(2,1)} custom-call(f32[8,8]{1,0:T(8,128)S(1)} %get-tuple-element.9.refs_0_, bf16[2,2,4096]{2,1,0:T(2,128)(2,1)S(1)} %pad_maximum_fusion.10.refs_1_, bf16[2,2,4096]{2,1,0:T(2,128)(2,1)S(1)} %collective-permute-done.9.refs_2_), custom_call_target="tpu_custom_call" | custom-call | tf_op jit(solution)/shard_map/pallas_call | solution.py:303
  (37 shorter events, 0.6 us)
Async XLA Ops:
  0.7 0.8 %copy-start.8 = (bf16[8,4096]{1,0:T(8,128)(2,1)S(1)}, bf16[8,4096]{1,0:T(8,128)(2,1)}, u32[]{:S(2)}) copy-start(bf16[8,4096]{1,0:T(8,128)(2,1)} %refs_0_.1) | copy-start | bytes 196612
  2.2 5.0 %collective-permute-start = (bf16[2,2,4224]{2,1,0:T(2,128)(2,1)S(1)}, bf16[2,2,4224]{2,1,0:T(2,128)(2,1)S(1)}, u32[]{:S(2)}, u32[]{:S(2)}) collective-permute-start(bf16[2,2,4224]{2,1,0:T(2,128)(2,1)S(1)} %pad_maximum_fusion.5), channel_id=1, source_target_pairs={{0,4},{4,0},{8,12},{12,8},{1,5},{5,1},{9,13},{13,9},{2,6},{6,2},{1... | collective-permute-start | bytes 101384 | tf_op jit(solution)/shard_map/ppermute | solution.py:17
  5.3 1.6 %copy-start = (bf16[1,4096,256]{2,1,0:T(8,128)(2,1)S(1)}, bf16[1,4096,256]{2,1,0:T(8,128)(2,1)}, u32[]{:S(2)}) copy-start(bf16[1,4096,256]{2,1,0:T(8,128)(2,1)} %param.15) | copy-start | bytes 6291460
  6.9 3.5 %copy-start.1 = (bf16[1,4096,256]{2,1,0:T(8,128)(2,1)S(1)}, bf16[1,4096,256]{2,1,0:T(8,128)(2,1)}, u32[]{:S(2)}) copy-start(bf16[1,4096,256]{2,1,0:T(8,128)(2,1)} %param.15) | copy-start | bytes 6291460
  7.2 5.0 %collective-permute-start.1 = (bf16[2,2,4224]{2,1,0:T(2,128)(2,1)S(1)}, bf16[2,2,4224]{2,1,0:T(2,128)(2,1)S(1)}, u32[]{:S(2)}, u32[]{:S(2)}) collective-permute-start(bf16[2,2,4224]{2,1,0:T(2,128)(2,1)S(1)} %pad_maximum_fusion.7), channel_id=1, source_target_pairs={{0,8},{4,12},{8,0},{12,4},{1,9},{5,13},{9,1},{13,5},{2,10},{6,14},... | collective-permute-start | bytes 101384 | tf_op jit(solution)/shard_map/ppermute | solution.py:17
  10.4 1.6 %copy-start.2 = (bf16[1,4096,256]{2,1,0:T(8,128)(2,1)S(1)}, bf16[1,4096,256]{2,1,0:T(8,128)(2,1)}, u32[]{:S(2)}) copy-start(bf16[1,4096,256]{2,1,0:T(8,128)(2,1)} %param.16) | copy-start | bytes 6291460
  12.0 2.3 %copy-start.5 = (bf16[1,6,16,4096]{3,2,1,0:T(8,128)(2,1)S(1)}, bf16[1,6,16,4096]{3,2,1,0:T(8,128)(2,1)}, u32[]{:S(2)}) copy-start(bf16[1,6,16,4096]{3,2,1,0:T(8,128)(2,1)} %param.18) | copy-start | bytes 2359300
  12.0 2.3 %copy-start.7 = (bf16[1,6,16,1024]{3,2,1,0:T(8,128)(2,1)S(1)}, bf16[1,6,16,1024]{3,2,1,0:T(8,128)(2,1)}, u32[]{:S(2)}) copy-start(bf16[1,6,16,1024]{3,2,1,0:T(8,128)(2,1)} %param.19) | copy-start | bytes 589828
  12.4 4.4 %collective-permute-start.2 = (bf16[8,4224]{1,0:T(8,128)(2,1)S(1)}, bf16[8,4224]{1,0:T(8,128)(2,1)S(1)}, u32[]{:S(2)}, u32[]{:S(2)}) collective-permute-start(bf16[8,4224]{1,0:T(8,128)(2,1)S(1)} %reshape.30.x_ref), channel_id=1, source_target_pairs={{0,2},{1,3},{2,0},{3,1},{4,6},{5,7},{6,4},{7,5},{8,10},{9,11},{10,... | collective-permute-start | bytes 202760 | tf_op jit(solution)/shard_map/ppermute | solution.py:17
  14.3 1.6 %copy-start.3 = (bf16[1,4096,256]{2,1,0:T(8,128)(2,1)S(1)}, bf16[1,4096,256]{2,1,0:T(8,128)(2,1)}, u32[]{:S(2)}) copy-start(bf16[1,4096,256]{2,1,0:T(8,128)(2,1)} %param.16) | copy-start | bytes 6291460
  15.9 2.3 %copy-start.4 = (bf16[1,4096,256]{2,1,0:T(8,128)(2,1)S(1)}, bf16[1,4096,256]{2,1,0:T(8,128)(2,1)}, u32[]{:S(2)}) copy-start(bf16[1,4096,256]{2,1,0:T(8,128)(2,1)} %param.16) | copy-start | bytes 6291460
  16.7 9.3 %copy-start.6 = (bf16[1,1024,1024]{2,1,0:T(8,128)(2,1)S(1)}, bf16[1,1024,1024]{2,1,0:T(8,128)(2,1)}, u32[]{:S(2)}) copy-start(bf16[1,1024,1024]{2,1,0:T(8,128)(2,1)} %param.17) | copy-start | bytes 6291460
  16.8 1.4 %collective-permute-start.3 = (bf16[16,4224]{1,0:T(8,128)(2,1)S(1)}, bf16[16,4224]{1,0:T(8,128)(2,1)S(1)}, u32[]{:S(2)}, u32[]{:S(2)}) collective-permute-start(bf16[16,4224]{1,0:T(8,128)(2,1)S(1)} %pad_maximum_fusion.refs_0_), channel_id=1, source_target_pairs={{0,1},{1,0},{2,3},{3,2},{4,5},{5,4},{6,7},{7,6},{8,9},{9,8},{10,11... | collective-permute-start | bytes 405512 | tf_op jit(solution)/shard_map/ppermute | solution.py:17
  19.6 5.0 %collective-permute-start.4 = (bf16[32,1536]{1,0:T(8,128)(2,1)S(1)}, bf16[32,1536]{1,0:T(8,128)(2,1)S(1)}, u32[]{:S(2)}, u32[]{:S(2)}) collective-permute-start(bf16[32,1536]{1,0:T(8,128)(2,1)S(1)} %shard_map.104), channel_id=1, source_target_pairs={{0,2},{1,3},{2,0},{3,1},{4,6},{5,7},{6,4},{7,5},{8,10},{9,11},{10,... | collective-permute-start | bytes 294920 | tf_op jit(solution)/shard_map/ppermute | solution.py:17
  24.6 1.4 %collective-permute-start.5 = (bf16[32,2048]{1,0:T(8,128)(2,1)S(1)}, bf16[32,2048]{1,0:T(8,128)(2,1)S(1)}, u32[]{:S(2)}, u32[]{:S(2)}) collective-permute-start(bf16[32,2048]{1,0:T(8,128)(2,1)S(1)} %pad_maximum_fusion.1.refs_0_), channel_id=1, source_target_pairs={{0,1},{1,0},{2,3},{3,2},{4,5},{5,4},{6,7},{7,6},{8,9},{9,8},{10,11... | collective-permute-start | bytes 393224 | tf_op jit(solution)/shard_map/ppermute | solution.py:17
  26.6 1.3 %collective-permute-start.6 = (bf16[8,2048]{1,0:T(8,128)(2,1)S(1)}, bf16[8,2048]{1,0:T(8,128)(2,1)S(1)}, u32[]{:S(2)}, u32[]{:S(2)}) collective-permute-start(bf16[8,2048]{1,0:T(8,128)(2,1)S(1)} %get-tuple-element.12), channel_id=1, source_target_pairs={{0,1},{1,0},{2,3},{3,2},{4,5},{5,4},{6,7},{7,6},{8,9},{9,8},{10,11... | collective-permute-start | bytes 98312 | tf_op jit(solution)/shard_map/ppermute | solution.py:17
  27.8 4.0 %collective-permute-start.7 = (bf16[8,2048]{1,0:T(8,128)(2,1)S(1)}, bf16[8,2048]{1,0:T(8,128)(2,1)S(1)}, u32[]{:S(2)}, u32[]{:S(2)}) collective-permute-start(bf16[8,2048]{1,0:T(8,128)(2,1)S(1)} %pad_maximum_fusion.8), channel_id=1, source_target_pairs={{0,2},{1,3},{2,0},{3,1},{4,6},{5,7},{6,4},{7,5},{8,10},{9,11},{10,... | collective-permute-start | bytes 98312 | tf_op jit(solution)/shard_map/ppermute | solution.py:17
  31.9 4.0 %collective-permute-start.8 = (bf16[2,2,4096]{2,1,0:T(2,128)(2,1)S(1)}, bf16[2,2,4096]{2,1,0:T(2,128)(2,1)S(1)}, u32[]{:S(2)}, u32[]{:S(2)}) collective-permute-start(bf16[2,2,4096]{2,1,0:T(2,128)(2,1)S(1)} %pad_maximum_fusion.9), channel_id=1, source_target_pairs={{0,4},{4,0},{8,12},{12,8},{1,5},{5,1},{9,13},{13,9},{2,6},{6,2},{1... | collective-permute-start | bytes 98312 | tf_op jit(solution)/shard_map/ppermute | solution.py:17
  36.0 4.9 %collective-permute-start.9 = (bf16[2,2,4096]{2,1,0:T(2,128)(2,1)S(1)}, bf16[2,2,4096]{2,1,0:T(2,128)(2,1)S(1)}, u32[]{:S(2)}, u32[]{:S(2)}) collective-permute-start(bf16[2,2,4096]{2,1,0:T(2,128)(2,1)S(1)} %pad_maximum_fusion.11), channel_id=1, source_target_pairs={{0,8},{4,12},{8,0},{12,4},{1,9},{5,13},{9,1},{13,5},{2,10},{6,14},... | collective-permute-start | bytes 98312 | tf_op jit(solution)/shard_map/ppermute | solution.py:17

commit v3 on v2

--- a/solution.py
+++ b/solution.py
@@ -37,16 +37,19 @@
     return jnp.concatenate([block[q] for q in names_out], axis=0)
 
 
-def slot_kernel(topk, tok_ref, meta_ref, sent_ref, mix_ref):
+def slot_kernel(
+    tok_ref, routing_ref, gate_ref, tenant_ref, lookup_ref, keep_ref, send_ref, mix_ref
+):
     tok_count, width = tok_ref.shape
-    experts, lanes = meta_ref.shape[0] - 3 * tok_count, meta_ref.shape[1]
-    slots = sent_ref.shape[0]
+    experts, tenants = lookup_ref.shape
+    slots = mix_ref.shape[1]
     cap = slots // experts
+    topk = routing_ref.shape[1]
     mine = lax.axis_index("expert")
     lane = lax.broadcasted_iota(I32, (tok_count, slots), 1)
     expert_of = (lane // cap) ^ mine
-    routing = meta_ref[:tok_count]
-    quant = meta_ref[tok_count : 2 * tok_count].astype(F32) * (1.0 / 32768.0)
+    routing = routing_ref[...]
+    quant = gate_ref[...].astype(F32) * (1.0 / 32768.0)
     assign = jnp.zeros((tok_count, slots), F32)
     coef = jnp.zeros((tok_count, slots), F32)
     for k in range(topk):
@@ -61,12 +64,15 @@
     )
     place = jnp.where(slot_rank == (lane % cap).astype(F32), assign, 0.0)
     mix_ref[...] = place * coef
-    who = meta_ref[2 * tok_count : 2 * tok_count + 1][:, :tok_count]
-    hot = jnp.where(lax.broadcasted_iota(I32, (lanes, tok_count), 0) == who, 1.0, 0.0)
+    row = lax.broadcasted_iota(I32, (tok_count, tenants), 0)
+    who = jnp.zeros((tok_count, tenants), I32)
+    for t in range(tok_count):
+        who = jnp.where(row == t, tenant_ref[t], who)
+    hot = jnp.where(lax.broadcasted_iota(I32, (tok_count, tenants), 1) == who, 1.0, 0.0)
     pages = lax.dot_general(
         hot.astype(BF),
-        meta_ref[3 * tok_count :].astype(F32).astype(BF),
-        (((0,), (1,)), ((), ())),
+        lookup_ref[...].astype(F32).astype(BF),
+        (((1,), (1,)), ((), ())),
         preferred_element_type=F32,
     )
     pick = jnp.where(
@@ -77,67 +83,85 @@
     )
     page = place * jnp.dot(pages.astype(BF), pick.astype(BF), preferred_element_type=F32)
     by_token = (((0,), (0,)), ((), ()))
-    sent_ref[:, :width] = lax.dot_general(
-        place.astype(BF), tok_ref[...], by_token, preferred_element_type=F32
-    ).astype(BF)
-    sent_ref[:, width:] = lax.dot_general(
+    rows = lax.dot_general(place.astype(BF), tok_ref[...], by_token, preferred_element_type=F32)
+    tail = lax.dot_general(
         page.astype(BF), jnp.ones((tok_count, TAIL), BF), by_token, preferred_element_type=F32
-    ).astype(BF)
-
-
-def expert_kernel(n_dp, rank, own_ref, came_ref, gate_ref, up_ref, shrink_ref, expand_ref, out_ref):
-    width = gate_ref.shape[0]
-    hid = gate_ref.shape[1]
-    wide = shrink_ref.shape[0]
+    )
+    for r in range(experts):
+        ref = send_ref if r % 2 else keep_ref
+        at = slice(r * cap, (r + 1) * cap)
+        ref[r // 2, :, :width] = rows[at].astype(BF)
+        ref[r // 2, :, width:] = tail[at].astype(BF)
+
+
+def rows_of(own_ref, came_ref, width):
+    return jnp.concatenate([own_ref[:, :width], came_ref[:, :width]], axis=0)
+
+
+def shrink_kernel(n_dp, rank, own_ref, came_ref, shrink_ref, out_ref):
+    wide, width = shrink_ref.shape
     col = lax.axis_index("dp")
-    x = jnp.concatenate([own_ref[:, :width], came_ref[:, :width]], axis=0)
+    x = rows_of(own_ref, came_ref, width)
     page = jnp.concatenate([own_ref[:, width:], came_ref[:, width:]], axis=0).astype(F32)[:, :1]
-    rows = x.shape[0]
-    order = gather_order(n_dp)
     prod = lax.dot_general(
         x, shrink_ref[...], (((1,), (1,)), ((), ())), preferred_element_type=F32
     )
-    page_of = col * (wide // rank) + lax.broadcasted_iota(I32, (rows, wide), 1) // rank
-    masked = jnp.where(page == page_of.astype(F32), prod, 0.0).astype(BF)
-    grown = jnp.dot(masked, expand_ref[...], preferred_element_type=F32)
+    page_of = col * (wide // rank) + lax.broadcasted_iota(I32, prod.shape, 1) // rank
+    masked = jnp.where(page == page_of.astype(F32), prod, 0.0)
+    out_ref[...] = turned(masked, col, n_dp, gather_order(n_dp), list(range(n_dp))).astype(BF)
+
+
+def expert_kernel(n_dp, own_ref, came_ref, gate_ref, up_ref, out_ref):
+    width, hid = gate_ref.shape
+    col = lax.axis_index("dp")
+    x = rows_of(own_ref, came_ref, width)
     gate = jnp.dot(x, gate_ref[...], preferred_element_type=F32)
     up = jnp.dot(x, up_ref[...], preferred_element_type=F32)
     act = gate / (1.0 + jnp.exp(-gate))
-
-    def put(at, y):
-        y = turned(y, col, n_dp, order, list(range(n_dp)))
-        out_ref[:, at : at + y.shape[1]] = y.astype(BF)
-
-    put(0, act)
-    put(hid, act * up)
-    put(2 * hid, grown)
-
-
-def down_kernel(n_dp, hid, own_ref, came_ref, down_ref, keep_ref, send_ref, add_ref):
+    for i, y in enumerate((act, act * up)):
+        y = turned(y, col, n_dp, gather_order(n_dp), list(range(n_dp)))
+        out_ref[:, i * hid : (i + 1) * hid] = y.astype(BF)
+
+
+def grow_kernel(n_dp, low_ref, low2_ref, expand_ref, expand2_ref, act_ref, out_ref):
+    here = lax.axis_index("dp") & 1
+    width = act_ref.shape[1]
+    hid = width // 2
+    out_ref[:, :width] = act_ref[...]
+    for i in range(n_dp // 2):
+        at = pl.ds(pl.multiple_of((2 * i + here) * hid, hid), hid)
+        part = jnp.dot(low_ref[...], expand_ref[:, at], preferred_element_type=F32)
+        part += jnp.dot(low2_ref[...], expand2_ref[:, at], preferred_element_type=F32)
+        out_ref[:, width + i * hid : width + (i + 1) * hid] = part.astype(BF)
+
+
+def down_kernel(n_dp, hid, own_ref, came_ref, down_ref, down2_ref, keep_ref, send_ref, add_ref):
     col = lax.axis_index("dp")
     order = gather_order(n_dp)
     half = n_dp // 2
-    split = 2 * hid * half
+    each = half // 2
+    split = 2 * hid * each
     rows = own_ref.shape[0]
-    block = rows // n_dp
     part = down_ref.shape[1]
     add_ref[...] = own_ref[:, split:].astype(F32) + came_ref[:, split:].astype(F32)
-    total = jnp.zeros((2 * rows, part), F32)
-    for i, p in enumerate(order):
-        ref = own_ref if i < half else came_ref
-        at = (i % half) * 2 * hid
-        start = pl.multiple_of((p ^ col) * hid, hid)
+    totals = [jnp.zeros((2 * rows, part), F32)] * 2
+    for i, p in enumerate(order[:half]):
+        ref = own_ref if i < each else came_ref
+        at = (i % each) * 2 * hid
+        unit = p ^ col
+        spot = pl.multiple_of((unit // 2) * hid, hid)
+        start = pl.multiple_of(unit * hid, hid)
         act = ref[:, at : at + hid]
         first = ref[:, at + hid : at + 2 * hid]
-        second = (act.astype(F32) * add_ref[:, pl.ds(start, hid)]).astype(BF)
+        second = (act.astype(F32) * add_ref[:, pl.ds(spot, hid)]).astype(BF)
         both = jnp.concatenate([first, second], axis=0)
-        total += jnp.dot(both, down_ref[pl.ds(start, hid), :], preferred_element_type=F32)
-    out = total[:rows] + total[rows:]
-    out = turned(out, col, n_dp, list(range(n_dp)), order)
-    for i in range(n_dp):
-        ref = keep_ref if i < half else send_ref
-        at = (i % half) * part
-        ref[:, at : at + part] = out[i * block : (i + 1) * block].astype(BF)
+        for k, weight in enumerate((down_ref, down2_ref)):
+            totals[k] += jnp.dot(both, weight[pl.ds(start, hid), :], preferred_element_type=F32)
+    for k in range(2):
+        out = totals[k][:rows] + totals[k][rows:]
+        out = turned(out, col, n_dp, list(range(n_dp)), order)
+        keep_ref[:, k * part : (k + 1) * part] = out[: rows // 2]
+        send_ref[:, (1 - k) * part : (2 - k) * part] = out[rows // 2 :].astype(BF)
 
 
 def mix_kernel(n_dp, part, mix_ref, kept_ref, came_ref, out_ref):
@@ -219,34 +243,27 @@
         rows = n_dp * block
         half = n_dp // 2
         shape = jax.ShapeDtypeStruct
-        topk = routing.shape[1]
-        lanes = max(tenant_page_lookup.shape[1], topk, tok_count)
-
-        def wide(x, rows):
-            return jnp.pad(x, ((0, rows - x.shape[0]), (0, lanes - x.shape[1])))
-
-        meta = jnp.concatenate(
-            [
-                wide(routing, tok_count),
-                wide(gate_quantized, tok_count),
-                wide(tenant[None], tok_count),
-                wide(tenant_page_lookup, experts),
-            ],
-            axis=0,
-        )
-        sent, mix = call(
-            lambda *refs: slot_kernel(topk, *refs),
-            (shape((block, width + TAIL), BF), shape((tok_count, block), F32)),
-            2,
-        )(tokens, meta)
-
-        state = sent.reshape(n_exp, cap, width + TAIL)
-        state = {r: state[r : r + 1] for r in range(n_exp)}
+        middle = n_exp // 2
+        kept, sent, mix = call(
+            slot_kernel,
+            (shape((middle, cap, width + TAIL), BF),) * 2 + (shape((tok_count, block), F32),),
+            5,
+            limit=None,
+            in_specs=[VM, VM, VM, pl.BlockSpec(memory_space=pltpu.SMEM), VM],
+        )(tokens, routing, gate_quantized, tenant, tenant_page_lookup)
+
+        state = {}
+        for i in range(middle):
+            state[2 * i], state[2 * i + 1] = kept[i : i + 1], sent[i : i + 1]
         gate_w = gate_weight.reshape(width, hid)
         up_w = up_projection.reshape(width, hid)
         shrink_w = adapter_shrink.reshape(pages * rank, width)
         expand_w = adapter_expand.reshape(pages * rank, hidden_all)
-        early = [(gate_w,), (gate_w, up_w)]
+        down_w = down_weight.reshape(-1, part)
+        expand2 = swap(expand_w, "dp", n_dp, 1)
+        down2 = swap(down_w, "dp", n_dp, 1)
+        plan = [(), (expand2, down2), (gate_w, up_w), (gate_w, up_w, shrink_w, expand_w)]
+        early = plan[:2]
         for mask in bits_of(n_exp):
             state = stage(state, "expert", n_exp, mask, 0, early.pop(0) if early else ())
         own = jnp.concatenate([state[r] for r in range(n_exp)], axis=0)
@@ -254,49 +271,51 @@
         masks = list(reversed(bits_of(n_dp)))
         for mask in masks[:-1]:
             other = swap(own, "dp", n_dp, mask)
-            own = jnp.concatenate([hold(own, gate_w, up_w, shrink_w, expand_w), other], axis=0)
+            own = jnp.concatenate([hold(own, *plan[2]), other], axis=0)
         came = swap(own, "dp", n_dp, masks[-1])
+        if plan[3]:
+            own = hold(own, *plan[3])
+        low = call(
+            lambda *refs: shrink_kernel(n_dp, rank, *refs), shape((rows, pages * rank), BF), 3
+        )(own, came, shrink_w)
+        low2 = swap(low, "dp", n_dp, 1)
+        acts = call(
+            lambda *refs: expert_kernel(n_dp, *refs),
+            shape((rows, 2 * hid), BF),
+            4,
+            cost_estimate=pl.CostEstimate(
+                flops=4 * rows * width * hid, bytes_accessed=4 * width * hid, transcendentals=0
+            ),
+        )(own, came, gate_w, up_w)
         packed = call(
-            lambda *refs: expert_kernel(n_dp, rank, *refs),
-            shape((rows, 2 * hid + hidden_all), BF),
-            6,
-        )(
-            own,
-            came,
-            gate_w,
-            up_w,
-            shrink_w,
-            expand_w,
-        )
-
-        for mask in masks[:-1]:
+            lambda *refs: grow_kernel(n_dp, *refs), shape((rows, 2 * hid + hidden_all // 2), BF), 5
+        )(low, low2, expand_w, expand2, acts)
+
+        for mask in masks[:-2]:
             other = swap(packed, "dp", n_dp, mask)
-            at = packed.shape[1] - hidden_all
+            at = packed.shape[1] - hidden_all // 2
             packed = jnp.concatenate(
                 [packed[:, :at], other[:, :at], packed[:, at:] + other[:, at:]], axis=1
             )
-        other = swap(packed, "dp", n_dp, masks[-1])
+        other = swap(packed, "dp", n_dp, masks[-2])
         keep, send = call(
             lambda *refs: down_kernel(n_dp, hid, *refs),
-            (shape((block, half * part), BF),) * 2,
-            3,
-            scratch_shapes=[pltpu.VMEM((rows, hidden_all), F32)],
-        )(packed, other, down_weight.reshape(-1, part))
+            (shape((rows // 2, 2 * part), F32), shape((rows // 2, 2 * part), BF)),
+            4,
+            scratch_shapes=[pltpu.VMEM((rows, hidden_all // 2), F32)],
+        )(packed, other, down_w, down2)
 
         back = swap(send, "dp", n_dp, 1)
-        order = gather_order(n_dp)
-        state = {}
-        for i, q in enumerate(order[:half]):
-            state[q] = keep[:, i * part : (i + 1) * part]
-            state[q ^ 1] = back[:, i * part : (i + 1) * part]
+        both = (keep + back.astype(F32)).astype(BF)
+        order = gather_order(n_dp)[:half]
+        state = {q: both[i * block : (i + 1) * block] for i, q in enumerate(order)}
         for mask in bits_of(n_dp)[1:]:
-            state = stage(state, "dp", n_dp, mask, 1)
-        home = jnp.concatenate([state[q] for q in range(n_dp)], axis=1)
+            state = stage(state, "dp", n_dp, mask, 0)
+        home = jnp.concatenate([state[q] for q in sorted(state)], axis=1)
         home = home.reshape(n_exp, cap, n_dp * part)
         state = {r: home[r : r + 1] for r in range(n_exp)}
         for mask in bits_of(n_exp)[:-1]:
             state = stage(state, "expert", n_exp, mask, 0)
-        middle = n_exp // 2
         kept = jnp.concatenate([state[r] for r in range(middle)], axis=0)
         sent = jnp.concatenate([state[r] for r in range(middle, n_exp)], axis=0)
         came = swap(sent, "expert", n_exp, middle)

time: 42 us -> 40.3 us (0.960)
  waiting for transfers between devices: 14.3 us -> 12.6 us
  Pallas kernels: 3.19 us -> 4.75 us
  local copies, waits for them, and re-layouts: 5.85 us -> 4.62 us
  other arithmetic: 1.22 us -> 0.42 us
  starting transfers between devices: 16.9 us -> 17.6 us
    unnamed x18, local copies, waits for them, and re-layouts: 5.62 us -> 3.77 us
    ppermute x10 -> x12, waiting for transfers between devices: 14.3 us -> 12.6 us  [swap(): return lax.ppermute(x, axis, [(i, i ^ mask) for i in range(size)])]
    pallas_call x3 -> x5, Pallas kernels: 2.37 us -> 3.93 us  [the longest x1 2.06 us: per_device(): call(slot_kernel, (shape((middle, cap, width + TAIL), BF),) * 2 + (shape(...]
    concatenate x4 -> x1, other arithmetic: 0.77 us -> 0.02 us  [per_device(): own = jnp.concatenate([hold(own, *plan[2]), other], axis=0)]
    slice x6 -> x2, local copies, waits for them, and re-layouts: 0.12 us -> 0.77 us  [the longest x1 0.76 us: per_device(): state[2 * i], state[2 * i + 1] = (kept[i:i + 1], sent[i:i + 1])]
    ppermute x10 -> x12, starting transfers between devices: 16.9 us -> 17.6 us  [swap(): return lax.ppermute(x, axis, [(i, i ^ mask) for i in range(size)])]
  transfers between devices with their start and end apart: 10 -> 12, of which waited for: 10 -> 10; matrix products, arithmetic and copies ran while one was open for 0% -> 2% of each run, Pallas kernels for 0% -> 2%
where the time goes in v3:
time: 40.3 us; the launch traced here: 40.1 us
  starting transfers between devices  17.6 us (44%)
  waiting for transfers between devices  12.6 us (31%)
  Pallas kernels  4.75 us (12%)
  local copies, waits for them, and re-layouts  4.62 us (11%)
  other arithmetic  0.42 us (1%)
    ppermute x12, starting transfers between devices, swap(): return lax.ppermute(x, axis, [(i, i ^ mask) for i in range(size)])  17.6 us
    ppermute x12, waiting for transfers between devices, swap(): return lax.ppermute(x, axis, [(i, i ^ mask) for i in range(size)])  12.6 us
    unnamed x18, local copies, waits for them, and re-layouts  3.77 us
    pallas_call x1, Pallas kernels, per_device(): call(slot_kernel, (shape((middle, cap, width + TAIL), BF),) * 2 + (shape(...  2.06 us
    pallas_call x1, Pallas kernels, per_device(): call(lambda *refs: expert_kernel(n_dp, *refs), shape((rows, 2 * hid), BF)...  0.85 us
  transfers between devices with their start and end apart: 12, of which 10 were waited for; matrix products, arithmetic and copies ran while one was open for 2% of the time, Pallas kernels for 2%

profile of v3, /device:TPU:0, one launch (start us, length us, event | category | flops | bytes accessed | tf_op | source)
XLA Modules:
  0.0 40.1 jit_solution(14356980760851781779)
XLA Ops:
  0.0 2.1 %shard_map.100 = (bf16[2,2,4224]{2,1,0:T(2,128)(2,1)}, bf16[2,2,4224]{2,1,0:T(2,128)(2,1)}, f32[8,8]{1,0:T(8,128)}) custom-call(bf16[8,4096]{1,0:T(8,128)(2,1)} %tok_ref.1, s32[8,8]{1,0:T(8,128)} %routing_ref.1, s32[8,8]{1,0:T(8,128)} %gate_ref.1, s32[8]{0:T(128)} %tenant_ref.1, s32[4,24]{1,0:T(4,128)} %lookup_ref.1), custom_call_target="tpu_custom_call" | custom-call | tf_op jit(solution)/shard_map/pallas_call | solution.py:247
  2.1 3.0 %collective-permute-start = (bf16[2,2,4224]{2,1,0:T(2,128)(2,1)}, bf16[2,2,4224]{2,1,0:T(2,128)(2,1)S(1)}, u32[]{:S(2)}, u32[]{:S(2)}) collective-permute-start(bf16[2,2,4224]{2,1,0:T(2,128)(2,1)} %get-tuple-element.12), channel_id=1, source_target_pairs={{0,4},{4,0},{8,12},{12,8},{1,5},{5,1},{9,13},{13,9},{2,6},{6,2},{1... | collective-permute-start | bytes 101384 | tf_op jit(solution)/shard_map/ppermute | solution.py:17
  5.1 0.5 %collective-permute-start.2 = (bf16[1024,1024]{1,0:T(8,128)(2,1)}, bf16[1024,1024]{1,0:T(8,128)(2,1)S(1)}, u32[]{:S(2)}, u32[]{:S(2)}) collective-permute-start(bf16[1024,1024]{1,0:T(8,128)(2,1)} %bitcast.21), channel_id=1, source_target_pairs={{0,1},{1,0},{2,3},{3,2},{4,5},{5,4},{6,7},{7,6},{8,9},{9,8},{10,11... | collective-permute-start | bytes 6291464 | tf_op jit(solution)/shard_map/ppermute | solution.py:17
  5.6 0.8 %fusion.8 = (bf16[1,2,4224]{2,1,0:T(2,128)(2,1)S(1)}, bf16[1,2,4224]{2,1,0:T(2,128)(2,1)S(1)}) fusion(bf16[2,2,4224]{2,1,0:T(2,128)(2,1)} %get-tuple-element.11), kind=kLoop, calls=%fused_computation.23 | loop fusion | bytes 67584 | tf_op jit(solution)/shard_map/slice | solution.py:257
  6.4 0.8 %collective-permute-done = bf16[2,2,4224]{2,1,0:T(2,128)(2,1)S(1)} collective-permute-done((bf16[2,2,4224]{2,1,0:T(2,128)(2,1)}, bf16[2,2,4224]{2,1,0:T(2,128)(2,1)S(1)}, u32[]{:S(2)}, u32[]{:S(2)}) %collective-permute-start) | collective-permute-done | bytes 33824 | tf_op jit(solution)/shard_map/ppermute | solution.py:17
  7.3 3.1 %collective-permute-start.3 = (bf16[2,2,4224]{2,1,0:T(2,128)(2,1)S(1)}, bf16[2,2,4224]{2,1,0:T(2,128)(2,1)S(1)}, u32[]{:S(2)}, u32[]{:S(2)}) collective-permute-start(bf16[2,2,4224]{2,1,0:T(2,128)(2,1)S(1)} %pad_maximum_fusion.3), channel_id=1, source_target_pairs={{0,8},{4,12},{8,0},{12,4},{1,9},{5,13},{9,1},{13,5},{2,10},{6,14},... | collective-permute-start | bytes 101384 | tf_op jit(solution)/shard_map/ppermute | solution.py:17
  10.5 1.3 %copy-done.3 = bf16[1024,1024]{1,0:T(8,128)(2,1)} copy-done((bf16[1024,1024]{1,0:T(8,128)(2,1)}, bf16[1024,1024]{1,0:T(8,128)(2,1)S(1)}, u32[]{:S(2)}) %copy-start.3) | copy-done | bytes 2097176
  11.8 0.5 %collective-permute-done.3 = bf16[2,2,4224]{2,1,0:T(2,128)(2,1)S(1)} collective-permute-done((bf16[2,2,4224]{2,1,0:T(2,128)(2,1)S(1)}, bf16[2,2,4224]{2,1,0:T(2,128)(2,1)S(1)}, u32[]{:S(2)}, u32[]{:S(2)}) %collective-permute-start.3) | collective-permute-done | bytes 33824 | tf_op jit(solution)/shard_map/ppermute | solution.py:17
  12.3 0.1 pad_maximum_fusion.1
  12.4 1.9 %collective-permute-start.4 = (bf16[8,4224]{1,0:T(8,128)(2,1)S(1)}, bf16[8,4224]{1,0:T(8,128)(2,1)S(1)}, u32[]{:S(2)}, u32[]{:S(2)}) collective-permute-start(bf16[8,4224]{1,0:T(8,128)(2,1)S(1)} %reshape.25.x_ref), channel_id=1, source_target_pairs={{0,2},{1,3},{2,0},{3,1},{4,6},{5,7},{6,4},{7,5},{8,10},{9,11},{10,... | collective-permute-start | bytes 202760 | tf_op jit(solution)/shard_map/ppermute | solution.py:17
  14.3 1.6 %copy-done.1 = bf16[1,4096,256]{2,1,0:T(8,128)(2,1)S(1)} copy-done((bf16[1,4096,256]{2,1,0:T(8,128)(2,1)S(1)}, bf16[1,4096,256]{2,1,0:T(8,128)(2,1)}, u32[]{:S(2)}) %copy-start.1) | copy-done | bytes 2097176
  15.9 0.9 %collective-permute-done.4 = bf16[8,4224]{1,0:T(8,128)(2,1)S(1)} collective-permute-done((bf16[8,4224]{1,0:T(8,128)(2,1)S(1)}, bf16[8,4224]{1,0:T(8,128)(2,1)S(1)}, u32[]{:S(2)}, u32[]{:S(2)}) %collective-permute-start.4) | collective-permute-done | bytes 67616 | tf_op jit(solution)/shard_map/ppermute | solution.py:17
  16.9 0.6 %copy-done.2 = bf16[1,4096,256]{2,1,0:T(8,128)(2,1)S(1)} copy-done((bf16[1,4096,256]{2,1,0:T(8,128)(2,1)S(1)}, bf16[1,4096,256]{2,1,0:T(8,128)(2,1)}, u32[]{:S(2)}) %copy-start.2) | copy-done | bytes 2097176
  17.5 0.2 copy-done.5
  17.7 0.5 %collective-permute-done.5.refs_1_ = bf16[16,4224]{1,0:T(8,128)(2,1)S(1)} collective-permute-done((bf16[16,4224]{1,0:T(8,128)(2,1)S(1)}, bf16[16,4224]{1,0:T(8,128)(2,1)S(1)}, u32[]{:S(2)}, u32[]{:S(2)}) %collective-permute-start.5) | collective-permute-done | bytes 135200 | tf_op jit(solution)/shard_map/ppermute | solution.py:17
  18.2 0.4 shard_map.104.refs_0_
  18.6 0.2 collective-permute-start.6
  18.8 0.8 %shard_map.105.refs_4_ = bf16[32,512]{1,0:T(8,128)(2,1)S(1)} custom-call(bf16[16,4224]{1,0:T(8,128)(2,1)S(1)} %shard_map.103.refs_0_, bf16[16,4224]{1,0:T(8,128)(2,1)S(1)} %collective-permute-done.5.refs_1_, bf16[4096,256]{1,0:T(8,128)(2,1)S(1)} %bitcast.15, bf16[4096,256]{1,0:T(8,128)(2,1)S(1)} %bitcast.18), custom_call_target="tpu_custom_call" | custom-call | flops 134217728 | bytes 4194304 | tf_op jit(solution)/shard_map/pallas_call | solution.py:282
  19.7 0.2 collective-permute-done.6.refs_1_
  19.9 0.1 shard_map.106.refs_0_
  20.0 1.9 %collective-permute-start.7 = (bf16[32,1024]{1,0:T(8,128)(2,1)S(1)}, bf16[32,1024]{1,0:T(8,128)(2,1)S(1)}, u32[]{:S(2)}, u32[]{:S(2)}) collective-permute-start(bf16[32,1024]{1,0:T(8,128)(2,1)S(1)} %shard_map.106.refs_0_), channel_id=1, source_target_pairs={{0,2},{1,3},{2,0},{3,1},{4,6},{5,7},{6,4},{7,5},{8,10},{9,11},{10,... | collective-permute-start | bytes 196616 | tf_op jit(solution)/shard_map/ppermute | solution.py:17
  21.9 2.5 %collective-permute-done.7.refs_1_ = bf16[32,1024]{1,0:T(8,128)(2,1)S(1)} collective-permute-done((bf16[32,1024]{1,0:T(8,128)(2,1)S(1)}, bf16[32,1024]{1,0:T(8,128)(2,1)S(1)}, u32[]{:S(2)}, u32[]{:S(2)}) %collective-permute-start.7) | collective-permute-done | bytes 65568 | tf_op jit(solution)/shard_map/ppermute | solution.py:17
  24.4 0.5 %shard_map.107 = (f32[16,2048]{1,0:T(8,128)S(1)}, bf16[16,2048]{1,0:T(8,128)(2,1)S(1)}) custom-call(bf16[32,1024]{1,0:T(8,128)(2,1)S(1)} %shard_map.106.refs_0_, bf16[32,1024]{1,0:T(8,128)(2,1)S(1)} %collective-permute-done.7.refs_1_, bf16[1024,1024]{1,0:T(8,128)(2,1)S(1)} %bitcast.22, bf16[1024,1024]{1,0:T(8,128)(2,1)S(1)} %copy-done.4), custom_call_target="tpu_custom_call" | custom-call | tf_op jit(solution)/shard_map/pallas_call | solution.py:301
  24.9 0.1 collective-permute-start.8
  25.0 1.2 %collective-permute-done.8 = bf16[16,2048]{1,0:T(8,128)(2,1)S(1)} collective-permute-done((bf16[16,2048]{1,0:T(8,128)(2,1)S(1)}, bf16[16,2048]{1,0:T(8,128)(2,1)S(1)}, u32[]{:S(2)}, u32[]{:S(2)}) %collective-permute-start.8) | collective-permute-done | bytes 65568 | tf_op jit(solution)/shard_map/ppermute | solution.py:17
  26.2 1.9 %collective-permute-start.9 = (bf16[8,2048]{1,0:T(8,128)(2,1)S(1)}, bf16[8,2048]{1,0:T(8,128)(2,1)S(1)}, u32[]{:S(2)}, u32[]{:S(2)}) collective-permute-start(bf16[8,2048]{1,0:T(8,128)(2,1)S(1)} %get-tuple-element.20), channel_id=1, source_target_pairs={{0,2},{1,3},{2,0},{3,1},{4,6},{5,7},{6,4},{7,5},{8,10},{9,11},{10,... | collective-permute-start | bytes 98312 | tf_op jit(solution)/shard_map/ppermute | solution.py:17
  28.1 2.1 %collective-permute-done.9 = bf16[8,2048]{1,0:T(8,128)(2,1)S(1)} collective-permute-done((bf16[8,2048]{1,0:T(8,128)(2,1)S(1)}, bf16[8,2048]{1,0:T(8,128)(2,1)S(1)}, u32[]{:S(2)}, u32[]{:S(2)}) %collective-permute-start.9) | collective-permute-done | bytes 32800 | tf_op jit(solution)/shard_map/ppermute | solution.py:17
  30.3 1.9 %collective-permute-start.10 = (bf16[2,2,4096]{2,1,0:T(2,128)(2,1)S(1)}, bf16[2,2,4096]{2,1,0:T(2,128)(2,1)S(1)}, u32[]{:S(2)}, u32[]{:S(2)}) collective-permute-start(bf16[2,2,4096]{2,1,0:T(2,128)(2,1)S(1)} %pad_maximum_fusion.4), channel_id=1, source_target_pairs={{0,4},{4,0},{8,12},{12,8},{1,5},{5,1},{9,13},{13,9},{2,6},{6,2},{1... | collective-permute-start | bytes 98312 | tf_op jit(solution)/shard_map/ppermute | solution.py:17
  32.3 2.0 %collective-permute-done.10 = bf16[2,2,4096]{2,1,0:T(2,128)(2,1)S(1)} collective-permute-done((bf16[2,2,4096]{2,1,0:T(2,128)(2,1)S(1)}, bf16[2,2,4096]{2,1,0:T(2,128)(2,1)S(1)}, u32[]{:S(2)}, u32[]{:S(2)}) %collective-permute-start.10) | collective-permute-done | bytes 32800 | tf_op jit(solution)/shard_map/ppermute | solution.py:17
  34.4 3.0 %collective-permute-start.11 = (bf16[2,2,4096]{2,1,0:T(2,128)(2,1)S(1)}, bf16[2,2,4096]{2,1,0:T(2,128)(2,1)S(1)}, u32[]{:S(2)}, u32[]{:S(2)}) collective-permute-start(bf16[2,2,4096]{2,1,0:T(2,128)(2,1)S(1)} %pad_maximum_fusion.6), channel_id=1, source_target_pairs={{0,8},{4,12},{8,0},{12,4},{1,9},{5,13},{9,1},{13,5},{2,10},{6,14},... | collective-permute-start | bytes 98312 | tf_op jit(solution)/shard_map/ppermute | solution.py:17
  37.4 1.8 %collective-permute-done.11.refs_2_ = bf16[2,2,4096]{2,1,0:T(2,128)(2,1)S(1)} collective-permute-done((bf16[2,2,4096]{2,1,0:T(2,128)(2,1)S(1)}, bf16[2,2,4096]{2,1,0:T(2,128)(2,1)S(1)}, u32[]{:S(2)}, u32[]{:S(2)}) %collective-permute-start.11) | collective-permute-done | bytes 32800 | tf_op jit(solution)/shard_map/ppermute | solution.py:17
  39.3 0.8 %shard_map.108 = bf16[8,4096]{1,0:T(8,128)(2,1)} custom-call(f32[8,8]{1,0:T(8,128)S(1)} %copy-done.8, bf16[2,2,4096]{2,1,0:T(2,128)(2,1)S(1)} %pad_maximum_fusion.5.refs_1_, bf16[2,2,4096]{2,1,0:T(2,128)(2,1)S(1)} %collective-permute-done.11.refs_2_), custom_call_target="tpu_custom_call" | custom-call | tf_op jit(solution)/shard_map/pallas_call | solution.py:322
  (33 shorter events, 0.6 us)
Async XLA Ops:
  0.0 14.3 %copy-start = (bf16[1,4096,256]{2,1,0:T(8,128)(2,1)S(1)}, bf16[1,4096,256]{2,1,0:T(8,128)(2,1)}, u32[]{:S(2)}) copy-start(bf16[1,4096,256]{2,1,0:T(8,128)(2,1)} %param.15) | copy-start | bytes 6291460
  2.1 5.1 %collective-permute-start = (bf16[2,2,4224]{2,1,0:T(2,128)(2,1)}, bf16[2,2,4224]{2,1,0:T(2,128)(2,1)S(1)}, u32[]{:S(2)}, u32[]{:S(2)}) collective-permute-start(bf16[2,2,4224]{2,1,0:T(2,128)(2,1)} %get-tuple-element.12), channel_id=1, source_target_pairs={{0,4},{4,0},{8,12},{12,8},{1,5},{5,1},{9,13},{13,9},{2,6},{6,2},{1... | collective-permute-start | bytes 101384 | tf_op jit(solution)/shard_map/ppermute | solution.py:17
  5.1 5.4 %collective-permute-start.1 = (bf16[96,1024]{1,0:T(8,128)(2,1)}, bf16[96,1024]{1,0:T(8,128)(2,1)S(1)}, u32[]{:S(2)}, u32[]{:S(2)}) collective-permute-start(bf16[96,1024]{1,0:T(8,128)(2,1)} %bitcast.23), channel_id=1, source_target_pairs={{0,1},{1,0},{2,3},{3,2},{4,5},{5,4},{6,7},{7,6},{8,9},{9,8},{10,11... | collective-permute-start | bytes 589832 | tf_op jit(solution)/shard_map/ppermute | solution.py:17
  5.1 5.4 %collective-permute-start.2 = (bf16[1024,1024]{1,0:T(8,128)(2,1)}, bf16[1024,1024]{1,0:T(8,128)(2,1)S(1)}, u32[]{:S(2)}, u32[]{:S(2)}) collective-permute-start(bf16[1024,1024]{1,0:T(8,128)(2,1)} %bitcast.21), channel_id=1, source_target_pairs={{0,1},{1,0},{2,3},{3,2},{4,5},{5,4},{6,7},{7,6},{8,9},{9,8},{10,11... | collective-permute-start | bytes 6291464 | tf_op jit(solution)/shard_map/ppermute | solution.py:17
  7.3 5.0 %collective-permute-start.3 = (bf16[2,2,4224]{2,1,0:T(2,128)(2,1)S(1)}, bf16[2,2,4224]{2,1,0:T(2,128)(2,1)S(1)}, u32[]{:S(2)}, u32[]{:S(2)}) collective-permute-start(bf16[2,2,4224]{2,1,0:T(2,128)(2,1)S(1)} %pad_maximum_fusion.3), channel_id=1, source_target_pairs={{0,8},{4,12},{8,0},{12,4},{1,9},{5,13},{9,1},{13,5},{2,10},{6,14},... | collective-permute-start | bytes 101384 | tf_op jit(solution)/shard_map/ppermute | solution.py:17
  10.5 1.3 %copy-start.3 = (bf16[1024,1024]{1,0:T(8,128)(2,1)}, bf16[1024,1024]{1,0:T(8,128)(2,1)S(1)}, u32[]{:S(2)}) copy-start(bf16[1024,1024]{1,0:T(8,128)(2,1)S(1)} %collective-permute-done.2.refs_1_.refs_3_) | copy-start | bytes 6291460
  12.4 4.4 %collective-permute-start.4 = (bf16[8,4224]{1,0:T(8,128)(2,1)S(1)}, bf16[8,4224]{1,0:T(8,128)(2,1)S(1)}, u32[]{:S(2)}, u32[]{:S(2)}) collective-permute-start(bf16[8,4224]{1,0:T(8,128)(2,1)S(1)} %reshape.25.x_ref), channel_id=1, source_target_pairs={{0,2},{1,3},{2,0},{3,1},{4,6},{5,7},{6,4},{7,5},{8,10},{9,11},{10,... | collective-permute-start | bytes 202760 | tf_op jit(solution)/shard_map/ppermute | solution.py:17
  14.3 1.6 %copy-start.1 = (bf16[1,4096,256]{2,1,0:T(8,128)(2,1)S(1)}, bf16[1,4096,256]{2,1,0:T(8,128)(2,1)}, u32[]{:S(2)}) copy-start(bf16[1,4096,256]{2,1,0:T(8,128)(2,1)} %param.16) | copy-start | bytes 6291460
  15.9 1.6 %copy-start.2 = (bf16[1,4096,256]{2,1,0:T(8,128)(2,1)S(1)}, bf16[1,4096,256]{2,1,0:T(8,128)(2,1)}, u32[]{:S(2)}) copy-start(bf16[1,4096,256]{2,1,0:T(8,128)(2,1)} %param.16) | copy-start | bytes 6291460
  15.9 1.8 %copy-start.5 = (bf16[1,6,16,4096]{3,2,1,0:T(8,128)(2,1)S(1)}, bf16[1,6,16,4096]{3,2,1,0:T(8,128)(2,1)}, u32[]{:S(2)}) copy-start(bf16[1,6,16,4096]{3,2,1,0:T(8,128)(2,1)} %param.18) | copy-start | bytes 2359300
  15.9 1.8 %copy-start.7 = (bf16[1,6,16,1024]{3,2,1,0:T(8,128)(2,1)S(1)}, bf16[1,6,16,1024]{3,2,1,0:T(8,128)(2,1)}, u32[]{:S(2)}) copy-start(bf16[1,6,16,1024]{3,2,1,0:T(8,128)(2,1)} %param.19) | copy-start | bytes 589828
  16.8 1.4 %collective-permute-start.5 = (bf16[16,4224]{1,0:T(8,128)(2,1)S(1)}, bf16[16,4224]{1,0:T(8,128)(2,1)S(1)}, u32[]{:S(2)}, u32[]{:S(2)}) collective-permute-start(bf16[16,4224]{1,0:T(8,128)(2,1)S(1)} %pad_maximum_fusion.x_ref), channel_id=1, source_target_pairs={{0,1},{1,0},{2,3},{3,2},{4,5},{5,4},{6,7},{7,6},{8,9},{9,8},{10,11... | collective-permute-start | bytes 405512 | tf_op jit(solution)/shard_map/ppermute | solution.py:17
  18.6 5.8 %copy-start.4 = (bf16[1024,1024]{1,0:T(8,128)(2,1)S(1)}, bf16[1024,1024]{1,0:T(8,128)(2,1)}, u32[]{:S(2)}) copy-start(bf16[1024,1024]{1,0:T(8,128)(2,1)} %copy-done.3) | copy-start | bytes 6291460
  18.6 5.8 %copy-start.6 = (bf16[1,1024,1024]{2,1,0:T(8,128)(2,1)S(1)}, bf16[1,1024,1024]{2,1,0:T(8,128)(2,1)}, u32[]{:S(2)}) copy-start(bf16[1,1024,1024]{2,1,0:T(8,128)(2,1)} %param.17) | copy-start | bytes 6291460
  18.6 1.2 %collective-permute-start.6 = (bf16[32,96]{1,0:T(8,128)(2,1)S(1)}, bf16[32,96]{1,0:T(8,128)(2,1)S(1)}, u32[]{:S(2)}, u32[]{:S(2)}) collective-permute-start(bf16[32,96]{1,0:T(8,128)(2,1)S(1)} %shard_map.104.refs_0_), channel_id=1, source_target_pairs={{0,1},{1,0},{2,3},{3,2},{4,5},{5,4},{6,7},{7,6},{8,9},{9,8},{10,11... | collective-permute-start | bytes 18440 | tf_op jit(solution)/shard_map/ppermute | solution.py:17
  20.0 19.3 %copy-start.8 = (f32[8,8]{1,0:T(8,128)S(1)}, f32[8,8]{1,0:T(8,128)}, u32[]{:S(2)}) copy-start(f32[8,8]{1,0:T(8,128)} %get-tuple-element.10.refs_0_) | copy-start | bytes 772
  20.0 4.4 %collective-permute-start.7 = (bf16[32,1024]{1,0:T(8,128)(2,1)S(1)}, bf16[32,1024]{1,0:T(8,128)(2,1)S(1)}, u32[]{:S(2)}, u32[]{:S(2)}) collective-permute-start(bf16[32,1024]{1,0:T(8,128)(2,1)S(1)} %shard_map.106.refs_0_), channel_id=1, source_target_pairs={{0,2},{1,3},{2,0},{3,1},{4,6},{5,7},{6,4},{7,5},{8,10},{9,11},{10,... | collective-permute-start | bytes 196616 | tf_op jit(solution)/shard_map/ppermute | solution.py:17
  24.9 1.3 %collective-permute-start.8 = (bf16[16,2048]{1,0:T(8,128)(2,1)S(1)}, bf16[16,2048]{1,0:T(8,128)(2,1)S(1)}, u32[]{:S(2)}, u32[]{:S(2)}) collective-permute-start(bf16[16,2048]{1,0:T(8,128)(2,1)S(1)} %get-tuple-element.14), channel_id=1, source_target_pairs={{0,1},{1,0},{2,3},{3,2},{4,5},{5,4},{6,7},{7,6},{8,9},{9,8},{10,11... | collective-permute-start | bytes 196616 | tf_op jit(solution)/shard_map/ppermute | solution.py:17
  26.2 4.0 %collective-permute-start.9 = (bf16[8,2048]{1,0:T(8,128)(2,1)S(1)}, bf16[8,2048]{1,0:T(8,128)(2,1)S(1)}, u32[]{:S(2)}, u32[]{:S(2)}) collective-permute-start(bf16[8,2048]{1,0:T(8,128)(2,1)S(1)} %get-tuple-element.20), channel_id=1, source_target_pairs={{0,2},{1,3},{2,0},{3,1},{4,6},{5,7},{6,4},{7,5},{8,10},{9,11},{10,... | collective-permute-start | bytes 98312 | tf_op jit(solution)/shard_map/ppermute | solution.py:17
  30.3 4.0 %collective-permute-start.10 = (bf16[2,2,4096]{2,1,0:T(2,128)(2,1)S(1)}, bf16[2,2,4096]{2,1,0:T(2,128)(2,1)S(1)}, u32[]{:S(2)}, u32[]{:S(2)}) collective-permute-start(bf16[2,2,4096]{2,1,0:T(2,128)(2,1)S(1)} %pad_maximum_fusion.4), channel_id=1, source_target_pairs={{0,4},{4,0},{8,12},{12,8},{1,5},{5,1},{9,13},{13,9},{2,6},{6,2},{1... | collective-permute-start | bytes 98312 | tf_op jit(solution)/shard_map/ppermute | solution.py:17
  34.4 4.9 %collective-permute-start.11 = (bf16[2,2,4096]{2,1,0:T(2,128)(2,1)S(1)}, bf16[2,2,4096]{2,1,0:T(2,128)(2,1)S(1)}, u32[]{:S(2)}, u32[]{:S(2)}) collective-permute-start(bf16[2,2,4096]{2,1,0:T(2,128)(2,1)S(1)} %pad_maximum_fusion.6), channel_id=1, source_target_pairs={{0,8},{4,12},{8,0},{12,4},{1,9},{5,13},{9,1},{13,5},{2,10},{6,14},... | collective-permute-start | bytes 98312 | tf_op jit(solution)/shard_map/ppermute | solution.py:17

commit v4 on v3

--- a/solution.py
+++ b/solution.py
@@ -118,24 +118,34 @@
     gate = jnp.dot(x, gate_ref[...], preferred_element_type=F32)
     up = jnp.dot(x, up_ref[...], preferred_element_type=F32)
     act = gate / (1.0 + jnp.exp(-gate))
-    for i, y in enumerate((act, act * up)):
+    for i, y in enumerate((act, up)):
         y = turned(y, col, n_dp, gather_order(n_dp), list(range(n_dp)))
-        out_ref[:, i * hid : (i + 1) * hid] = y.astype(BF)
+        out_ref[:, i * hid : (i + 1) * hid] = y
 
 
 def grow_kernel(n_dp, low_ref, low2_ref, expand_ref, expand2_ref, act_ref, out_ref):
-    here = lax.axis_index("dp") & 1
-    width = act_ref.shape[1]
-    hid = width // 2
-    out_ref[:, :width] = act_ref[...]
-    for i in range(n_dp // 2):
-        at = pl.ds(pl.multiple_of((2 * i + here) * hid, hid), hid)
-        part = jnp.dot(low_ref[...], expand_ref[:, at], preferred_element_type=F32)
-        part += jnp.dot(low2_ref[...], expand2_ref[:, at], preferred_element_type=F32)
-        out_ref[:, width + i * hid : width + (i + 1) * hid] = part.astype(BF)
-
-
-def down_kernel(n_dp, hid, own_ref, came_ref, down_ref, down2_ref, keep_ref, send_ref, add_ref):
+    col = lax.axis_index("dp")
+    hid = act_ref.shape[1] // 2
+    half = n_dp // 2
+
+    def update(unit):
+        at = pl.ds(pl.multiple_of(unit * hid, hid), hid)
+        y = jnp.dot(low_ref[...], expand_ref[:, at], preferred_element_type=F32)
+        return y + jnp.dot(low2_ref[...], expand2_ref[:, at], preferred_element_type=F32)
+
+    act = act_ref[:, :hid]
+    out_ref[:, :hid] = act.astype(BF)
+    out_ref[:, hid : 2 * hid] = (act * (act_ref[:, hid:] + update(col))).astype(BF)
+    if half == 2:
+        out_ref[:, 2 * hid :] = update(col ^ 2).astype(BF)
+    else:
+        for i in range(half):
+            unit = 2 * i + (col & 1)
+            y = jnp.where(unit == col, 0.0, update(unit))
+            out_ref[:, (2 + i) * hid : (3 + i) * hid] = y.astype(BF)
+
+
+def down_kernel(n_dp, hid, own_ref, came_ref, down_ref, down2_ref, keep_ref, send_ref):
     col = lax.axis_index("dp")
     order = gather_order(n_dp)
     half = n_dp // 2
@@ -143,17 +153,19 @@
     split = 2 * hid * each
     rows = own_ref.shape[0]
     part = down_ref.shape[1]
-    add_ref[...] = own_ref[:, split:].astype(F32) + came_ref[:, split:].astype(F32)
     totals = [jnp.zeros((2 * rows, part), F32)] * 2
     for i, p in enumerate(order[:half]):
-        ref = own_ref if i < each else came_ref
+        ref, other = (own_ref, came_ref) if i < each else (came_ref, own_ref)
         at = (i % each) * 2 * hid
         unit = p ^ col
-        spot = pl.multiple_of((unit // 2) * hid, hid)
         start = pl.multiple_of(unit * hid, hid)
-        act = ref[:, at : at + hid]
+        if half == 2:
+            add = other[:, split:].astype(F32)
+        else:
+            spot = pl.ds(pl.multiple_of(split + (unit // 2) * hid, hid), hid)
+            add = ref[:, spot].astype(F32) + other[:, spot].astype(F32)
         first = ref[:, at + hid : at + 2 * hid]
-        second = (act.astype(F32) * add_ref[:, pl.ds(spot, hid)]).astype(BF)
+        second = (ref[:, at : at + hid].astype(F32) * add).astype(BF)
         both = jnp.concatenate([first, second], axis=0)
         for k, weight in enumerate((down_ref, down2_ref)):
             totals[k] += jnp.dot(both, weight[pl.ds(start, hid), :], preferred_element_type=F32)
@@ -281,19 +293,21 @@
         low2 = swap(low, "dp", n_dp, 1)
         acts = call(
             lambda *refs: expert_kernel(n_dp, *refs),
-            shape((rows, 2 * hid), BF),
+            shape((rows, 2 * hid), F32),
             4,
             cost_estimate=pl.CostEstimate(
                 flops=4 * rows * width * hid, bytes_accessed=4 * width * hid, transcendentals=0
             ),
         )(own, came, gate_w, up_w)
+        split = 2 * hid
+        parts = 1 if half == 2 else half
         packed = call(
-            lambda *refs: grow_kernel(n_dp, *refs), shape((rows, 2 * hid + hidden_all // 2), BF), 5
+            lambda *refs: grow_kernel(n_dp, *refs), shape((rows, split + parts * hid), BF), 5
         )(low, low2, expand_w, expand2, acts)
 
         for mask in masks[:-2]:
             other = swap(packed, "dp", n_dp, mask)
-            at = packed.shape[1] - hidden_all // 2
+            at = packed.shape[1] - parts * hid
             packed = jnp.concatenate(
                 [packed[:, :at], other[:, :at], packed[:, at:] + other[:, at:]], axis=1
             )
@@ -302,7 +316,6 @@
             lambda *refs: down_kernel(n_dp, hid, *refs),
             (shape((rows // 2, 2 * part), F32), shape((rows // 2, 2 * part), BF)),
             4,
-            scratch_shapes=[pltpu.VMEM((rows, hidden_all // 2), F32)],
         )(packed, other, down_w, down2)
 
         back = swap(send, "dp", n_dp, 1)

time: 40.3 us -> 40.1 us (level)
  no operation moved by 1% of the time
where the time goes in v4:
time: 40.1 us; the launch traced here: 39.9 us
  starting transfers between devices  17.6 us (44%)
  waiting for transfers between devices  12.3 us (31%)
  Pallas kernels  4.74 us (12%)
  local copies, waits for them, and re-layouts  4.62 us (12%)
  other arithmetic  0.42 us (1%)
    ppermute x12, starting transfers between devices, swap(): return lax.ppermute(x, axis, [(i, i ^ mask) for i in range(size)])  17.6 us
    ppermute x12, waiting for transfers between devices, swap(): return lax.ppermute(x, axis, [(i, i ^ mask) for i in range(size)])  12.3 us
    unnamed x18, local copies, waits for them, and re-layouts  3.77 us
    pallas_call x1, Pallas kernels, per_device(): call(slot_kernel, (shape((middle, cap, width + TAIL), BF),) * 2 + (shape(...  2.06 us
    pallas_call x1, Pallas kernels, per_device(): call(lambda *refs: expert_kernel(n_dp, *refs), shape((rows, 2 * hid), F32...  0.84 us
  transfers between devices with their start and end apart: 12, of which 10 were waited for; matrix products, arithmetic and copies ran while one was open for 2% of the time, Pallas kernels for 2%

profile of v4, /device:TPU:0, one launch (start us, length us, event | category | flops | bytes accessed | tf_op | source)
XLA Modules:
  0.0 39.9 jit_solution(18432103823489215578)
XLA Ops:
  0.0 2.1 %shard_map.100 = (bf16[2,2,4224]{2,1,0:T(2,128)(2,1)}, bf16[2,2,4224]{2,1,0:T(2,128)(2,1)}, f32[8,8]{1,0:T(8,128)}) custom-call(bf16[8,4096]{1,0:T(8,128)(2,1)} %tok_ref.1, s32[8,8]{1,0:T(8,128)} %routing_ref.1, s32[8,8]{1,0:T(8,128)} %gate_ref.1, s32[8]{0:T(128)} %tenant_ref.1, s32[4,24]{1,0:T(4,128)} %lookup_ref.1), custom_call_target="tpu_custom_call" | custom-call | tf_op jit(solution)/shard_map/pallas_call | solution.py:259
  2.1 3.0 %collective-permute-start = (bf16[2,2,4224]{2,1,0:T(2,128)(2,1)}, bf16[2,2,4224]{2,1,0:T(2,128)(2,1)S(1)}, u32[]{:S(2)}, u32[]{:S(2)}) collective-permute-start(bf16[2,2,4224]{2,1,0:T(2,128)(2,1)} %get-tuple-element.12), channel_id=1, source_target_pairs={{0,4},{4,0},{8,12},{12,8},{1,5},{5,1},{9,13},{13,9},{2,6},{6,2},{1... | collective-permute-start | bytes 101384 | tf_op jit(solution)/shard_map/ppermute | solution.py:17
  5.1 0.5 %collective-permute-start.2 = (bf16[1024,1024]{1,0:T(8,128)(2,1)}, bf16[1024,1024]{1,0:T(8,128)(2,1)S(1)}, u32[]{:S(2)}, u32[]{:S(2)}) collective-permute-start(bf16[1024,1024]{1,0:T(8,128)(2,1)} %bitcast.21), channel_id=1, source_target_pairs={{0,1},{1,0},{2,3},{3,2},{4,5},{5,4},{6,7},{7,6},{8,9},{9,8},{10,11... | collective-permute-start | bytes 6291464 | tf_op jit(solution)/shard_map/ppermute | solution.py:17
  5.6 0.8 %fusion.8 = (bf16[1,2,4224]{2,1,0:T(2,128)(2,1)S(1)}, bf16[1,2,4224]{2,1,0:T(2,128)(2,1)S(1)}) fusion(bf16[2,2,4224]{2,1,0:T(2,128)(2,1)} %get-tuple-element.11), kind=kLoop, calls=%fused_computation.23 | loop fusion | bytes 67584 | tf_op jit(solution)/shard_map/slice | solution.py:269
  6.4 0.8 %collective-permute-done = bf16[2,2,4224]{2,1,0:T(2,128)(2,1)S(1)} collective-permute-done((bf16[2,2,4224]{2,1,0:T(2,128)(2,1)}, bf16[2,2,4224]{2,1,0:T(2,128)(2,1)S(1)}, u32[]{:S(2)}, u32[]{:S(2)}) %collective-permute-start) | collective-permute-done | bytes 33824 | tf_op jit(solution)/shard_map/ppermute | solution.py:17
  7.3 3.1 %collective-permute-start.3 = (bf16[2,2,4224]{2,1,0:T(2,128)(2,1)S(1)}, bf16[2,2,4224]{2,1,0:T(2,128)(2,1)S(1)}, u32[]{:S(2)}, u32[]{:S(2)}) collective-permute-start(bf16[2,2,4224]{2,1,0:T(2,128)(2,1)S(1)} %pad_maximum_fusion.3), channel_id=1, source_target_pairs={{0,8},{4,12},{8,0},{12,4},{1,9},{5,13},{9,1},{13,5},{2,10},{6,14},... | collective-permute-start | bytes 101384 | tf_op jit(solution)/shard_map/ppermute | solution.py:17
  10.5 1.3 %copy-done.3 = bf16[1024,1024]{1,0:T(8,128)(2,1)} copy-done((bf16[1024,1024]{1,0:T(8,128)(2,1)}, bf16[1024,1024]{1,0:T(8,128)(2,1)S(1)}, u32[]{:S(2)}) %copy-start.3) | copy-done | bytes 2097176
  11.8 0.5 %collective-permute-done.3 = bf16[2,2,4224]{2,1,0:T(2,128)(2,1)S(1)} collective-permute-done((bf16[2,2,4224]{2,1,0:T(2,128)(2,1)S(1)}, bf16[2,2,4224]{2,1,0:T(2,128)(2,1)S(1)}, u32[]{:S(2)}, u32[]{:S(2)}) %collective-permute-start.3) | collective-permute-done | bytes 33824 | tf_op jit(solution)/shard_map/ppermute | solution.py:17
  12.3 0.1 pad_maximum_fusion.1
  12.4 1.9 %collective-permute-start.4 = (bf16[8,4224]{1,0:T(8,128)(2,1)S(1)}, bf16[8,4224]{1,0:T(8,128)(2,1)S(1)}, u32[]{:S(2)}, u32[]{:S(2)}) collective-permute-start(bf16[8,4224]{1,0:T(8,128)(2,1)S(1)} %reshape.25.x_ref), channel_id=1, source_target_pairs={{0,2},{1,3},{2,0},{3,1},{4,6},{5,7},{6,4},{7,5},{8,10},{9,11},{10,... | collective-permute-start | bytes 202760 | tf_op jit(solution)/shard_map/ppermute | solution.py:17
  14.3 1.6 %copy-done.1 = bf16[1,4096,256]{2,1,0:T(8,128)(2,1)S(1)} copy-done((bf16[1,4096,256]{2,1,0:T(8,128)(2,1)S(1)}, bf16[1,4096,256]{2,1,0:T(8,128)(2,1)}, u32[]{:S(2)}) %copy-start.1) | copy-done | bytes 2097176
  15.9 0.9 %collective-permute-done.4 = bf16[8,4224]{1,0:T(8,128)(2,1)S(1)} collective-permute-done((bf16[8,4224]{1,0:T(8,128)(2,1)S(1)}, bf16[8,4224]{1,0:T(8,128)(2,1)S(1)}, u32[]{:S(2)}, u32[]{:S(2)}) %collective-permute-start.4) | collective-permute-done | bytes 67616 | tf_op jit(solution)/shard_map/ppermute | solution.py:17
  16.9 0.6 %copy-done.2 = bf16[1,4096,256]{2,1,0:T(8,128)(2,1)S(1)} copy-done((bf16[1,4096,256]{2,1,0:T(8,128)(2,1)S(1)}, bf16[1,4096,256]{2,1,0:T(8,128)(2,1)}, u32[]{:S(2)}) %copy-start.2) | copy-done | bytes 2097176
  17.5 0.2 copy-done.5
  17.7 0.5 %collective-permute-done.5.refs_1_ = bf16[16,4224]{1,0:T(8,128)(2,1)S(1)} collective-permute-done((bf16[16,4224]{1,0:T(8,128)(2,1)S(1)}, bf16[16,4224]{1,0:T(8,128)(2,1)S(1)}, u32[]{:S(2)}, u32[]{:S(2)}) %collective-permute-start.5) | collective-permute-done | bytes 135200 | tf_op jit(solution)/shard_map/ppermute | solution.py:17
  18.2 0.4 shard_map.104.refs_0_
  18.6 0.2 collective-permute-start.6
  18.8 0.8 %shard_map.105.refs_4_ = f32[32,512]{1,0:T(8,128)S(1)} custom-call(bf16[16,4224]{1,0:T(8,128)(2,1)S(1)} %shard_map.103.refs_0_, bf16[16,4224]{1,0:T(8,128)(2,1)S(1)} %collective-permute-done.5.refs_1_, bf16[4096,256]{1,0:T(8,128)(2,1)S(1)} %bitcast.15, bf16[4096,256]{1,0:T(8,128)(2,1)S(1)} %bitcast.18), custom_call_target="tpu_custom_call" | custom-call | flops 134217728 | bytes 4194304 | tf_op jit(solution)/shard_map/pallas_call | solution.py:294
  19.7 0.2 collective-permute-done.6.refs_1_
  19.9 0.1 shard_map.106.refs_0_
  20.0 1.9 %collective-permute-start.7 = (bf16[32,768]{1,0:T(8,128)(2,1)S(1)}, bf16[32,768]{1,0:T(8,128)(2,1)S(1)}, u32[]{:S(2)}, u32[]{:S(2)}) collective-permute-start(bf16[32,768]{1,0:T(8,128)(2,1)S(1)} %shard_map.106.refs_0_), channel_id=1, source_target_pairs={{0,2},{1,3},{2,0},{3,1},{4,6},{5,7},{6,4},{7,5},{8,10},{9,11},{10,... | collective-permute-start | bytes 147464 | tf_op jit(solution)/shard_map/ppermute | solution.py:17
  21.9 2.3 %collective-permute-done.7.refs_1_ = bf16[32,768]{1,0:T(8,128)(2,1)S(1)} collective-permute-done((bf16[32,768]{1,0:T(8,128)(2,1)S(1)}, bf16[32,768]{1,0:T(8,128)(2,1)S(1)}, u32[]{:S(2)}, u32[]{:S(2)}) %collective-permute-start.7) | collective-permute-done | bytes 49184 | tf_op jit(solution)/shard_map/ppermute | solution.py:17
  24.2 0.5 %shard_map.107 = (f32[16,2048]{1,0:T(8,128)S(1)}, bf16[16,2048]{1,0:T(8,128)(2,1)S(1)}) custom-call(bf16[32,768]{1,0:T(8,128)(2,1)S(1)} %shard_map.106.refs_0_, bf16[32,768]{1,0:T(8,128)(2,1)S(1)} %collective-permute-done.7.refs_1_, bf16[1024,1024]{1,0:T(8,128)(2,1)S(1)} %bitcast.22, bf16[1024,1024]{1,0:T(8,128)(2,1)S(1)} %copy-done.4), custom_call_target="tpu_custom_call" | custom-call | tf_op jit(solution)/shard_map/pallas_call | solution.py:315
  24.7 0.1 collective-permute-start.8
  24.8 1.2 %collective-permute-done.8 = bf16[16,2048]{1,0:T(8,128)(2,1)S(1)} collective-permute-done((bf16[16,2048]{1,0:T(8,128)(2,1)S(1)}, bf16[16,2048]{1,0:T(8,128)(2,1)S(1)}, u32[]{:S(2)}, u32[]{:S(2)}) %collective-permute-start.8) | collective-permute-done | bytes 65568 | tf_op jit(solution)/shard_map/ppermute | solution.py:17
  26.0 1.9 %collective-permute-start.9 = (bf16[8,2048]{1,0:T(8,128)(2,1)S(1)}, bf16[8,2048]{1,0:T(8,128)(2,1)S(1)}, u32[]{:S(2)}, u32[]{:S(2)}) collective-permute-start(bf16[8,2048]{1,0:T(8,128)(2,1)S(1)} %get-tuple-element.20), channel_id=1, source_target_pairs={{0,2},{1,3},{2,0},{3,1},{4,6},{5,7},{6,4},{7,5},{8,10},{9,11},{10,... | collective-permute-start | bytes 98312 | tf_op jit(solution)/shard_map/ppermute | solution.py:17
  27.9 2.1 %collective-permute-done.9 = bf16[8,2048]{1,0:T(8,128)(2,1)S(1)} collective-permute-done((bf16[8,2048]{1,0:T(8,128)(2,1)S(1)}, bf16[8,2048]{1,0:T(8,128)(2,1)S(1)}, u32[]{:S(2)}, u32[]{:S(2)}) %collective-permute-start.9) | collective-permute-done | bytes 32800 | tf_op jit(solution)/shard_map/ppermute | solution.py:17
  30.1 2.0 %collective-permute-start.10 = (bf16[2,2,4096]{2,1,0:T(2,128)(2,1)S(1)}, bf16[2,2,4096]{2,1,0:T(2,128)(2,1)S(1)}, u32[]{:S(2)}, u32[]{:S(2)}) collective-permute-start(bf16[2,2,4096]{2,1,0:T(2,128)(2,1)S(1)} %pad_maximum_fusion.4), channel_id=1, source_target_pairs={{0,4},{4,0},{8,12},{12,8},{1,5},{5,1},{9,13},{13,9},{2,6},{6,2},{1... | collective-permute-start | bytes 98312 | tf_op jit(solution)/shard_map/ppermute | solution.py:17
  32.1 2.0 %collective-permute-done.10 = bf16[2,2,4096]{2,1,0:T(2,128)(2,1)S(1)} collective-permute-done((bf16[2,2,4096]{2,1,0:T(2,128)(2,1)S(1)}, bf16[2,2,4096]{2,1,0:T(2,128)(2,1)S(1)}, u32[]{:S(2)}, u32[]{:S(2)}) %collective-permute-start.10) | collective-permute-done | bytes 32800 | tf_op jit(solution)/shard_map/ppermute | solution.py:17
  34.2 3.0 %collective-permute-start.11 = (bf16[2,2,4096]{2,1,0:T(2,128)(2,1)S(1)}, bf16[2,2,4096]{2,1,0:T(2,128)(2,1)S(1)}, u32[]{:S(2)}, u32[]{:S(2)}) collective-permute-start(bf16[2,2,4096]{2,1,0:T(2,128)(2,1)S(1)} %pad_maximum_fusion.6), channel_id=1, source_target_pairs={{0,8},{4,12},{8,0},{12,4},{1,9},{5,13},{9,1},{13,5},{2,10},{6,14},... | collective-permute-start | bytes 98312 | tf_op jit(solution)/shard_map/ppermute | solution.py:17
  37.2 1.8 %collective-permute-done.11.refs_2_ = bf16[2,2,4096]{2,1,0:T(2,128)(2,1)S(1)} collective-permute-done((bf16[2,2,4096]{2,1,0:T(2,128)(2,1)S(1)}, bf16[2,2,4096]{2,1,0:T(2,128)(2,1)S(1)}, u32[]{:S(2)}, u32[]{:S(2)}) %collective-permute-start.11) | collective-permute-done | bytes 32800 | tf_op jit(solution)/shard_map/ppermute | solution.py:17
  39.1 0.8 %shard_map.108 = bf16[8,4096]{1,0:T(8,128)(2,1)} custom-call(f32[8,8]{1,0:T(8,128)S(1)} %copy-done.8, bf16[2,2,4096]{2,1,0:T(2,128)(2,1)S(1)} %pad_maximum_fusion.5.refs_1_, bf16[2,2,4096]{2,1,0:T(2,128)(2,1)S(1)} %collective-permute-done.11.refs_2_), custom_call_target="tpu_custom_call" | custom-call | tf_op jit(solution)/shard_map/pallas_call | solution.py:335
  (33 shorter events, 0.6 us)
Async XLA Ops:
  0.0 14.3 %copy-start = (bf16[1,4096,256]{2,1,0:T(8,128)(2,1)S(1)}, bf16[1,4096,256]{2,1,0:T(8,128)(2,1)}, u32[]{:S(2)}) copy-start(bf16[1,4096,256]{2,1,0:T(8,128)(2,1)} %param.15) | copy-start | bytes 6291460
  2.1 5.1 %collective-permute-start = (bf16[2,2,4224]{2,1,0:T(2,128)(2,1)}, bf16[2,2,4224]{2,1,0:T(2,128)(2,1)S(1)}, u32[]{:S(2)}, u32[]{:S(2)}) collective-permute-start(bf16[2,2,4224]{2,1,0:T(2,128)(2,1)} %get-tuple-element.12), channel_id=1, source_target_pairs={{0,4},{4,0},{8,12},{12,8},{1,5},{5,1},{9,13},{13,9},{2,6},{6,2},{1... | collective-permute-start | bytes 101384 | tf_op jit(solution)/shard_map/ppermute | solution.py:17
  5.1 5.4 %collective-permute-start.1 = (bf16[96,1024]{1,0:T(8,128)(2,1)}, bf16[96,1024]{1,0:T(8,128)(2,1)S(1)}, u32[]{:S(2)}, u32[]{:S(2)}) collective-permute-start(bf16[96,1024]{1,0:T(8,128)(2,1)} %bitcast.23), channel_id=1, source_target_pairs={{0,1},{1,0},{2,3},{3,2},{4,5},{5,4},{6,7},{7,6},{8,9},{9,8},{10,11... | collective-permute-start | bytes 589832 | tf_op jit(solution)/shard_map/ppermute | solution.py:17
  5.1 5.4 %collective-permute-start.2 = (bf16[1024,1024]{1,0:T(8,128)(2,1)}, bf16[1024,1024]{1,0:T(8,128)(2,1)S(1)}, u32[]{:S(2)}, u32[]{:S(2)}) collective-permute-start(bf16[1024,1024]{1,0:T(8,128)(2,1)} %bitcast.21), channel_id=1, source_target_pairs={{0,1},{1,0},{2,3},{3,2},{4,5},{5,4},{6,7},{7,6},{8,9},{9,8},{10,11... | collective-permute-start | bytes 6291464 | tf_op jit(solution)/shard_map/ppermute | solution.py:17
  7.3 5.0 %collective-permute-start.3 = (bf16[2,2,4224]{2,1,0:T(2,128)(2,1)S(1)}, bf16[2,2,4224]{2,1,0:T(2,128)(2,1)S(1)}, u32[]{:S(2)}, u32[]{:S(2)}) collective-permute-start(bf16[2,2,4224]{2,1,0:T(2,128)(2,1)S(1)} %pad_maximum_fusion.3), channel_id=1, source_target_pairs={{0,8},{4,12},{8,0},{12,4},{1,9},{5,13},{9,1},{13,5},{2,10},{6,14},... | collective-permute-start | bytes 101384 | tf_op jit(solution)/shard_map/ppermute | solution.py:17
  10.5 1.3 %copy-start.3 = (bf16[1024,1024]{1,0:T(8,128)(2,1)}, bf16[1024,1024]{1,0:T(8,128)(2,1)S(1)}, u32[]{:S(2)}) copy-start(bf16[1024,1024]{1,0:T(8,128)(2,1)S(1)} %collective-permute-done.2.refs_1_.refs_3_) | copy-start | bytes 6291460
  12.4 4.4 %collective-permute-start.4 = (bf16[8,4224]{1,0:T(8,128)(2,1)S(1)}, bf16[8,4224]{1,0:T(8,128)(2,1)S(1)}, u32[]{:S(2)}, u32[]{:S(2)}) collective-permute-start(bf16[8,4224]{1,0:T(8,128)(2,1)S(1)} %reshape.25.x_ref), channel_id=1, source_target_pairs={{0,2},{1,3},{2,0},{3,1},{4,6},{5,7},{6,4},{7,5},{8,10},{9,11},{10,... | collective-permute-start | bytes 202760 | tf_op jit(solution)/shard_map/ppermute | solution.py:17
  14.3 1.6 %copy-start.1 = (bf16[1,4096,256]{2,1,0:T(8,128)(2,1)S(1)}, bf16[1,4096,256]{2,1,0:T(8,128)(2,1)}, u32[]{:S(2)}) copy-start(bf16[1,4096,256]{2,1,0:T(8,128)(2,1)} %param.16) | copy-start | bytes 6291460
  15.9 1.6 %copy-start.2 = (bf16[1,4096,256]{2,1,0:T(8,128)(2,1)S(1)}, bf16[1,4096,256]{2,1,0:T(8,128)(2,1)}, u32[]{:S(2)}) copy-start(bf16[1,4096,256]{2,1,0:T(8,128)(2,1)} %param.16) | copy-start | bytes 6291460
  15.9 1.8 %copy-start.5 = (bf16[1,6,16,4096]{3,2,1,0:T(8,128)(2,1)S(1)}, bf16[1,6,16,4096]{3,2,1,0:T(8,128)(2,1)}, u32[]{:S(2)}) copy-start(bf16[1,6,16,4096]{3,2,1,0:T(8,128)(2,1)} %param.18) | copy-start | bytes 2359300
  15.9 1.8 %copy-start.7 = (bf16[1,6,16,1024]{3,2,1,0:T(8,128)(2,1)S(1)}, bf16[1,6,16,1024]{3,2,1,0:T(8,128)(2,1)}, u32[]{:S(2)}) copy-start(bf16[1,6,16,1024]{3,2,1,0:T(8,128)(2,1)} %param.19) | copy-start | bytes 589828
  16.8 1.4 %collective-permute-start.5 = (bf16[16,4224]{1,0:T(8,128)(2,1)S(1)}, bf16[16,4224]{1,0:T(8,128)(2,1)S(1)}, u32[]{:S(2)}, u32[]{:S(2)}) collective-permute-start(bf16[16,4224]{1,0:T(8,128)(2,1)S(1)} %pad_maximum_fusion.x_ref), channel_id=1, source_target_pairs={{0,1},{1,0},{2,3},{3,2},{4,5},{5,4},{6,7},{7,6},{8,9},{9,8},{10,11... | collective-permute-start | bytes 405512 | tf_op jit(solution)/shard_map/ppermute | solution.py:17
  18.6 5.6 %copy-start.4 = (bf16[1024,1024]{1,0:T(8,128)(2,1)S(1)}, bf16[1024,1024]{1,0:T(8,128)(2,1)}, u32[]{:S(2)}) copy-start(bf16[1024,1024]{1,0:T(8,128)(2,1)} %copy-done.3) | copy-start | bytes 6291460
  18.6 5.6 %copy-start.6 = (bf16[1,1024,1024]{2,1,0:T(8,128)(2,1)S(1)}, bf16[1,1024,1024]{2,1,0:T(8,128)(2,1)}, u32[]{:S(2)}) copy-start(bf16[1,1024,1024]{2,1,0:T(8,128)(2,1)} %param.17) | copy-start | bytes 6291460
  18.6 1.2 %collective-permute-start.6 = (bf16[32,96]{1,0:T(8,128)(2,1)S(1)}, bf16[32,96]{1,0:T(8,128)(2,1)S(1)}, u32[]{:S(2)}, u32[]{:S(2)}) collective-permute-start(bf16[32,96]{1,0:T(8,128)(2,1)S(1)} %shard_map.104.refs_0_), channel_id=1, source_target_pairs={{0,1},{1,0},{2,3},{3,2},{4,5},{5,4},{6,7},{7,6},{8,9},{9,8},{10,11... | collective-permute-start | bytes 18440 | tf_op jit(solution)/shard_map/ppermute | solution.py:17
  20.0 19.1 %copy-start.8 = (f32[8,8]{1,0:T(8,128)S(1)}, f32[8,8]{1,0:T(8,128)}, u32[]{:S(2)}) copy-start(f32[8,8]{1,0:T(8,128)} %get-tuple-element.10.refs_0_) | copy-start | bytes 772
  20.0 4.2 %collective-permute-start.7 = (bf16[32,768]{1,0:T(8,128)(2,1)S(1)}, bf16[32,768]{1,0:T(8,128)(2,1)S(1)}, u32[]{:S(2)}, u32[]{:S(2)}) collective-permute-start(bf16[32,768]{1,0:T(8,128)(2,1)S(1)} %shard_map.106.refs_0_), channel_id=1, source_target_pairs={{0,2},{1,3},{2,0},{3,1},{4,6},{5,7},{6,4},{7,5},{8,10},{9,11},{10,... | collective-permute-start | bytes 147464 | tf_op jit(solution)/shard_map/ppermute | solution.py:17
  24.7 1.3 %collective-permute-start.8 = (bf16[16,2048]{1,0:T(8,128)(2,1)S(1)}, bf16[16,2048]{1,0:T(8,128)(2,1)S(1)}, u32[]{:S(2)}, u32[]{:S(2)}) collective-permute-start(bf16[16,2048]{1,0:T(8,128)(2,1)S(1)} %get-tuple-element.14), channel_id=1, source_target_pairs={{0,1},{1,0},{2,3},{3,2},{4,5},{5,4},{6,7},{7,6},{8,9},{9,8},{10,11... | collective-permute-start | bytes 196616 | tf_op jit(solution)/shard_map/ppermute | solution.py:17
  26.0 4.0 %collective-permute-start.9 = (bf16[8,2048]{1,0:T(8,128)(2,1)S(1)}, bf16[8,2048]{1,0:T(8,128)(2,1)S(1)}, u32[]{:S(2)}, u32[]{:S(2)}) collective-permute-start(bf16[8,2048]{1,0:T(8,128)(2,1)S(1)} %get-tuple-element.20), channel_id=1, source_target_pairs={{0,2},{1,3},{2,0},{3,1},{4,6},{5,7},{6,4},{7,5},{8,10},{9,11},{10,... | collective-permute-start | bytes 98312 | tf_op jit(solution)/shard_map/ppermute | solution.py:17
  30.1 4.0 %collective-permute-start.10 = (bf16[2,2,4096]{2,1,0:T(2,128)(2,1)S(1)}, bf16[2,2,4096]{2,1,0:T(2,128)(2,1)S(1)}, u32[]{:S(2)}, u32[]{:S(2)}) collective-permute-start(bf16[2,2,4096]{2,1,0:T(2,128)(2,1)S(1)} %pad_maximum_fusion.4), channel_id=1, source_target_pairs={{0,4},{4,0},{8,12},{12,8},{1,5},{5,1},{9,13},{13,9},{2,6},{6,2},{1... | collective-permute-start | bytes 98312 | tf_op jit(solution)/shard_map/ppermute | solution.py:17
  34.2 4.9 %collective-permute-start.11 = (bf16[2,2,4096]{2,1,0:T(2,128)(2,1)S(1)}, bf16[2,2,4096]{2,1,0:T(2,128)(2,1)S(1)}, u32[]{:S(2)}, u32[]{:S(2)}) collective-permute-start(bf16[2,2,4096]{2,1,0:T(2,128)(2,1)S(1)} %pad_maximum_fusion.6), channel_id=1, source_target_pairs={{0,8},{4,12},{8,0},{12,4},{1,9},{5,13},{9,1},{13,5},{2,10},{6,14},... | collective-permute-start | bytes 98312 | tf_op jit(solution)/shard_map/ppermute | solution.py:17

commit v5 on v4

--- a/solution.py
+++ b/solution.py
@@ -23,7 +23,7 @@
 
 def gather_order(size):
     order = [0]
-    for mask in reversed(bits_of(size)):
+    for mask in bits_of(size)[1:] + [1]:
         order = order + [q ^ mask for q in order]
     return order
 
@@ -88,10 +88,11 @@
         page.astype(BF), jnp.ones((tok_count, TAIL), BF), by_token, preferred_element_type=F32
     )
     for r in range(experts):
-        ref = send_ref if r % 2 else keep_ref
+        middle = experts // 2
+        ref = send_ref if r >= middle else keep_ref
         at = slice(r * cap, (r + 1) * cap)
-        ref[r // 2, :, :width] = rows[at].astype(BF)
-        ref[r // 2, :, width:] = tail[at].astype(BF)
+        ref[r % middle, :, :width] = rows[at].astype(BF)
+        ref[r % middle, :, width:] = tail[at].astype(BF)
 
 
 def rows_of(own_ref, came_ref, width):
@@ -221,15 +222,13 @@
 def build(mesh):
     n_exp, n_dp = mesh.shape["expert"], mesh.shape["dp"]
 
-    def stage(blocks, axis, size, mask, dim, early=()):
-        labels = sorted(blocks)
-        sent = [q for q in labels if q & mask]
+    n_all = n_exp * n_dp
+    both_axes = ("expert", "dp")
+
+    def stage(blocks, axis, size, mask, dim):
+        sent = [q for q in sorted(blocks) if q & mask]
         x = jnp.concatenate([blocks[q] for q in sent], axis=dim)
         came = jnp.split(swap(x, axis, size, mask), len(sent), axis=dim)
-        if early:
-            stay = [q for q in labels if not q & mask]
-            x = hold(jnp.concatenate([blocks[q] for q in stay], axis=dim), *early)
-            blocks = {**blocks, **dict(zip(stay, jnp.split(x, len(stay), axis=dim)))}
         return {**blocks, **dict(zip(sent, came))}
 
     def per_device(
@@ -266,7 +265,7 @@
 
         state = {}
         for i in range(middle):
-            state[2 * i], state[2 * i + 1] = kept[i : i + 1], sent[i : i + 1]
+            state[i], state[middle + i] = kept[i : i + 1], sent[i : i + 1]
         gate_w = gate_weight.reshape(width, hid)
         up_w = up_projection.reshape(width, hid)
         shrink_w = adapter_shrink.reshape(pages * rank, width)
@@ -274,19 +273,21 @@
         down_w = down_weight.reshape(-1, part)
         expand2 = swap(expand_w, "dp", n_dp, 1)
         down2 = swap(down_w, "dp", n_dp, 1)
-        plan = [(), (expand2, down2), (gate_w, up_w), (gate_w, up_w, shrink_w, expand_w)]
-        early = plan[:2]
-        for mask in bits_of(n_exp):
-            state = stage(state, "expert", n_exp, mask, 0, early.pop(0) if early else ())
-        own = jnp.concatenate([state[r] for r in range(n_exp)], axis=0)
-        own = own.reshape(block, width + TAIL)
-        masks = list(reversed(bits_of(n_dp)))
-        for mask in masks[:-1]:
-            other = swap(own, "dp", n_dp, mask)
-            own = jnp.concatenate([hold(own, *plan[2]), other], axis=0)
-        came = swap(own, "dp", n_dp, masks[-1])
-        if plan[3]:
-            own = hold(own, *plan[3])
+        for mask in reversed(bits_of(n_exp)[1:]):
+            state = stage(state, "expert", n_exp, mask, 0)
+        even = jnp.concatenate([state[r] for r in range(0, n_exp, 2)], axis=0)
+        odd = jnp.concatenate([state[r] for r in range(1, n_exp, 2)], axis=0)
+        beside = swap(even, "dp", n_dp, 2)
+        across = swap(odd, "expert", n_exp, 1)
+        corner = swap(odd, both_axes, n_all, n_dp | 2)
+        even = hold(hold(even, expand2, down2), gate_w, up_w)
+        own = jnp.concatenate([even, across, beside, corner], axis=0)
+        own = own.reshape(2 * block, width + TAIL)
+        masks = bits_of(n_dp)[1:] + [1]
+        for mask in masks[1:-1]:
+            own = jnp.concatenate([own, swap(own, "dp", n_dp, mask)], axis=0)
+        came = swap(own, "dp", n_dp, 1)
+        own = hold(own, gate_w, shrink_w, expand_w)
         low = call(
             lambda *refs: shrink_kernel(n_dp, rank, *refs), shape((rows, pages * rank), BF), 3
         )(own, came, shrink_w)
@@ -321,13 +322,29 @@
         back = swap(send, "dp", n_dp, 1)
         both = (keep + back.astype(F32)).astype(BF)
         order = gather_order(n_dp)[:half]
-        state = {q: both[i * block : (i + 1) * block] for i, q in enumerate(order)}
-        for mask in bits_of(n_dp)[1:]:
-            state = stage(state, "dp", n_dp, mask, 0)
-        home = jnp.concatenate([state[q] for q in sorted(state)], axis=1)
+        each = block // 2
+        state = {}
+        for i, q in enumerate(order):
+            for odd in range(2):
+                at = i * block + odd * each
+                state[q, odd] = both[at : at + each]
+        for odd, far, axis, size, mask in (
+            (0, 2, "dp", n_dp, 2),
+            (1, 0, "expert", n_exp, 1),
+            (1, 2, both_axes, n_all, n_dp | 2),
+        ):
+            sent = [q for q in order if (q & 2) == far]
+            came = swap(jnp.concatenate([state[q, odd] for q in sent], axis=0), axis, size, mask)
+            for q, x in zip(sent, jnp.split(came, len(sent), axis=0)):
+                state[q, odd] = x
+        home = {q: jnp.concatenate([state[q, 0], state[q, 1]], axis=0) for q in order}
+        for mask in masks[1:-1]:
+            home = stage(home, "dp", n_dp, mask, 0)
+        home = jnp.concatenate([home[q] for q in sorted(home)], axis=1)
         home = home.reshape(n_exp, cap, n_dp * part)
-        state = {r: home[r : r + 1] for r in range(n_exp)}
-        for mask in bits_of(n_exp)[:-1]:
+        labels = list(range(0, n_exp, 2)) + list(range(1, n_exp, 2))
+        state = {r: home[i : i + 1] for i, r in enumerate(labels)}
+        for mask in bits_of(n_exp)[1:-1]:
             state = stage(state, "expert", n_exp, mask, 0)
         kept = jnp.concatenate([state[r] for r in range(middle)], axis=0)
         sent = jnp.concatenate([state[r] for r in range(middle, n_exp)], axis=0)

time: 40.1 us -> 38.5 us (0.960)
  starting transfers between devices: 17.6 us -> 15.8 us
  waiting for transfers between devices: 12.3 us -> 13.8 us
  local copies, waits for them, and re-layouts: 4.62 us -> 3.29 us
    ppermute x12 -> x14, starting transfers between devices: 17.6 us -> 15.8 us  [swap(): return lax.ppermute(x, axis, [(i, i ^ mask) for i in range(size)])]
    ppermute x12 -> x14, waiting for transfers between devices: 12.3 us -> 13.8 us  [swap(): return lax.ppermute(x, axis, [(i, i ^ mask) for i in range(size)])]
    unnamed x18, local copies, waits for them, and re-layouts: 3.77 us -> 2.37 us
    slice x2 -> x3, local copies, waits for them, and re-layouts: 0.77 us -> 0.84 us  [the longest x1 0.76 us: per_device(): state[i], state[middle + i] = (kept[i:i + 1], sent[i:i + 1])]
  transfers between devices with their start and end apart: 12 -> 14, of which waited for: 10 -> 11; matrix products, arithmetic and copies ran while one was open for 2% -> 2% of each run, Pallas kernels for 2% -> 2%
where the time goes in v5:
time: 38.5 us; the launch traced here: 38.3 us
  starting transfers between devices  15.8 us (41%)
  waiting for transfers between devices  13.8 us (36%)
  Pallas kernels  4.74 us (12%)
  local copies, waits for them, and re-layouts  3.29 us (9%)
  other arithmetic  0.45 us (1%)
    ppermute x14, starting transfers between devices, swap(): return lax.ppermute(x, axis, [(i, i ^ mask) for i in range(size)])  15.8 us
    ppermute x14, waiting for transfers between devices, swap(): return lax.ppermute(x, axis, [(i, i ^ mask) for i in range(size)])  13.8 us
    unnamed x18, local copies, waits for them, and re-layouts  2.37 us
    pallas_call x1, Pallas kernels, per_device(): call(slot_kernel, (shape((middle, cap, width + TAIL), BF),) * 2 + (shape(...  2.06 us
    pallas_call x1, Pallas kernels, per_device(): call(lambda *refs: expert_kernel(n_dp, *refs), shape((rows, 2 * hid), F32...  0.84 us
    pallas_call x1, Pallas kernels, per_device(): call(lambda *refs: mix_kernel(n_dp, part, *refs), shape((tok_count, n_dp...  0.8 us
  transfers between devices with their start and end apart: 14, of which 11 were waited for; matrix products, arithmetic and copies ran while one was open for 2% of the time, Pallas kernels for 2%

profile of v5, /device:TPU:0, one launch (start us, length us, event | category | flops | bytes accessed | tf_op | source)
XLA Modules:
  0.0 38.3 jit_solution(6116337351809561463)
XLA Ops:
  0.0 2.1 %shard_map.100 = (bf16[2,2,4224]{2,1,0:T(2,128)(2,1)}, bf16[2,2,4224]{2,1,0:T(2,128)(2,1)}, f32[8,8]{1,0:T(8,128)}) custom-call(bf16[8,4096]{1,0:T(8,128)(2,1)} %tok_ref.1, s32[8,8]{1,0:T(8,128)} %routing_ref.1, s32[8,8]{1,0:T(8,128)} %gate_ref.1, s32[8]{0:T(128)} %tenant_ref.1, s32[4,24]{1,0:T(4,128)} %lookup_ref.1), custom_call_target="tpu_custom_call" | custom-call | tf_op jit(solution)/shard_map/pallas_call | solution.py:258
  2.1 4.0 %collective-permute-start = (bf16[2,2,4224]{2,1,0:T(2,128)(2,1)}, bf16[2,2,4224]{2,1,0:T(2,128)(2,1)S(1)}, u32[]{:S(2)}, u32[]{:S(2)}) collective-permute-start(bf16[2,2,4224]{2,1,0:T(2,128)(2,1)} %get-tuple-element.12), channel_id=1, source_target_pairs={{0,8},{4,12},{8,0},{12,4},{1,9},{5,13},{9,1},{13,5},{2,10},{6,14},... | collective-permute-start | bytes 101384 | tf_op jit(solution)/shard_map/ppermute | solution.py:17
  6.1 0.5 %collective-permute-start.2 = (bf16[1024,1024]{1,0:T(8,128)(2,1)}, bf16[1024,1024]{1,0:T(8,128)(2,1)S(1)}, u32[]{:S(2)}, u32[]{:S(2)}) collective-permute-start(bf16[1024,1024]{1,0:T(8,128)(2,1)} %bitcast.20), channel_id=1, source_target_pairs={{0,1},{1,0},{2,3},{3,2},{4,5},{5,4},{6,7},{7,6},{8,9},{9,8},{10,11... | collective-permute-start | bytes 6291464 | tf_op jit(solution)/shard_map/ppermute | solution.py:17
  6.6 0.8 %fusion.1 = (bf16[1,2,4224]{2,1,0:T(2,128)(2,1)S(1)}, bf16[1,2,4224]{2,1,0:T(2,128)(2,1)S(1)}) fusion(bf16[2,2,4224]{2,1,0:T(2,128)(2,1)} %get-tuple-element.11), kind=kLoop, calls=%fused_computation.12 | loop fusion | bytes 67584 | tf_op jit(solution)/shard_map/slice | solution.py:268
  7.4 1.2 %collective-permute-done = bf16[2,2,4224]{2,1,0:T(2,128)(2,1)S(1)} collective-permute-done((bf16[2,2,4224]{2,1,0:T(2,128)(2,1)}, bf16[2,2,4224]{2,1,0:T(2,128)(2,1)S(1)}, u32[]{:S(2)}, u32[]{:S(2)}) %collective-permute-start) | collective-permute-done | bytes 33824 | tf_op jit(solution)/shard_map/ppermute | solution.py:17
  8.7 2.5 %collective-permute-start.5 = (bf16[2,2,4224]{2,1,0:T(2,128)(2,1)S(1)}, bf16[2,2,4224]{2,1,0:T(2,128)(2,1)S(1)}, u32[]{:S(2)}, u32[]{:S(2)}) collective-permute-start(bf16[2,2,4224]{2,1,0:T(2,128)(2,1)S(1)} %pad_maximum_fusion.2), channel_id=1, source_target_pairs={{0,6},{1,7},{2,4},{3,5},{4,2},{5,3},{6,0},{7,1},{8,14},{9,15},{10,... | collective-permute-start | bytes 101384 | tf_op jit(solution)/shard_map/ppermute | solution.py:17
  11.2 0.7 %collective-permute-start.3 = (bf16[2,2,4224]{2,1,0:T(2,128)(2,1)S(1)}, bf16[2,2,4224]{2,1,0:T(2,128)(2,1)S(1)}, u32[]{:S(2)}, u32[]{:S(2)}) collective-permute-start(bf16[2,2,4224]{2,1,0:T(2,128)(2,1)S(1)} %pad_maximum_fusion.2), channel_id=1, source_target_pairs={{0,4},{4,0},{8,12},{12,8},{1,5},{5,1},{9,13},{13,9},{2,6},{6,2},{1... | collective-permute-start | bytes 101384 | tf_op jit(solution)/shard_map/ppermute | solution.py:17
  11.9 0.4 %collective-permute-start.4 = (bf16[2,2,4224]{2,1,0:T(2,128)(2,1)S(1)}, bf16[2,2,4224]{2,1,0:T(2,128)(2,1)S(1)}, u32[]{:S(2)}, u32[]{:S(2)}) collective-permute-start(bf16[2,2,4224]{2,1,0:T(2,128)(2,1)S(1)} %pad_maximum_fusion.1.x_ref), channel_id=1, source_target_pairs={{0,2},{1,3},{2,0},{3,1},{4,6},{5,7},{6,4},{7,5},{8,10},{9,11},{10,... | collective-permute-start | bytes 101384 | tf_op jit(solution)/shard_map/ppermute | solution.py:17
  12.4 2.3 %copy-done.1 = bf16[1,4096,256]{2,1,0:T(8,128)(2,1)S(1)} copy-done((bf16[1,4096,256]{2,1,0:T(8,128)(2,1)S(1)}, bf16[1,4096,256]{2,1,0:T(8,128)(2,1)}, u32[]{:S(2)}) %copy-start.1) | copy-done | bytes 2097176
  14.7 0.4 %collective-permute-done.3 = bf16[2,2,4224]{2,1,0:T(2,128)(2,1)S(1)} collective-permute-done((bf16[2,2,4224]{2,1,0:T(2,128)(2,1)S(1)}, bf16[2,2,4224]{2,1,0:T(2,128)(2,1)S(1)}, u32[]{:S(2)}, u32[]{:S(2)}) %collective-permute-start.3) | collective-permute-done | bytes 33824 | tf_op jit(solution)/shard_map/ppermute | solution.py:17
  15.1 0.8 %collective-permute-done.4 = bf16[2,2,4224]{2,1,0:T(2,128)(2,1)S(1)} collective-permute-done((bf16[2,2,4224]{2,1,0:T(2,128)(2,1)S(1)}, bf16[2,2,4224]{2,1,0:T(2,128)(2,1)S(1)}, u32[]{:S(2)}, u32[]{:S(2)}) %collective-permute-start.4) | collective-permute-done | bytes 33824 | tf_op jit(solution)/shard_map/ppermute | solution.py:17
  15.9 0.2 pad_maximum_fusion
  16.2 0.1 collective-permute-start.6
  16.3 1.3 %collective-permute-done.6.refs_1_ = bf16[16,4224]{1,0:T(8,128)(2,1)S(1)} collective-permute-done((bf16[16,4224]{1,0:T(8,128)(2,1)S(1)}, bf16[16,4224]{1,0:T(8,128)(2,1)S(1)}, u32[]{:S(2)}, u32[]{:S(2)}) %collective-permute-start.6) | collective-permute-done | bytes 135200 | tf_op jit(solution)/shard_map/ppermute | solution.py:17
  17.6 0.4 %shard_map.104.refs_0_ = bf16[32,96]{1,0:T(8,128)(2,1)S(1)} custom-call(bf16[16,4224]{1,0:T(8,128)(2,1)S(1)} %shard_map.103.refs_0_, bf16[16,4224]{1,0:T(8,128)(2,1)S(1)} %collective-permute-done.6.refs_1_, bf16[96,4096]{1,0:T(8,128)(2,1)S(1)} %bitcast.19), custom_call_target="tpu_custom_call" | custom-call | tf_op jit(solution)/shard_map/pallas_call | solution.py:291
  18.0 0.2 collective-permute-start.7
  18.2 0.8 %shard_map.105.refs_4_ = f32[32,512]{1,0:T(8,128)S(1)} custom-call(bf16[16,4224]{1,0:T(8,128)(2,1)S(1)} %shard_map.103.refs_0_, bf16[16,4224]{1,0:T(8,128)(2,1)S(1)} %collective-permute-done.6.refs_1_, bf16[4096,256]{1,0:T(8,128)(2,1)S(1)} %bitcast.15, bf16[4096,256]{1,0:T(8,128)(2,1)S(1)} %bitcast.17), custom_call_target="tpu_custom_call" | custom-call | flops 134217728 | bytes 4194304 | tf_op jit(solution)/shard_map/pallas_call | solution.py:295
  19.1 0.2 collective-permute-done.7.refs_1_
  19.3 0.2 shard_map.106.refs_0_
  19.4 0.8 %collective-permute-start.8 = (bf16[32,768]{1,0:T(8,128)(2,1)S(1)}, bf16[32,768]{1,0:T(8,128)(2,1)S(1)}, u32[]{:S(2)}, u32[]{:S(2)}) collective-permute-start(bf16[32,768]{1,0:T(8,128)(2,1)S(1)} %shard_map.106.refs_0_), channel_id=1, source_target_pairs={{0,2},{1,3},{2,0},{3,1},{4,6},{5,7},{6,4},{7,5},{8,10},{9,11},{10,... | collective-permute-start | bytes 147464 | tf_op jit(solution)/shard_map/ppermute | solution.py:17
  20.3 3.3 %collective-permute-done.8.refs_1_ = bf16[32,768]{1,0:T(8,128)(2,1)S(1)} collective-permute-done((bf16[32,768]{1,0:T(8,128)(2,1)S(1)}, bf16[32,768]{1,0:T(8,128)(2,1)S(1)}, u32[]{:S(2)}, u32[]{:S(2)}) %collective-permute-start.8) | collective-permute-done | bytes 49184 | tf_op jit(solution)/shard_map/ppermute | solution.py:17
  23.6 0.5 %shard_map.107 = (f32[16,2048]{1,0:T(8,128)S(1)}, bf16[16,2048]{1,0:T(8,128)(2,1)S(1)}) custom-call(bf16[32,768]{1,0:T(8,128)(2,1)S(1)} %shard_map.106.refs_0_, bf16[32,768]{1,0:T(8,128)(2,1)S(1)} %collective-permute-done.8.refs_1_, bf16[1024,1024]{1,0:T(8,128)(2,1)S(1)} %bitcast.21, bf16[1024,1024]{1,0:T(8,128)(2,1)S(1)} %copy-done.4), custom_call_target="tpu_custom_call" | custom-call | tf_op jit(solution)/shard_map/pallas_call | solution.py:316
  24.2 1.2 %collective-permute-done.9 = bf16[16,2048]{1,0:T(8,128)(2,1)S(1)} collective-permute-done((bf16[16,2048]{1,0:T(8,128)(2,1)S(1)}, bf16[16,2048]{1,0:T(8,128)(2,1)S(1)}, u32[]{:S(2)}, u32[]{:S(2)}) %collective-permute-start.9) | collective-permute-done | bytes 65568 | tf_op jit(solution)/shard_map/ppermute | solution.py:17
  25.5 1.6 %collective-permute-start.12 = (bf16[4,2048]{1,0:T(4,128)(2,1)S(1)}, bf16[4,2048]{1,0:T(4,128)(2,1)S(1)}, u32[]{:S(2)}, u32[]{:S(2)}) collective-permute-start(bf16[4,2048]{1,0:T(4,128)(2,1)S(1)} %get-tuple-element.20), channel_id=1, source_target_pairs={{0,6},{1,7},{2,4},{3,5},{4,2},{5,3},{6,0},{7,1},{8,14},{9,15},{10,... | collective-permute-start | bytes 49160 | tf_op jit(solution)/shard_map/ppermute | solution.py:17
  27.1 1.3 %collective-permute-start.11 = (bf16[4,2048]{1,0:T(4,128)(2,1)S(1)}, bf16[4,2048]{1,0:T(4,128)(2,1)S(1)}, u32[]{:S(2)}, u32[]{:S(2)}) collective-permute-start(bf16[4,2048]{1,0:T(4,128)(2,1)S(1)} %get-tuple-element.21), channel_id=1, source_target_pairs={{0,2},{1,3},{2,0},{3,1},{4,6},{5,7},{6,4},{7,5},{8,10},{9,11},{10,... | collective-permute-start | bytes 49160 | tf_op jit(solution)/shard_map/ppermute | solution.py:17
  28.3 0.7 %collective-permute-start.10 = (bf16[4,2048]{1,0:T(4,128)(2,1)S(1)}, bf16[4,2048]{1,0:T(4,128)(2,1)S(1)}, u32[]{:S(2)}, u32[]{:S(2)}) collective-permute-start(bf16[4,2048]{1,0:T(4,128)(2,1)S(1)} %get-tuple-element.22), channel_id=1, source_target_pairs={{0,4},{4,0},{8,12},{12,8},{1,5},{5,1},{9,13},{13,9},{2,6},{6,2},{1... | collective-permute-start | bytes 49160 | tf_op jit(solution)/shard_map/ppermute | solution.py:17
  29.0 1.1 %collective-permute-done.12 = bf16[4,2048]{1,0:T(4,128)(2,1)S(1)} collective-permute-done((bf16[4,2048]{1,0:T(4,128)(2,1)S(1)}, bf16[4,2048]{1,0:T(4,128)(2,1)S(1)}, u32[]{:S(2)}, u32[]{:S(2)}) %collective-permute-start.12) | collective-permute-done | bytes 16416 | tf_op jit(solution)/shard_map/ppermute | solution.py:17
  30.2 0.6 %collective-permute-done.11 = bf16[4,2048]{1,0:T(4,128)(2,1)S(1)} collective-permute-done((bf16[4,2048]{1,0:T(4,128)(2,1)S(1)}, bf16[4,2048]{1,0:T(4,128)(2,1)S(1)}, u32[]{:S(2)}, u32[]{:S(2)}) %collective-permute-start.11) | collective-permute-done | bytes 16416 | tf_op jit(solution)/shard_map/ppermute | solution.py:17
  30.8 1.3 %collective-permute-done.10 = bf16[4,2048]{1,0:T(4,128)(2,1)S(1)} collective-permute-done((bf16[4,2048]{1,0:T(4,128)(2,1)S(1)}, bf16[4,2048]{1,0:T(4,128)(2,1)S(1)}, u32[]{:S(2)}, u32[]{:S(2)}) %collective-permute-start.10) | collective-permute-done | bytes 16416 | tf_op jit(solution)/shard_map/ppermute | solution.py:17
  32.2 2.9 %collective-permute-start.13 = (bf16[2,2,4096]{2,1,0:T(2,128)(2,1)S(1)}, bf16[2,2,4096]{2,1,0:T(2,128)(2,1)S(1)}, u32[]{:S(2)}, u32[]{:S(2)}) collective-permute-start(bf16[2,2,4096]{2,1,0:T(2,128)(2,1)S(1)} %pad_maximum_fusion.4), channel_id=1, source_target_pairs={{0,8},{4,12},{8,0},{12,4},{1,9},{5,13},{9,1},{13,5},{2,10},{6,14},... | collective-permute-start | bytes 98312 | tf_op jit(solution)/shard_map/ppermute | solution.py:17
  35.2 2.3 %collective-permute-done.13.refs_2_ = bf16[2,2,4096]{2,1,0:T(2,128)(2,1)S(1)} collective-permute-done((bf16[2,2,4096]{2,1,0:T(2,128)(2,1)S(1)}, bf16[2,2,4096]{2,1,0:T(2,128)(2,1)S(1)}, u32[]{:S(2)}, u32[]{:S(2)}) %collective-permute-start.13) | collective-permute-done | bytes 32800 | tf_op jit(solution)/shard_map/ppermute | solution.py:17
  37.5 0.8 %shard_map.108 = bf16[8,4096]{1,0:T(8,128)(2,1)} custom-call(f32[8,8]{1,0:T(8,128)S(1)} %copy-done.8, bf16[2,2,4096]{2,1,0:T(2,128)(2,1)S(1)} %pad_maximum_fusion.3.refs_1_, bf16[2,2,4096]{2,1,0:T(2,128)(2,1)S(1)} %collective-permute-done.13.refs_2_), custom_call_target="tpu_custom_call" | custom-call | tf_op jit(solution)/shard_map/pallas_call | solution.py:352
  (35 shorter events, 0.6 us)
Async XLA Ops:
  0.0 12.4 %copy-start = (bf16[1,4096,256]{2,1,0:T(8,128)(2,1)S(1)}, bf16[1,4096,256]{2,1,0:T(8,128)(2,1)}, u32[]{:S(2)}) copy-start(bf16[1,4096,256]{2,1,0:T(8,128)(2,1)} %param.15) | copy-start | bytes 6291460
  2.1 6.5 %collective-permute-start = (bf16[2,2,4224]{2,1,0:T(2,128)(2,1)}, bf16[2,2,4224]{2,1,0:T(2,128)(2,1)S(1)}, u32[]{:S(2)}, u32[]{:S(2)}) collective-permute-start(bf16[2,2,4224]{2,1,0:T(2,128)(2,1)} %get-tuple-element.12), channel_id=1, source_target_pairs={{0,8},{4,12},{8,0},{12,4},{1,9},{5,13},{9,1},{13,5},{2,10},{6,14},... | collective-permute-start | bytes 101384 | tf_op jit(solution)/shard_map/ppermute | solution.py:17
  6.1 6.2 %collective-permute-start.1 = (bf16[96,1024]{1,0:T(8,128)(2,1)}, bf16[96,1024]{1,0:T(8,128)(2,1)S(1)}, u32[]{:S(2)}, u32[]{:S(2)}) collective-permute-start(bf16[96,1024]{1,0:T(8,128)(2,1)} %bitcast.22), channel_id=1, source_target_pairs={{0,1},{1,0},{2,3},{3,2},{4,5},{5,4},{6,7},{7,6},{8,9},{9,8},{10,11... | collective-permute-start | bytes 589832 | tf_op jit(solution)/shard_map/ppermute | solution.py:17
  6.1 6.2 %collective-permute-start.2 = (bf16[1024,1024]{1,0:T(8,128)(2,1)}, bf16[1024,1024]{1,0:T(8,128)(2,1)S(1)}, u32[]{:S(2)}, u32[]{:S(2)}) collective-permute-start(bf16[1024,1024]{1,0:T(8,128)(2,1)} %bitcast.20), channel_id=1, source_target_pairs={{0,1},{1,0},{2,3},{3,2},{4,5},{5,4},{6,7},{7,6},{8,9},{9,8},{10,11... | collective-permute-start | bytes 6291464 | tf_op jit(solution)/shard_map/ppermute | solution.py:17
  8.7 6.1 %collective-permute-start.5 = (bf16[2,2,4224]{2,1,0:T(2,128)(2,1)S(1)}, bf16[2,2,4224]{2,1,0:T(2,128)(2,1)S(1)}, u32[]{:S(2)}, u32[]{:S(2)}) collective-permute-start(bf16[2,2,4224]{2,1,0:T(2,128)(2,1)S(1)} %pad_maximum_fusion.2), channel_id=1, source_target_pairs={{0,6},{1,7},{2,4},{3,5},{4,2},{5,3},{6,0},{7,1},{8,14},{9,15},{10,... | collective-permute-start | bytes 101384 | tf_op jit(solution)/shard_map/ppermute | solution.py:17
  11.2 3.9 %collective-permute-start.3 = (bf16[2,2,4224]{2,1,0:T(2,128)(2,1)S(1)}, bf16[2,2,4224]{2,1,0:T(2,128)(2,1)S(1)}, u32[]{:S(2)}, u32[]{:S(2)}) collective-permute-start(bf16[2,2,4224]{2,1,0:T(2,128)(2,1)S(1)} %pad_maximum_fusion.2), channel_id=1, source_target_pairs={{0,4},{4,0},{8,12},{12,8},{1,5},{5,1},{9,13},{13,9},{2,6},{6,2},{1... | collective-permute-start | bytes 101384 | tf_op jit(solution)/shard_map/ppermute | solution.py:17
  11.9 4.0 %collective-permute-start.4 = (bf16[2,2,4224]{2,1,0:T(2,128)(2,1)S(1)}, bf16[2,2,4224]{2,1,0:T(2,128)(2,1)S(1)}, u32[]{:S(2)}, u32[]{:S(2)}) collective-permute-start(bf16[2,2,4224]{2,1,0:T(2,128)(2,1)S(1)} %pad_maximum_fusion.1.x_ref), channel_id=1, source_target_pairs={{0,2},{1,3},{2,0},{3,1},{4,6},{5,7},{6,4},{7,5},{8,10},{9,11},{10,... | collective-permute-start | bytes 101384 | tf_op jit(solution)/shard_map/ppermute | solution.py:17
  12.3 2.4 %copy-start.3 = (bf16[1024,1024]{1,0:T(8,128)(2,1)}, bf16[1024,1024]{1,0:T(8,128)(2,1)S(1)}, u32[]{:S(2)}) copy-start(bf16[1024,1024]{1,0:T(8,128)(2,1)S(1)} %collective-permute-done.2.refs_1_.refs_3_) | copy-start | bytes 6291460
  12.4 2.3 %copy-start.1 = (bf16[1,4096,256]{2,1,0:T(8,128)(2,1)S(1)}, bf16[1,4096,256]{2,1,0:T(8,128)(2,1)}, u32[]{:S(2)}) copy-start(bf16[1,4096,256]{2,1,0:T(8,128)(2,1)} %param.16) | copy-start | bytes 6291460
  14.7 1.6 %copy-start.5 = (bf16[1,6,16,4096]{3,2,1,0:T(8,128)(2,1)S(1)}, bf16[1,6,16,4096]{3,2,1,0:T(8,128)(2,1)}, u32[]{:S(2)}) copy-start(bf16[1,6,16,4096]{3,2,1,0:T(8,128)(2,1)} %param.18) | copy-start | bytes 2359300
  14.7 1.6 %copy-start.7 = (bf16[1,6,16,1024]{3,2,1,0:T(8,128)(2,1)S(1)}, bf16[1,6,16,1024]{3,2,1,0:T(8,128)(2,1)}, u32[]{:S(2)}) copy-start(bf16[1,6,16,1024]{3,2,1,0:T(8,128)(2,1)} %param.19) | copy-start | bytes 589828
  16.2 1.4 %collective-permute-start.6 = (bf16[16,4224]{1,0:T(8,128)(2,1)S(1)}, bf16[16,4224]{1,0:T(8,128)(2,1)S(1)}, u32[]{:S(2)}, u32[]{:S(2)}) collective-permute-start(bf16[16,4224]{1,0:T(8,128)(2,1)S(1)} %reshape.27.x_ref), channel_id=1, source_target_pairs={{0,1},{1,0},{2,3},{3,2},{4,5},{5,4},{6,7},{7,6},{8,9},{9,8},{10,11... | collective-permute-start | bytes 405512 | tf_op jit(solution)/shard_map/ppermute | solution.py:17
  16.3 2.0 %copy-start.2 = (bf16[1,4096,256]{2,1,0:T(8,128)(2,1)S(1)}, bf16[1,4096,256]{2,1,0:T(8,128)(2,1)}, u32[]{:S(2)}) copy-start(bf16[1,4096,256]{2,1,0:T(8,128)(2,1)} %param.16) | copy-start | bytes 6291460
  18.0 5.6 %copy-start.4 = (bf16[1024,1024]{1,0:T(8,128)(2,1)S(1)}, bf16[1024,1024]{1,0:T(8,128)(2,1)}, u32[]{:S(2)}) copy-start(bf16[1024,1024]{1,0:T(8,128)(2,1)} %copy-done.3) | copy-start | bytes 6291460
  18.0 5.6 %copy-start.6 = (bf16[1,1024,1024]{2,1,0:T(8,128)(2,1)S(1)}, bf16[1,1024,1024]{2,1,0:T(8,128)(2,1)}, u32[]{:S(2)}) copy-start(bf16[1,1024,1024]{2,1,0:T(8,128)(2,1)} %param.17) | copy-start | bytes 6291460
  18.0 1.2 %collective-permute-start.7 = (bf16[32,96]{1,0:T(8,128)(2,1)S(1)}, bf16[32,96]{1,0:T(8,128)(2,1)S(1)}, u32[]{:S(2)}, u32[]{:S(2)}) collective-permute-start(bf16[32,96]{1,0:T(8,128)(2,1)S(1)} %shard_map.104.refs_0_), channel_id=1, source_target_pairs={{0,1},{1,0},{2,3},{3,2},{4,5},{5,4},{6,7},{7,6},{8,9},{9,8},{10,11... | collective-permute-start | bytes 18440 | tf_op jit(solution)/shard_map/ppermute | solution.py:17
  19.4 18.0 %copy-start.8 = (f32[8,8]{1,0:T(8,128)S(1)}, f32[8,8]{1,0:T(8,128)}, u32[]{:S(2)}) copy-start(f32[8,8]{1,0:T(8,128)} %get-tuple-element.10.refs_0_) | copy-start | bytes 772
  19.4 4.2 %collective-permute-start.8 = (bf16[32,768]{1,0:T(8,128)(2,1)S(1)}, bf16[32,768]{1,0:T(8,128)(2,1)S(1)}, u32[]{:S(2)}, u32[]{:S(2)}) collective-permute-start(bf16[32,768]{1,0:T(8,128)(2,1)S(1)} %shard_map.106.refs_0_), channel_id=1, source_target_pairs={{0,2},{1,3},{2,0},{3,1},{4,6},{5,7},{6,4},{7,5},{8,10},{9,11},{10,... | collective-permute-start | bytes 147464 | tf_op jit(solution)/shard_map/ppermute | solution.py:17
  24.1 1.3 %collective-permute-start.9 = (bf16[16,2048]{1,0:T(8,128)(2,1)S(1)}, bf16[16,2048]{1,0:T(8,128)(2,1)S(1)}, u32[]{:S(2)}, u32[]{:S(2)}) collective-permute-start(bf16[16,2048]{1,0:T(8,128)(2,1)S(1)} %get-tuple-element.14), channel_id=1, source_target_pairs={{0,1},{1,0},{2,3},{3,2},{4,5},{5,4},{6,7},{7,6},{8,9},{9,8},{10,11... | collective-permute-start | bytes 196616 | tf_op jit(solution)/shard_map/ppermute | solution.py:17
  25.5 4.7 %collective-permute-start.12 = (bf16[4,2048]{1,0:T(4,128)(2,1)S(1)}, bf16[4,2048]{1,0:T(4,128)(2,1)S(1)}, u32[]{:S(2)}, u32[]{:S(2)}) collective-permute-start(bf16[4,2048]{1,0:T(4,128)(2,1)S(1)} %get-tuple-element.20), channel_id=1, source_target_pairs={{0,6},{1,7},{2,4},{3,5},{4,2},{5,3},{6,0},{7,1},{8,14},{9,15},{10,... | collective-permute-start | bytes 49160 | tf_op jit(solution)/shard_map/ppermute | solution.py:17
  27.1 3.7 %collective-permute-start.11 = (bf16[4,2048]{1,0:T(4,128)(2,1)S(1)}, bf16[4,2048]{1,0:T(4,128)(2,1)S(1)}, u32[]{:S(2)}, u32[]{:S(2)}) collective-permute-start(bf16[4,2048]{1,0:T(4,128)(2,1)S(1)} %get-tuple-element.21), channel_id=1, source_target_pairs={{0,2},{1,3},{2,0},{3,1},{4,6},{5,7},{6,4},{7,5},{8,10},{9,11},{10,... | collective-permute-start | bytes 49160 | tf_op jit(solution)/shard_map/ppermute | solution.py:17
  28.3 3.7 %collective-permute-start.10 = (bf16[4,2048]{1,0:T(4,128)(2,1)S(1)}, bf16[4,2048]{1,0:T(4,128)(2,1)S(1)}, u32[]{:S(2)}, u32[]{:S(2)}) collective-permute-start(bf16[4,2048]{1,0:T(4,128)(2,1)S(1)} %get-tuple-element.22), channel_id=1, source_target_pairs={{0,4},{4,0},{8,12},{12,8},{1,5},{5,1},{9,13},{13,9},{2,6},{6,2},{1... | collective-permute-start | bytes 49160 | tf_op jit(solution)/shard_map/ppermute | solution.py:17
  32.2 5.2 %collective-permute-start.13 = (bf16[2,2,4096]{2,1,0:T(2,128)(2,1)S(1)}, bf16[2,2,4096]{2,1,0:T(2,128)(2,1)S(1)}, u32[]{:S(2)}, u32[]{:S(2)}) collective-permute-start(bf16[2,2,4096]{2,1,0:T(2,128)(2,1)S(1)} %pad_maximum_fusion.4), channel_id=1, source_target_pairs={{0,8},{4,12},{8,0},{12,4},{1,9},{5,13},{9,1},{13,5},{2,10},{6,14},... | collective-permute-start | bytes 98312 | tf_op jit(solution)/shard_map/ppermute | solution.py:17

commit v6 on v5

--- a/solution.py
+++ b/solution.py
@@ -95,55 +95,45 @@
         ref[r % middle, :, width:] = tail[at].astype(BF)
 
 
-def rows_of(own_ref, came_ref, width):
-    return jnp.concatenate([own_ref[:, :width], came_ref[:, :width]], axis=0)
-
-
-def shrink_kernel(n_dp, rank, own_ref, came_ref, shrink_ref, out_ref):
-    wide, width = shrink_ref.shape
+def expert_kernel(
+    n_dp, rank, own_ref, came_ref, gate_ref, up_ref, shrink_ref, shrink2_ref, expand_ref, expand2_ref, out_ref
+):
+    width, hid = gate_ref.shape
+    wide = shrink_ref.shape[0]
+    half = n_dp // 2
     col = lax.axis_index("dp")
-    x = rows_of(own_ref, came_ref, width)
+    order = gather_order(n_dp)
+    x = jnp.concatenate([own_ref[:, :width], came_ref[:, :width]], axis=0)
     page = jnp.concatenate([own_ref[:, width:], came_ref[:, width:]], axis=0).astype(F32)[:, :1]
-    prod = lax.dot_general(
-        x, shrink_ref[...], (((1,), (1,)), ((), ())), preferred_element_type=F32
-    )
-    page_of = col * (wide // rank) + lax.broadcasted_iota(I32, prod.shape, 1) // rank
-    masked = jnp.where(page == page_of.astype(F32), prod, 0.0)
-    out_ref[...] = turned(masked, col, n_dp, gather_order(n_dp), list(range(n_dp))).astype(BF)
-
-
-def expert_kernel(n_dp, own_ref, came_ref, gate_ref, up_ref, out_ref):
-    width, hid = gate_ref.shape
-    col = lax.axis_index("dp")
-    x = rows_of(own_ref, came_ref, width)
+
+    def low(k, shrink):
+        prod = lax.dot_general(
+            x, shrink[...], (((1,), (1,)), ((), ())), preferred_element_type=F32
+        )
+        page_of = (col ^ k) * (wide // rank) + lax.broadcasted_iota(I32, prod.shape, 1) // rank
+        return jnp.where(page == page_of.astype(F32), prod, 0.0).astype(BF)
+
+    lows = (low(0, shrink_ref), low(1, shrink2_ref))
+
+    def update(unit):
+        at = pl.ds(pl.multiple_of(unit * hid, hid), hid)
+        y = jnp.dot(lows[0], expand_ref[:, at], preferred_element_type=F32)
+        return y + jnp.dot(lows[1], expand2_ref[:, at], preferred_element_type=F32)
+
+    def put(at, y):
+        out_ref[:, at : at + hid] = turned(y, col, n_dp, order, list(range(n_dp))).astype(BF)
+
     gate = jnp.dot(x, gate_ref[...], preferred_element_type=F32)
     up = jnp.dot(x, up_ref[...], preferred_element_type=F32)
     act = gate / (1.0 + jnp.exp(-gate))
-    for i, y in enumerate((act, up)):
-        y = turned(y, col, n_dp, gather_order(n_dp), list(range(n_dp)))
-        out_ref[:, i * hid : (i + 1) * hid] = y
-
-
-def grow_kernel(n_dp, low_ref, low2_ref, expand_ref, expand2_ref, act_ref, out_ref):
-    col = lax.axis_index("dp")
-    hid = act_ref.shape[1] // 2
-    half = n_dp // 2
-
-    def update(unit):
-        at = pl.ds(pl.multiple_of(unit * hid, hid), hid)
-        y = jnp.dot(low_ref[...], expand_ref[:, at], preferred_element_type=F32)
-        return y + jnp.dot(low2_ref[...], expand2_ref[:, at], preferred_element_type=F32)
-
-    act = act_ref[:, :hid]
-    out_ref[:, :hid] = act.astype(BF)
-    out_ref[:, hid : 2 * hid] = (act * (act_ref[:, hid:] + update(col))).astype(BF)
+    put(0, act)
+    put(hid, act * (up + update(col)))
     if half == 2:
-        out_ref[:, 2 * hid :] = update(col ^ 2).astype(BF)
+        put(2 * hid, update(col ^ 2))
     else:
         for i in range(half):
             unit = 2 * i + (col & 1)
-            y = jnp.where(unit == col, 0.0, update(unit))
-            out_ref[:, (2 + i) * hid : (3 + i) * hid] = y.astype(BF)
+            put((2 + i) * hid, jnp.where(unit == col, 0.0, update(unit)))
 
 
 def down_kernel(n_dp, hid, own_ref, came_ref, down_ref, down2_ref, keep_ref, send_ref):
@@ -177,19 +167,30 @@
         send_ref[:, (1 - k) * part : (2 - k) * part] = out[rows // 2 :].astype(BF)
 
 
-def mix_kernel(n_dp, part, mix_ref, kept_ref, came_ref, out_ref):
+def weighted(mix_ref, x_ref, first, lanes):
+    mix = mix_ref[...]
+    blocks, cap = x_ref.shape[:2]
+    total = jnp.zeros((mix.shape[0], lanes.stop - lanes.start), F32)
+    for r in range(blocks):
+        x = x_ref[r, :, lanes].astype(F32)
+        for c in range(cap):
+            at = first + r * cap + c
+            total += mix[:, at : at + 1] * x[c : c + 1]
+    return total
+
+
+def half_mix_kernel(part, mix_ref, kept_ref, out_ref):
+    for at in range(0, out_ref.shape[1], part):
+        lanes = slice(at, at + part)
+        out_ref[:, lanes] = weighted(mix_ref, kept_ref, 0, lanes)
+
+
+def mix_kernel(n_dp, part, mix_ref, half_ref, came_ref, out_ref):
     col = lax.axis_index("dp")
-    mix = mix_ref[...]
-    blocks, cap = kept_ref.shape[:2]
+    first = came_ref.shape[0] * came_ref.shape[1]
     for p in range(n_dp):
         lanes = slice(p * part, (p + 1) * part)
-        total = jnp.zeros((mix.shape[0], part), F32)
-        for i, ref in enumerate((kept_ref, came_ref)):
-            for r in range(blocks):
-                x = ref[r, :, lanes].astype(F32)
-                for c in range(cap):
-                    at = (i * blocks + r) * cap + c
-                    total += mix[:, at : at + 1] * x[c : c + 1]
+        total = half_ref[:, lanes] + weighted(mix_ref, came_ref, first, lanes)
         out_ref[:, pl.ds(pl.multiple_of((p ^ col) * part, part), part)] = total.astype(BF)
 
 
@@ -280,31 +281,22 @@
         beside = swap(even, "dp", n_dp, 2)
         across = swap(odd, "expert", n_exp, 1)
         corner = swap(odd, both_axes, n_all, n_dp | 2)
-        even = hold(hold(even, expand2, down2), gate_w, up_w)
+        shrink2 = swap(shrink_w, "dp", n_dp, 1)
+        even = hold(hold(even, expand2, down2, shrink2), gate_w, up_w)
         own = jnp.concatenate([even, across, beside, corner], axis=0)
         own = own.reshape(2 * block, width + TAIL)
         masks = bits_of(n_dp)[1:] + [1]
         for mask in masks[1:-1]:
             own = jnp.concatenate([own, swap(own, "dp", n_dp, mask)], axis=0)
         came = swap(own, "dp", n_dp, 1)
-        own = hold(own, gate_w, shrink_w, expand_w)
-        low = call(
-            lambda *refs: shrink_kernel(n_dp, rank, *refs), shape((rows, pages * rank), BF), 3
-        )(own, came, shrink_w)
-        low2 = swap(low, "dp", n_dp, 1)
-        acts = call(
-            lambda *refs: expert_kernel(n_dp, *refs),
-            shape((rows, 2 * hid), F32),
-            4,
-            cost_estimate=pl.CostEstimate(
-                flops=4 * rows * width * hid, bytes_accessed=4 * width * hid, transcendentals=0
-            ),
-        )(own, came, gate_w, up_w)
+        own = hold(own, gate_w, shrink_w)
         split = 2 * hid
         parts = 1 if half == 2 else half
         packed = call(
-            lambda *refs: grow_kernel(n_dp, *refs), shape((rows, split + parts * hid), BF), 5
-        )(low, low2, expand_w, expand2, acts)
+            lambda *refs: expert_kernel(n_dp, rank, *refs),
+            shape((rows, split + parts * hid), BF),
+            8,
+        )(own, came, gate_w, up_w, shrink_w, shrink2, expand_w, expand2)
 
         for mask in masks[:-2]:
             other = swap(packed, "dp", n_dp, mask)
@@ -349,11 +341,21 @@
         kept = jnp.concatenate([state[r] for r in range(middle)], axis=0)
         sent = jnp.concatenate([state[r] for r in range(middle, n_exp)], axis=0)
         came = swap(sent, "expert", n_exp, middle)
+        mixed = call(
+            lambda *refs: half_mix_kernel(part, *refs),
+            shape((tok_count, n_dp * part), F32),
+            2,
+            cost_estimate=pl.CostEstimate(
+                flops=2 * tok_count * middle * cap * n_dp * part,
+                bytes_accessed=4 * tok_count * n_dp * part,
+                transcendentals=0,
+            ),
+        )(mix, kept)
         return call(
             lambda *refs: mix_kernel(n_dp, part, *refs),
             shape((tok_count, n_dp * part), BF),
             3,
-        )(mix, kept, came)
+        )(mix, mixed, came)
 
     return per_device
 

time: 38.5 us -> 38.4 us (level)
  waiting for transfers between devices: 13.8 us -> 13.1 us
  local copies, waits for them, and re-layouts: 3.29 us -> 3.88 us
    ppermute x14, waiting for transfers between devices: 13.8 us -> 13.1 us  [swap(): return lax.ppermute(x, axis, [(i, i ^ mask) for i in range(size)])]
    unnamed x18 -> x22, local copies, waits for them, and re-layouts: 2.37 us -> 2.97 us
    pallas_call x3 -> x2, Pallas kernels: 1.38 us -> 1.49 us  [the longest x1 1.39 us: per_device(): call(lambda *refs: expert_kernel(n_dp, rank, *refs), shape((rows, split +...]
  transfers between devices with their start and end apart: 14 -> 14, of which waited for: 11 -> 10; matrix products, arithmetic and copies ran while one was open for 2% -> 2% of each run, Pallas kernels for 2% -> 0%
where the time goes in v6:
time: 38.4 us; the launch traced here: 38.2 us
  starting transfers between devices  15.7 us (41%)
  waiting for transfers between devices  13.1 us (34%)
  Pallas kernels  4.79 us (12%)
  local copies, waits for them, and re-layouts  3.88 us (10%)
  other arithmetic  0.45 us (1%)
    ppermute x14, starting transfers between devices, swap(): return lax.ppermute(x, axis, [(i, i ^ mask) for i in range(size)])  15.7 us
    ppermute x14, waiting for transfers between devices, swap(): return lax.ppermute(x, axis, [(i, i ^ mask) for i in range(size)])  13.1 us
    unnamed x22, local copies, waits for them, and re-layouts  2.97 us
    pallas_call x1, Pallas kernels, per_device(): call(slot_kernel, (shape((middle, cap, width + TAIL), BF),) * 2 + (shape(...  2.06 us
    pallas_call x1, Pallas kernels, per_device(): call(lambda *refs: expert_kernel(n_dp, rank, *refs), shape((rows, split +...  1.39 us
  transfers between devices with their start and end apart: 14, of which 10 were waited for; matrix products, arithmetic and copies ran while one was open for 2% of the time, Pallas kernels for 0%

profile of v6, /device:TPU:0, one launch (start us, length us, event | category | flops | bytes accessed | tf_op | source)
XLA Modules:
  0.0 38.2 jit_solution(15238321111108542347)
XLA Ops:
  0.0 2.1 %shard_map.100 = (bf16[2,2,4224]{2,1,0:T(2,128)(2,1)}, bf16[2,2,4224]{2,1,0:T(2,128)(2,1)}, f32[8,8]{1,0:T(8,128)}) custom-call(bf16[8,4096]{1,0:T(8,128)(2,1)} %tok_ref.1, s32[8,8]{1,0:T(8,128)} %routing_ref.1, s32[8,8]{1,0:T(8,128)} %gate_ref.1, s32[8]{0:T(128)} %tenant_ref.1, s32[4,24]{1,0:T(4,128)} %lookup_ref.1), custom_call_target="tpu_custom_call" | custom-call | tf_op jit(solution)/shard_map/pallas_call | solution.py:259
  2.1 4.0 %collective-permute-start = (bf16[2,2,4224]{2,1,0:T(2,128)(2,1)}, bf16[2,2,4224]{2,1,0:T(2,128)(2,1)S(1)}, u32[]{:S(2)}, u32[]{:S(2)}) collective-permute-start(bf16[2,2,4224]{2,1,0:T(2,128)(2,1)} %get-tuple-element.12), channel_id=1, source_target_pairs={{0,8},{4,12},{8,0},{12,4},{1,9},{5,13},{9,1},{13,5},{2,10},{6,14},... | collective-permute-start | bytes 101384 | tf_op jit(solution)/shard_map/ppermute | solution.py:17
  6.1 0.5 %collective-permute-start.3 = (bf16[96,4096]{1,0:T(8,128)(2,1)}, bf16[96,4096]{1,0:T(8,128)(2,1)S(1)}, u32[]{:S(2)}, u32[]{:S(2)}) collective-permute-start(bf16[96,4096]{1,0:T(8,128)(2,1)} %bitcast.18), channel_id=1, source_target_pairs={{0,1},{1,0},{2,3},{3,2},{4,5},{5,4},{6,7},{7,6},{8,9},{9,8},{10,11... | collective-permute-start | bytes 2359304 | tf_op jit(solution)/shard_map/ppermute | solution.py:17
  6.6 0.8 %fusion.1 = (bf16[1,2,4224]{2,1,0:T(2,128)(2,1)S(1)}, bf16[1,2,4224]{2,1,0:T(2,128)(2,1)S(1)}) fusion(bf16[2,2,4224]{2,1,0:T(2,128)(2,1)} %get-tuple-element.11), kind=kLoop, calls=%fused_computation.12 | loop fusion | bytes 67584 | tf_op jit(solution)/shard_map/slice | solution.py:269
  7.4 1.2 %collective-permute-done = bf16[2,2,4224]{2,1,0:T(2,128)(2,1)S(1)} collective-permute-done((bf16[2,2,4224]{2,1,0:T(2,128)(2,1)}, bf16[2,2,4224]{2,1,0:T(2,128)(2,1)S(1)}, u32[]{:S(2)}, u32[]{:S(2)}) %collective-permute-start) | collective-permute-done | bytes 33824 | tf_op jit(solution)/shard_map/ppermute | solution.py:17
  8.7 2.5 %collective-permute-start.6 = (bf16[2,2,4224]{2,1,0:T(2,128)(2,1)S(1)}, bf16[2,2,4224]{2,1,0:T(2,128)(2,1)S(1)}, u32[]{:S(2)}, u32[]{:S(2)}) collective-permute-start(bf16[2,2,4224]{2,1,0:T(2,128)(2,1)S(1)} %pad_maximum_fusion.2), channel_id=1, source_target_pairs={{0,6},{1,7},{2,4},{3,5},{4,2},{5,3},{6,0},{7,1},{8,14},{9,15},{10,... | collective-permute-start | bytes 101384 | tf_op jit(solution)/shard_map/ppermute | solution.py:17
  11.2 0.7 %collective-permute-start.4 = (bf16[2,2,4224]{2,1,0:T(2,128)(2,1)S(1)}, bf16[2,2,4224]{2,1,0:T(2,128)(2,1)S(1)}, u32[]{:S(2)}, u32[]{:S(2)}) collective-permute-start(bf16[2,2,4224]{2,1,0:T(2,128)(2,1)S(1)} %pad_maximum_fusion.2), channel_id=1, source_target_pairs={{0,4},{4,0},{8,12},{12,8},{1,5},{5,1},{9,13},{13,9},{2,6},{6,2},{1... | collective-permute-start | bytes 101384 | tf_op jit(solution)/shard_map/ppermute | solution.py:17
  11.9 0.4 %collective-permute-start.5 = (bf16[2,2,4224]{2,1,0:T(2,128)(2,1)S(1)}, bf16[2,2,4224]{2,1,0:T(2,128)(2,1)S(1)}, u32[]{:S(2)}, u32[]{:S(2)}) collective-permute-start(bf16[2,2,4224]{2,1,0:T(2,128)(2,1)S(1)} %pad_maximum_fusion.1.x_ref), channel_id=1, source_target_pairs={{0,2},{1,3},{2,0},{3,1},{4,6},{5,7},{6,4},{7,5},{8,10},{9,11},{10,... | collective-permute-start | bytes 101384 | tf_op jit(solution)/shard_map/ppermute | solution.py:17
  12.4 2.6 %copy-done.1 = bf16[1,4096,256]{2,1,0:T(8,128)(2,1)S(1)} copy-done((bf16[1,4096,256]{2,1,0:T(8,128)(2,1)S(1)}, bf16[1,4096,256]{2,1,0:T(8,128)(2,1)}, u32[]{:S(2)}) %copy-start.1) | copy-done | bytes 2097176
  15.0 0.1 collective-permute-done.4
  15.1 0.8 %collective-permute-done.5 = bf16[2,2,4224]{2,1,0:T(2,128)(2,1)S(1)} collective-permute-done((bf16[2,2,4224]{2,1,0:T(2,128)(2,1)S(1)}, bf16[2,2,4224]{2,1,0:T(2,128)(2,1)S(1)}, u32[]{:S(2)}, u32[]{:S(2)}) %collective-permute-start.5) | collective-permute-done | bytes 33824 | tf_op jit(solution)/shard_map/ppermute | solution.py:17
  15.9 0.2 pad_maximum_fusion
  16.2 0.1 collective-permute-start.7
  16.4 1.3 %collective-permute-done.7.refs_1_ = bf16[16,4224]{1,0:T(8,128)(2,1)S(1)} collective-permute-done((bf16[16,4224]{1,0:T(8,128)(2,1)S(1)}, bf16[16,4224]{1,0:T(8,128)(2,1)S(1)}, u32[]{:S(2)}, u32[]{:S(2)}) %collective-permute-start.7) | collective-permute-done | bytes 135200 | tf_op jit(solution)/shard_map/ppermute | solution.py:17
  17.6 0.1 copy-done.2
  17.8 0.2 copy-done.7
  18.0 1.4 %shard_map.104.refs_0_ = bf16[32,768]{1,0:T(8,128)(2,1)S(1)} custom-call(bf16[16,4224]{1,0:T(8,128)(2,1)S(1)} %shard_map.103.refs_0_, bf16[16,4224]{1,0:T(8,128)(2,1)S(1)} %collective-permute-done.7.refs_1_, bf16[4096,256]{1,0:T(8,128)(2,1)S(1)} %bitcast.15, bf16[4096,256]{1,0:T(8,128)(2,1)S(1)} %bitcast.17, bf16[96,4096]{1,0:T(8,128)(2,1)S(1)} %bitcast.20, ...), custom_call_target="tpu_custom_call" | custom-call | tf_op jit(solution)/shard_map/pallas_call | solution.py:295
  19.4 1.0 %collective-permute-start.8 = (bf16[32,768]{1,0:T(8,128)(2,1)S(1)}, bf16[32,768]{1,0:T(8,128)(2,1)S(1)}, u32[]{:S(2)}, u32[]{:S(2)}) collective-permute-start(bf16[32,768]{1,0:T(8,128)(2,1)S(1)} %shard_map.104.refs_0_), channel_id=1, source_target_pairs={{0,2},{1,3},{2,0},{3,1},{4,6},{5,7},{6,4},{7,5},{8,10},{9,11},{10,... | collective-permute-start | bytes 147464 | tf_op jit(solution)/shard_map/ppermute | solution.py:17
  20.3 3.2 %collective-permute-done.8.refs_1_ = bf16[32,768]{1,0:T(8,128)(2,1)S(1)} collective-permute-done((bf16[32,768]{1,0:T(8,128)(2,1)S(1)}, bf16[32,768]{1,0:T(8,128)(2,1)S(1)}, u32[]{:S(2)}, u32[]{:S(2)}) %collective-permute-start.8) | collective-permute-done | bytes 49184 | tf_op jit(solution)/shard_map/ppermute | solution.py:17
  23.5 0.5 %shard_map.105 = (f32[16,2048]{1,0:T(8,128)S(1)}, bf16[16,2048]{1,0:T(8,128)(2,1)S(1)}) custom-call(bf16[32,768]{1,0:T(8,128)(2,1)S(1)} %shard_map.104.refs_0_, bf16[32,768]{1,0:T(8,128)(2,1)S(1)} %collective-permute-done.8.refs_1_, bf16[1024,1024]{1,0:T(8,128)(2,1)S(1)} %bitcast.22, bf16[1024,1024]{1,0:T(8,128)(2,1)S(1)} %copy-done.4), custom_call_target="tpu_custom_call" | custom-call | tf_op jit(solution)/shard_map/pallas_call | solution.py:308
  24.0 0.1 collective-permute-start.9
  24.1 1.2 %collective-permute-done.9 = bf16[16,2048]{1,0:T(8,128)(2,1)S(1)} collective-permute-done((bf16[16,2048]{1,0:T(8,128)(2,1)S(1)}, bf16[16,2048]{1,0:T(8,128)(2,1)S(1)}, u32[]{:S(2)}, u32[]{:S(2)}) %collective-permute-start.9) | collective-permute-done | bytes 65568 | tf_op jit(solution)/shard_map/ppermute | solution.py:17
  25.4 1.7 %collective-permute-start.12 = (bf16[4,2048]{1,0:T(4,128)(2,1)S(1)}, bf16[4,2048]{1,0:T(4,128)(2,1)S(1)}, u32[]{:S(2)}, u32[]{:S(2)}) collective-permute-start(bf16[4,2048]{1,0:T(4,128)(2,1)S(1)} %get-tuple-element.20), channel_id=1, source_target_pairs={{0,6},{1,7},{2,4},{3,5},{4,2},{5,3},{6,0},{7,1},{8,14},{9,15},{10,... | collective-permute-start | bytes 49160 | tf_op jit(solution)/shard_map/ppermute | solution.py:17
  27.1 1.2 %collective-permute-start.11 = (bf16[4,2048]{1,0:T(4,128)(2,1)S(1)}, bf16[4,2048]{1,0:T(4,128)(2,1)S(1)}, u32[]{:S(2)}, u32[]{:S(2)}) collective-permute-start(bf16[4,2048]{1,0:T(4,128)(2,1)S(1)} %get-tuple-element.21), channel_id=1, source_target_pairs={{0,2},{1,3},{2,0},{3,1},{4,6},{5,7},{6,4},{7,5},{8,10},{9,11},{10,... | collective-permute-start | bytes 49160 | tf_op jit(solution)/shard_map/ppermute | solution.py:17
  28.3 0.6 %collective-permute-start.10 = (bf16[4,2048]{1,0:T(4,128)(2,1)S(1)}, bf16[4,2048]{1,0:T(4,128)(2,1)S(1)}, u32[]{:S(2)}, u32[]{:S(2)}) collective-permute-start(bf16[4,2048]{1,0:T(4,128)(2,1)S(1)} %get-tuple-element.22), channel_id=1, source_target_pairs={{0,4},{4,0},{8,12},{12,8},{1,5},{5,1},{9,13},{13,9},{2,6},{6,2},{1... | collective-permute-start | bytes 49160 | tf_op jit(solution)/shard_map/ppermute | solution.py:17
  29.0 1.1 %collective-permute-done.12 = bf16[4,2048]{1,0:T(4,128)(2,1)S(1)} collective-permute-done((bf16[4,2048]{1,0:T(4,128)(2,1)S(1)}, bf16[4,2048]{1,0:T(4,128)(2,1)S(1)}, u32[]{:S(2)}, u32[]{:S(2)}) %collective-permute-start.12) | collective-permute-done | bytes 16416 | tf_op jit(solution)/shard_map/ppermute | solution.py:17
  30.1 0.8 %collective-permute-done.11 = bf16[4,2048]{1,0:T(4,128)(2,1)S(1)} collective-permute-done((bf16[4,2048]{1,0:T(4,128)(2,1)S(1)}, bf16[4,2048]{1,0:T(4,128)(2,1)S(1)}, u32[]{:S(2)}, u32[]{:S(2)}) %collective-permute-start.11) | collective-permute-done | bytes 16416 | tf_op jit(solution)/shard_map/ppermute | solution.py:17
  30.9 1.2 %collective-permute-done.10 = bf16[4,2048]{1,0:T(4,128)(2,1)S(1)} collective-permute-done((bf16[4,2048]{1,0:T(4,128)(2,1)S(1)}, bf16[4,2048]{1,0:T(4,128)(2,1)S(1)}, u32[]{:S(2)}, u32[]{:S(2)}) %collective-permute-start.10) | collective-permute-done | bytes 16416 | tf_op jit(solution)/shard_map/ppermute | solution.py:17
  32.2 2.9 %collective-permute-start.13 = (bf16[2,2,4096]{2,1,0:T(2,128)(2,1)S(1)}, bf16[2,2,4096]{2,1,0:T(2,128)(2,1)S(1)}, u32[]{:S(2)}, u32[]{:S(2)}) collective-permute-start(bf16[2,2,4096]{2,1,0:T(2,128)(2,1)S(1)} %pad_maximum_fusion.4), channel_id=1, source_target_pairs={{0,8},{4,12},{8,0},{12,4},{1,9},{5,13},{9,1},{13,5},{2,10},{6,14},... | collective-permute-start | bytes 98312 | tf_op jit(solution)/shard_map/ppermute | solution.py:17
  35.2 0.1 shard_map.106.refs_1_
  35.3 2.2 %collective-permute-done.13.refs_2_ = bf16[2,2,4096]{2,1,0:T(2,128)(2,1)S(1)} collective-permute-done((bf16[2,2,4096]{2,1,0:T(2,128)(2,1)S(1)}, bf16[2,2,4096]{2,1,0:T(2,128)(2,1)S(1)}, u32[]{:S(2)}, u32[]{:S(2)}) %collective-permute-start.13) | collective-permute-done | bytes 32800 | tf_op jit(solution)/shard_map/ppermute | solution.py:17
  37.4 0.7 %shard_map.107 = bf16[8,4096]{1,0:T(8,128)(2,1)} custom-call(f32[8,8]{1,0:T(8,128)S(1)} %copy-done.10, f32[8,4096]{1,0:T(8,128)S(1)} %shard_map.106.refs_1_, bf16[2,2,4096]{2,1,0:T(2,128)(2,1)S(1)} %collective-permute-done.13.refs_2_), custom_call_target="tpu_custom_call" | custom-call | tf_op jit(solution)/shard_map/pallas_call | solution.py:354
  (38 shorter events, 0.5 us)
Async XLA Ops:
  0.0 12.4 %copy-start = (bf16[1,4096,256]{2,1,0:T(8,128)(2,1)S(1)}, bf16[1,4096,256]{2,1,0:T(8,128)(2,1)}, u32[]{:S(2)}) copy-start(bf16[1,4096,256]{2,1,0:T(8,128)(2,1)} %param.15) | copy-start | bytes 6291460
  2.1 6.5 %collective-permute-start = (bf16[2,2,4224]{2,1,0:T(2,128)(2,1)}, bf16[2,2,4224]{2,1,0:T(2,128)(2,1)S(1)}, u32[]{:S(2)}, u32[]{:S(2)}) collective-permute-start(bf16[2,2,4224]{2,1,0:T(2,128)(2,1)} %get-tuple-element.12), channel_id=1, source_target_pairs={{0,8},{4,12},{8,0},{12,4},{1,9},{5,13},{9,1},{13,5},{2,10},{6,14},... | collective-permute-start | bytes 101384 | tf_op jit(solution)/shard_map/ppermute | solution.py:17
  6.1 5.8 %collective-permute-start.1 = (bf16[96,1024]{1,0:T(8,128)(2,1)}, bf16[96,1024]{1,0:T(8,128)(2,1)S(1)}, u32[]{:S(2)}, u32[]{:S(2)}) collective-permute-start(bf16[96,1024]{1,0:T(8,128)(2,1)} %bitcast.23), channel_id=1, source_target_pairs={{0,1},{1,0},{2,3},{3,2},{4,5},{5,4},{6,7},{7,6},{8,9},{9,8},{10,11... | collective-permute-start | bytes 589832 | tf_op jit(solution)/shard_map/ppermute | solution.py:17
  6.1 6.2 %collective-permute-start.3 = (bf16[96,4096]{1,0:T(8,128)(2,1)}, bf16[96,4096]{1,0:T(8,128)(2,1)S(1)}, u32[]{:S(2)}, u32[]{:S(2)}) collective-permute-start(bf16[96,4096]{1,0:T(8,128)(2,1)} %bitcast.18), channel_id=1, source_target_pairs={{0,1},{1,0},{2,3},{3,2},{4,5},{5,4},{6,7},{7,6},{8,9},{9,8},{10,11... | collective-permute-start | bytes 2359304 | tf_op jit(solution)/shard_map/ppermute | solution.py:17
  6.6 5.7 %collective-permute-start.2 = (bf16[1024,1024]{1,0:T(8,128)(2,1)}, bf16[1024,1024]{1,0:T(8,128)(2,1)S(1)}, u32[]{:S(2)}, u32[]{:S(2)}) collective-permute-start(bf16[1024,1024]{1,0:T(8,128)(2,1)} %bitcast.21), channel_id=1, source_target_pairs={{0,1},{1,0},{2,3},{3,2},{4,5},{5,4},{6,7},{7,6},{8,9},{9,8},{10,11... | collective-permute-start | bytes 6291464 | tf_op jit(solution)/shard_map/ppermute | solution.py:17
  8.7 6.4 %collective-permute-start.6 = (bf16[2,2,4224]{2,1,0:T(2,128)(2,1)S(1)}, bf16[2,2,4224]{2,1,0:T(2,128)(2,1)S(1)}, u32[]{:S(2)}, u32[]{:S(2)}) collective-permute-start(bf16[2,2,4224]{2,1,0:T(2,128)(2,1)S(1)} %pad_maximum_fusion.2), channel_id=1, source_target_pairs={{0,6},{1,7},{2,4},{3,5},{4,2},{5,3},{6,0},{7,1},{8,14},{9,15},{10,... | collective-permute-start | bytes 101384 | tf_op jit(solution)/shard_map/ppermute | solution.py:17
  11.2 3.9 %collective-permute-start.4 = (bf16[2,2,4224]{2,1,0:T(2,128)(2,1)S(1)}, bf16[2,2,4224]{2,1,0:T(2,128)(2,1)S(1)}, u32[]{:S(2)}, u32[]{:S(2)}) collective-permute-start(bf16[2,2,4224]{2,1,0:T(2,128)(2,1)S(1)} %pad_maximum_fusion.2), channel_id=1, source_target_pairs={{0,4},{4,0},{8,12},{12,8},{1,5},{5,1},{9,13},{13,9},{2,6},{6,2},{1... | collective-permute-start | bytes 101384 | tf_op jit(solution)/shard_map/ppermute | solution.py:17
  11.9 4.0 %collective-permute-start.5 = (bf16[2,2,4224]{2,1,0:T(2,128)(2,1)S(1)}, bf16[2,2,4224]{2,1,0:T(2,128)(2,1)S(1)}, u32[]{:S(2)}, u32[]{:S(2)}) collective-permute-start(bf16[2,2,4224]{2,1,0:T(2,128)(2,1)S(1)} %pad_maximum_fusion.1.x_ref), channel_id=1, source_target_pairs={{0,2},{1,3},{2,0},{3,1},{4,6},{5,7},{6,4},{7,5},{8,10},{9,11},{10,... | collective-permute-start | bytes 101384 | tf_op jit(solution)/shard_map/ppermute | solution.py:17
  12.3 2.7 %copy-start.6 = (bf16[96,4096]{1,0:T(8,128)(2,1)}, bf16[96,4096]{1,0:T(8,128)(2,1)S(1)}, u32[]{:S(2)}) copy-start(bf16[96,4096]{1,0:T(8,128)(2,1)S(1)} %collective-permute-done.3.refs_2_.refs_5_) | copy-start | bytes 2359300
  12.3 2.7 %copy-start.3 = (bf16[1024,1024]{1,0:T(8,128)(2,1)}, bf16[1024,1024]{1,0:T(8,128)(2,1)S(1)}, u32[]{:S(2)}) copy-start(bf16[1024,1024]{1,0:T(8,128)(2,1)S(1)} %collective-permute-done.2.refs_1_.refs_3_) | copy-start | bytes 6291460
  12.4 2.6 %copy-start.1 = (bf16[1,4096,256]{2,1,0:T(8,128)(2,1)S(1)}, bf16[1,4096,256]{2,1,0:T(8,128)(2,1)}, u32[]{:S(2)}) copy-start(bf16[1,4096,256]{2,1,0:T(8,128)(2,1)} %param.16) | copy-start | bytes 6291460
  15.0 1.3 %copy-start.5 = (bf16[1,6,16,4096]{3,2,1,0:T(8,128)(2,1)S(1)}, bf16[1,6,16,4096]{3,2,1,0:T(8,128)(2,1)}, u32[]{:S(2)}) copy-start(bf16[1,6,16,4096]{3,2,1,0:T(8,128)(2,1)} %param.18) | copy-start | bytes 2359300
  15.0 2.6 %copy-start.9 = (bf16[1,6,16,1024]{3,2,1,0:T(8,128)(2,1)S(1)}, bf16[1,6,16,1024]{3,2,1,0:T(8,128)(2,1)}, u32[]{:S(2)}) copy-start(bf16[1,6,16,1024]{3,2,1,0:T(8,128)(2,1)} %param.19) | copy-start | bytes 589828
  16.2 1.6 %copy-start.2 = (bf16[1,4096,256]{2,1,0:T(8,128)(2,1)S(1)}, bf16[1,4096,256]{2,1,0:T(8,128)(2,1)}, u32[]{:S(2)}) copy-start(bf16[1,4096,256]{2,1,0:T(8,128)(2,1)} %param.16) | copy-start | bytes 6291460
  16.2 1.8 %copy-start.7 = (bf16[96,4096]{1,0:T(8,128)(2,1)S(1)}, bf16[96,4096]{1,0:T(8,128)(2,1)}, u32[]{:S(2)}) copy-start(bf16[96,4096]{1,0:T(8,128)(2,1)} %copy-done.6) | copy-start | bytes 2359300
  16.2 1.4 %collective-permute-start.7 = (bf16[16,4224]{1,0:T(8,128)(2,1)S(1)}, bf16[16,4224]{1,0:T(8,128)(2,1)S(1)}, u32[]{:S(2)}, u32[]{:S(2)}) collective-permute-start(bf16[16,4224]{1,0:T(8,128)(2,1)S(1)} %reshape.28.x_ref), channel_id=1, source_target_pairs={{0,1},{1,0},{2,3},{3,2},{4,5},{5,4},{6,7},{7,6},{8,9},{9,8},{10,11... | collective-permute-start | bytes 405512 | tf_op jit(solution)/shard_map/ppermute | solution.py:17
  16.3 7.2 %copy-start.4 = (bf16[1024,1024]{1,0:T(8,128)(2,1)S(1)}, bf16[1024,1024]{1,0:T(8,128)(2,1)}, u32[]{:S(2)}) copy-start(bf16[1024,1024]{1,0:T(8,128)(2,1)} %copy-done.3) | copy-start | bytes 6291460
  16.3 7.2 %copy-start.8 = (bf16[1,1024,1024]{2,1,0:T(8,128)(2,1)S(1)}, bf16[1,1024,1024]{2,1,0:T(8,128)(2,1)}, u32[]{:S(2)}) copy-start(bf16[1,1024,1024]{2,1,0:T(8,128)(2,1)} %param.17) | copy-start | bytes 6291460
  19.4 15.8 %copy-start.10 = (f32[8,8]{1,0:T(8,128)S(1)}, f32[8,8]{1,0:T(8,128)}, u32[]{:S(2)}) copy-start(f32[8,8]{1,0:T(8,128)} %get-tuple-element.10.refs_0_) | copy-start | bytes 772
  19.4 4.2 %collective-permute-start.8 = (bf16[32,768]{1,0:T(8,128)(2,1)S(1)}, bf16[32,768]{1,0:T(8,128)(2,1)S(1)}, u32[]{:S(2)}, u32[]{:S(2)}) collective-permute-start(bf16[32,768]{1,0:T(8,128)(2,1)S(1)} %shard_map.104.refs_0_), channel_id=1, source_target_pairs={{0,2},{1,3},{2,0},{3,1},{4,6},{5,7},{6,4},{7,5},{8,10},{9,11},{10,... | collective-permute-start | bytes 147464 | tf_op jit(solution)/shard_map/ppermute | solution.py:17
  24.0 1.3 %collective-permute-start.9 = (bf16[16,2048]{1,0:T(8,128)(2,1)S(1)}, bf16[16,2048]{1,0:T(8,128)(2,1)S(1)}, u32[]{:S(2)}, u32[]{:S(2)}) collective-permute-start(bf16[16,2048]{1,0:T(8,128)(2,1)S(1)} %get-tuple-element.14), channel_id=1, source_target_pairs={{0,1},{1,0},{2,3},{3,2},{4,5},{5,4},{6,7},{7,6},{8,9},{9,8},{10,11... | collective-permute-start | bytes 196616 | tf_op jit(solution)/shard_map/ppermute | solution.py:17
  25.4 4.7 %collective-permute-start.12 = (bf16[4,2048]{1,0:T(4,128)(2,1)S(1)}, bf16[4,2048]{1,0:T(4,128)(2,1)S(1)}, u32[]{:S(2)}, u32[]{:S(2)}) collective-permute-start(bf16[4,2048]{1,0:T(4,128)(2,1)S(1)} %get-tuple-element.20), channel_id=1, source_target_pairs={{0,6},{1,7},{2,4},{3,5},{4,2},{5,3},{6,0},{7,1},{8,14},{9,15},{10,... | collective-permute-start | bytes 49160 | tf_op jit(solution)/shard_map/ppermute | solution.py:17
  27.1 3.7 %collective-permute-start.11 = (bf16[4,2048]{1,0:T(4,128)(2,1)S(1)}, bf16[4,2048]{1,0:T(4,128)(2,1)S(1)}, u32[]{:S(2)}, u32[]{:S(2)}) collective-permute-start(bf16[4,2048]{1,0:T(4,128)(2,1)S(1)} %get-tuple-element.21), channel_id=1, source_target_pairs={{0,2},{1,3},{2,0},{3,1},{4,6},{5,7},{6,4},{7,5},{8,10},{9,11},{10,... | collective-permute-start | bytes 49160 | tf_op jit(solution)/shard_map/ppermute | solution.py:17
  28.3 3.7 %collective-permute-start.10 = (bf16[4,2048]{1,0:T(4,128)(2,1)S(1)}, bf16[4,2048]{1,0:T(4,128)(2,1)S(1)}, u32[]{:S(2)}, u32[]{:S(2)}) collective-permute-start(bf16[4,2048]{1,0:T(4,128)(2,1)S(1)} %get-tuple-element.22), channel_id=1, source_target_pairs={{0,4},{4,0},{8,12},{12,8},{1,5},{5,1},{9,13},{13,9},{2,6},{6,2},{1... | collective-permute-start | bytes 49160 | tf_op jit(solution)/shard_map/ppermute | solution.py:17
  32.2 5.2 %collective-permute-start.13 = (bf16[2,2,4096]{2,1,0:T(2,128)(2,1)S(1)}, bf16[2,2,4096]{2,1,0:T(2,128)(2,1)S(1)}, u32[]{:S(2)}, u32[]{:S(2)}) collective-permute-start(bf16[2,2,4096]{2,1,0:T(2,128)(2,1)S(1)} %pad_maximum_fusion.4), channel_id=1, source_target_pairs={{0,8},{4,12},{8,0},{12,4},{1,9},{5,13},{9,1},{13,5},{2,10},{6,14},... | collective-permute-start | bytes 98312 | tf_op jit(solution)/shard_map/ppermute | solution.py:17

commit v7 on v5

--- a/solution.py
+++ b/solution.py
@@ -177,19 +177,30 @@
         send_ref[:, (1 - k) * part : (2 - k) * part] = out[rows // 2 :].astype(BF)
 
 
-def mix_kernel(n_dp, part, mix_ref, kept_ref, came_ref, out_ref):
+def weighted(mix_ref, x_ref, first, lanes):
+    mix = mix_ref[...]
+    blocks, cap = x_ref.shape[:2]
+    total = jnp.zeros((mix.shape[0], lanes.stop - lanes.start), F32)
+    for r in range(blocks):
+        x = x_ref[r, :, lanes].astype(F32)
+        for c in range(cap):
+            at = first + r * cap + c
+            total += mix[:, at : at + 1] * x[c : c + 1]
+    return total
+
+
+def half_mix_kernel(part, mix_ref, kept_ref, out_ref):
+    for at in range(0, out_ref.shape[1], part):
+        lanes = slice(at, at + part)
+        out_ref[:, lanes] = weighted(mix_ref, kept_ref, 0, lanes)
+
+
+def mix_kernel(n_dp, part, mix_ref, half_ref, came_ref, out_ref):
     col = lax.axis_index("dp")
-    mix = mix_ref[...]
-    blocks, cap = kept_ref.shape[:2]
+    first = came_ref.shape[0] * came_ref.shape[1]
     for p in range(n_dp):
         lanes = slice(p * part, (p + 1) * part)
-        total = jnp.zeros((mix.shape[0], part), F32)
-        for i, ref in enumerate((kept_ref, came_ref)):
-            for r in range(blocks):
-                x = ref[r, :, lanes].astype(F32)
-                for c in range(cap):
-                    at = (i * blocks + r) * cap + c
-                    total += mix[:, at : at + 1] * x[c : c + 1]
+        total = half_ref[:, lanes] + weighted(mix_ref, came_ref, first, lanes)
         out_ref[:, pl.ds(pl.multiple_of((p ^ col) * part, part), part)] = total.astype(BF)
 
 
@@ -277,9 +288,9 @@
             state = stage(state, "expert", n_exp, mask, 0)
         even = jnp.concatenate([state[r] for r in range(0, n_exp, 2)], axis=0)
         odd = jnp.concatenate([state[r] for r in range(1, n_exp, 2)], axis=0)
-        beside = swap(even, "dp", n_dp, 2)
         across = swap(odd, "expert", n_exp, 1)
         corner = swap(odd, both_axes, n_all, n_dp | 2)
+        beside = swap(even, "dp", n_dp, 2)
         even = hold(hold(even, expand2, down2), gate_w, up_w)
         own = jnp.concatenate([even, across, beside, corner], axis=0)
         own = own.reshape(2 * block, width + TAIL)
@@ -349,11 +360,21 @@
         kept = jnp.concatenate([state[r] for r in range(middle)], axis=0)
         sent = jnp.concatenate([state[r] for r in range(middle, n_exp)], axis=0)
         came = swap(sent, "expert", n_exp, middle)
+        mixed = call(
+            lambda *refs: half_mix_kernel(part, *refs),
+            shape((tok_count, n_dp * part), F32),
+            2,
+            cost_estimate=pl.CostEstimate(
+                flops=2 * tok_count * middle * cap * n_dp * part,
+                bytes_accessed=4 * tok_count * n_dp * part,
+                transcendentals=0,
+            ),
+        )(mix, kept)
         return call(
             lambda *refs: mix_kernel(n_dp, part, *refs),
             shape((tok_count, n_dp * part), BF),
             3,
-        )(mix, kept, came)
+        )(mix, mixed, came)
 
     return per_device
 

time: 38.5 us -> 38.4 us (level)
  transfers between devices with their start and end apart: 14 -> 14, of which waited for: 11 -> 11; matrix products, arithmetic and copies ran while one was open for 2% -> 2% of each run, Pallas kernels for 2% -> 3%
where the time goes in v7:
time: 38.4 us; the launch traced here: 38.2 us
  starting transfers between devices  15.8 us (41%)
  waiting for transfers between devices  13.7 us (36%)
  Pallas kernels  4.78 us (12%)
  local copies, waits for them, and re-layouts  3.29 us (9%)
  other arithmetic  0.45 us (1%)
    ppermute x14, starting transfers between devices, swap(): return lax.ppermute(x, axis, [(i, i ^ mask) for i in range(size)])  15.8 us
    ppermute x14, waiting for transfers between devices, swap(): return lax.ppermute(x, axis, [(i, i ^ mask) for i in range(size)])  13.7 us
    unnamed x18, local copies, waits for them, and re-layouts  2.37 us
    pallas_call x1, Pallas kernels, per_device(): call(slot_kernel, (shape((middle, cap, width + TAIL), BF),) * 2 + (shape(...  2.06 us
    pallas_call x1, Pallas kernels, per_device(): call(lambda *refs: expert_kernel(n_dp, *refs), shape((rows, 2 * hid), F32...  0.84 us
  transfers between devices with their start and end apart: 14, of which 11 were waited for; matrix products, arithmetic and copies ran while one was open for 2% of the time, Pallas kernels for 3%

profile of v7, /device:TPU:0, one launch (start us, length us, event | category | flops | bytes accessed | tf_op | source)
XLA Modules:
  0.0 38.2 jit_solution(4483876155770302500)
XLA Ops:
  0.0 2.1 %shard_map.100 = (bf16[2,2,4224]{2,1,0:T(2,128)(2,1)}, bf16[2,2,4224]{2,1,0:T(2,128)(2,1)}, f32[8,8]{1,0:T(8,128)}) custom-call(bf16[8,4096]{1,0:T(8,128)(2,1)} %tok_ref.1, s32[8,8]{1,0:T(8,128)} %routing_ref.1, s32[8,8]{1,0:T(8,128)} %gate_ref.1, s32[8]{0:T(128)} %tenant_ref.1, s32[4,24]{1,0:T(4,128)} %lookup_ref.1), custom_call_target="tpu_custom_call" | custom-call | tf_op jit(solution)/shard_map/pallas_call | solution.py:269
  2.1 4.0 %collective-permute-start = (bf16[2,2,4224]{2,1,0:T(2,128)(2,1)}, bf16[2,2,4224]{2,1,0:T(2,128)(2,1)S(1)}, u32[]{:S(2)}, u32[]{:S(2)}) collective-permute-start(bf16[2,2,4224]{2,1,0:T(2,128)(2,1)} %get-tuple-element.12), channel_id=1, source_target_pairs={{0,8},{4,12},{8,0},{12,4},{1,9},{5,13},{9,1},{13,5},{2,10},{6,14},... | collective-permute-start | bytes 101384 | tf_op jit(solution)/shard_map/ppermute | solution.py:17
  6.1 0.5 %collective-permute-start.2 = (bf16[1024,1024]{1,0:T(8,128)(2,1)}, bf16[1024,1024]{1,0:T(8,128)(2,1)S(1)}, u32[]{:S(2)}, u32[]{:S(2)}) collective-permute-start(bf16[1024,1024]{1,0:T(8,128)(2,1)} %bitcast.20), channel_id=1, source_target_pairs={{0,1},{1,0},{2,3},{3,2},{4,5},{5,4},{6,7},{7,6},{8,9},{9,8},{10,11... | collective-permute-start | bytes 6291464 | tf_op jit(solution)/shard_map/ppermute | solution.py:17
  6.6 0.8 %fusion.1 = (bf16[1,2,4224]{2,1,0:T(2,128)(2,1)S(1)}, bf16[1,2,4224]{2,1,0:T(2,128)(2,1)S(1)}) fusion(bf16[2,2,4224]{2,1,0:T(2,128)(2,1)} %get-tuple-element.11), kind=kLoop, calls=%fused_computation.12 | loop fusion | bytes 67584 | tf_op jit(solution)/shard_map/slice | solution.py:279
  7.4 1.2 %collective-permute-done = bf16[2,2,4224]{2,1,0:T(2,128)(2,1)S(1)} collective-permute-done((bf16[2,2,4224]{2,1,0:T(2,128)(2,1)}, bf16[2,2,4224]{2,1,0:T(2,128)(2,1)S(1)}, u32[]{:S(2)}, u32[]{:S(2)}) %collective-permute-start) | collective-permute-done | bytes 33824 | tf_op jit(solution)/shard_map/ppermute | solution.py:17
  8.7 2.5 %collective-permute-start.5 = (bf16[2,2,4224]{2,1,0:T(2,128)(2,1)S(1)}, bf16[2,2,4224]{2,1,0:T(2,128)(2,1)S(1)}, u32[]{:S(2)}, u32[]{:S(2)}) collective-permute-start(bf16[2,2,4224]{2,1,0:T(2,128)(2,1)S(1)} %pad_maximum_fusion.2), channel_id=1, source_target_pairs={{0,6},{1,7},{2,4},{3,5},{4,2},{5,3},{6,0},{7,1},{8,14},{9,15},{10,... | collective-permute-start | bytes 101384 | tf_op jit(solution)/shard_map/ppermute | solution.py:17
  11.2 0.7 %collective-permute-start.3 = (bf16[2,2,4224]{2,1,0:T(2,128)(2,1)S(1)}, bf16[2,2,4224]{2,1,0:T(2,128)(2,1)S(1)}, u32[]{:S(2)}, u32[]{:S(2)}) collective-permute-start(bf16[2,2,4224]{2,1,0:T(2,128)(2,1)S(1)} %pad_maximum_fusion.2), channel_id=1, source_target_pairs={{0,4},{4,0},{8,12},{12,8},{1,5},{5,1},{9,13},{13,9},{2,6},{6,2},{1... | collective-permute-start | bytes 101384 | tf_op jit(solution)/shard_map/ppermute | solution.py:17
  11.9 0.4 %collective-permute-start.4 = (bf16[2,2,4224]{2,1,0:T(2,128)(2,1)S(1)}, bf16[2,2,4224]{2,1,0:T(2,128)(2,1)S(1)}, u32[]{:S(2)}, u32[]{:S(2)}) collective-permute-start(bf16[2,2,4224]{2,1,0:T(2,128)(2,1)S(1)} %pad_maximum_fusion.1.x_ref), channel_id=1, source_target_pairs={{0,2},{1,3},{2,0},{3,1},{4,6},{5,7},{6,4},{7,5},{8,10},{9,11},{10,... | collective-permute-start | bytes 101384 | tf_op jit(solution)/shard_map/ppermute | solution.py:17
  12.4 2.3 %copy-done.1 = bf16[1,4096,256]{2,1,0:T(8,128)(2,1)S(1)} copy-done((bf16[1,4096,256]{2,1,0:T(8,128)(2,1)S(1)}, bf16[1,4096,256]{2,1,0:T(8,128)(2,1)}, u32[]{:S(2)}) %copy-start.1) | copy-done | bytes 2097176
  14.7 0.4 %collective-permute-done.3 = bf16[2,2,4224]{2,1,0:T(2,128)(2,1)S(1)} collective-permute-done((bf16[2,2,4224]{2,1,0:T(2,128)(2,1)S(1)}, bf16[2,2,4224]{2,1,0:T(2,128)(2,1)S(1)}, u32[]{:S(2)}, u32[]{:S(2)}) %collective-permute-start.3) | collective-permute-done | bytes 33824 | tf_op jit(solution)/shard_map/ppermute | solution.py:17
  15.1 0.8 %collective-permute-done.4 = bf16[2,2,4224]{2,1,0:T(2,128)(2,1)S(1)} collective-permute-done((bf16[2,2,4224]{2,1,0:T(2,128)(2,1)S(1)}, bf16[2,2,4224]{2,1,0:T(2,128)(2,1)S(1)}, u32[]{:S(2)}, u32[]{:S(2)}) %collective-permute-start.4) | collective-permute-done | bytes 33824 | tf_op jit(solution)/shard_map/ppermute | solution.py:17
  15.9 0.2 pad_maximum_fusion
  16.3 1.3 %collective-permute-done.6.refs_1_ = bf16[16,4224]{1,0:T(8,128)(2,1)S(1)} collective-permute-done((bf16[16,4224]{1,0:T(8,128)(2,1)S(1)}, bf16[16,4224]{1,0:T(8,128)(2,1)S(1)}, u32[]{:S(2)}, u32[]{:S(2)}) %collective-permute-start.6) | collective-permute-done | bytes 135200 | tf_op jit(solution)/shard_map/ppermute | solution.py:17
  17.6 0.4 %shard_map.104.refs_0_ = bf16[32,96]{1,0:T(8,128)(2,1)S(1)} custom-call(bf16[16,4224]{1,0:T(8,128)(2,1)S(1)} %shard_map.103.refs_0_, bf16[16,4224]{1,0:T(8,128)(2,1)S(1)} %collective-permute-done.6.refs_1_, bf16[96,4096]{1,0:T(8,128)(2,1)S(1)} %bitcast.19), custom_call_target="tpu_custom_call" | custom-call | tf_op jit(solution)/shard_map/pallas_call | solution.py:302
  18.0 0.2 collective-permute-start.7
  18.2 0.8 %shard_map.105.refs_4_ = f32[32,512]{1,0:T(8,128)S(1)} custom-call(bf16[16,4224]{1,0:T(8,128)(2,1)S(1)} %shard_map.103.refs_0_, bf16[16,4224]{1,0:T(8,128)(2,1)S(1)} %collective-permute-done.6.refs_1_, bf16[4096,256]{1,0:T(8,128)(2,1)S(1)} %bitcast.15, bf16[4096,256]{1,0:T(8,128)(2,1)S(1)} %bitcast.17), custom_call_target="tpu_custom_call" | custom-call | flops 134217728 | bytes 4194304 | tf_op jit(solution)/shard_map/pallas_call | solution.py:306
  19.1 0.2 collective-permute-done.7.refs_1_
  19.3 0.2 shard_map.106.refs_0_
  19.4 0.8 %collective-permute-start.8 = (bf16[32,768]{1,0:T(8,128)(2,1)S(1)}, bf16[32,768]{1,0:T(8,128)(2,1)S(1)}, u32[]{:S(2)}, u32[]{:S(2)}) collective-permute-start(bf16[32,768]{1,0:T(8,128)(2,1)S(1)} %shard_map.106.refs_0_), channel_id=1, source_target_pairs={{0,2},{1,3},{2,0},{3,1},{4,6},{5,7},{6,4},{7,5},{8,10},{9,11},{10,... | collective-permute-start | bytes 147464 | tf_op jit(solution)/shard_map/ppermute | solution.py:17
  20.3 3.3 %collective-permute-done.8.refs_1_ = bf16[32,768]{1,0:T(8,128)(2,1)S(1)} collective-permute-done((bf16[32,768]{1,0:T(8,128)(2,1)S(1)}, bf16[32,768]{1,0:T(8,128)(2,1)S(1)}, u32[]{:S(2)}, u32[]{:S(2)}) %collective-permute-start.8) | collective-permute-done | bytes 49184 | tf_op jit(solution)/shard_map/ppermute | solution.py:17
  23.6 0.5 %shard_map.107 = (f32[16,2048]{1,0:T(8,128)S(1)}, bf16[16,2048]{1,0:T(8,128)(2,1)S(1)}) custom-call(bf16[32,768]{1,0:T(8,128)(2,1)S(1)} %shard_map.106.refs_0_, bf16[32,768]{1,0:T(8,128)(2,1)S(1)} %collective-permute-done.8.refs_1_, bf16[1024,1024]{1,0:T(8,128)(2,1)S(1)} %bitcast.21, bf16[1024,1024]{1,0:T(8,128)(2,1)S(1)} %copy-done.4), custom_call_target="tpu_custom_call" | custom-call | tf_op jit(solution)/shard_map/pallas_call | solution.py:327
  24.2 1.2 %collective-permute-done.9 = bf16[16,2048]{1,0:T(8,128)(2,1)S(1)} collective-permute-done((bf16[16,2048]{1,0:T(8,128)(2,1)S(1)}, bf16[16,2048]{1,0:T(8,128)(2,1)S(1)}, u32[]{:S(2)}, u32[]{:S(2)}) %collective-permute-start.9) | collective-permute-done | bytes 65568 | tf_op jit(solution)/shard_map/ppermute | solution.py:17
  25.5 1.6 %collective-permute-start.12 = (bf16[4,2048]{1,0:T(4,128)(2,1)S(1)}, bf16[4,2048]{1,0:T(4,128)(2,1)S(1)}, u32[]{:S(2)}, u32[]{:S(2)}) collective-permute-start(bf16[4,2048]{1,0:T(4,128)(2,1)S(1)} %get-tuple-element.20), channel_id=1, source_target_pairs={{0,6},{1,7},{2,4},{3,5},{4,2},{5,3},{6,0},{7,1},{8,14},{9,15},{10,... | collective-permute-start | bytes 49160 | tf_op jit(solution)/shard_map/ppermute | solution.py:17
  27.1 1.3 %collective-permute-start.11 = (bf16[4,2048]{1,0:T(4,128)(2,1)S(1)}, bf16[4,2048]{1,0:T(4,128)(2,1)S(1)}, u32[]{:S(2)}, u32[]{:S(2)}) collective-permute-start(bf16[4,2048]{1,0:T(4,128)(2,1)S(1)} %get-tuple-element.21), channel_id=1, source_target_pairs={{0,2},{1,3},{2,0},{3,1},{4,6},{5,7},{6,4},{7,5},{8,10},{9,11},{10,... | collective-permute-start | bytes 49160 | tf_op jit(solution)/shard_map/ppermute | solution.py:17
  28.3 0.7 %collective-permute-start.10 = (bf16[4,2048]{1,0:T(4,128)(2,1)S(1)}, bf16[4,2048]{1,0:T(4,128)(2,1)S(1)}, u32[]{:S(2)}, u32[]{:S(2)}) collective-permute-start(bf16[4,2048]{1,0:T(4,128)(2,1)S(1)} %get-tuple-element.22), channel_id=1, source_target_pairs={{0,4},{4,0},{8,12},{12,8},{1,5},{5,1},{9,13},{13,9},{2,6},{6,2},{1... | collective-permute-start | bytes 49160 | tf_op jit(solution)/shard_map/ppermute | solution.py:17
  29.0 1.1 %collective-permute-done.12 = bf16[4,2048]{1,0:T(4,128)(2,1)S(1)} collective-permute-done((bf16[4,2048]{1,0:T(4,128)(2,1)S(1)}, bf16[4,2048]{1,0:T(4,128)(2,1)S(1)}, u32[]{:S(2)}, u32[]{:S(2)}) %collective-permute-start.12) | collective-permute-done | bytes 16416 | tf_op jit(solution)/shard_map/ppermute | solution.py:17
  30.2 0.6 %collective-permute-done.11 = bf16[4,2048]{1,0:T(4,128)(2,1)S(1)} collective-permute-done((bf16[4,2048]{1,0:T(4,128)(2,1)S(1)}, bf16[4,2048]{1,0:T(4,128)(2,1)S(1)}, u32[]{:S(2)}, u32[]{:S(2)}) %collective-permute-start.11) | collective-permute-done | bytes 16416 | tf_op jit(solution)/shard_map/ppermute | solution.py:17
  30.8 1.3 %collective-permute-done.10 = bf16[4,2048]{1,0:T(4,128)(2,1)S(1)} collective-permute-done((bf16[4,2048]{1,0:T(4,128)(2,1)S(1)}, bf16[4,2048]{1,0:T(4,128)(2,1)S(1)}, u32[]{:S(2)}, u32[]{:S(2)}) %collective-permute-start.10) | collective-permute-done | bytes 16416 | tf_op jit(solution)/shard_map/ppermute | solution.py:17
  32.2 2.9 %collective-permute-start.13 = (bf16[2,2,4096]{2,1,0:T(2,128)(2,1)S(1)}, bf16[2,2,4096]{2,1,0:T(2,128)(2,1)S(1)}, u32[]{:S(2)}, u32[]{:S(2)}) collective-permute-start(bf16[2,2,4096]{2,1,0:T(2,128)(2,1)S(1)} %pad_maximum_fusion.4), channel_id=1, source_target_pairs={{0,8},{4,12},{8,0},{12,4},{1,9},{5,13},{9,1},{13,5},{2,10},{6,14},... | collective-permute-start | bytes 98312 | tf_op jit(solution)/shard_map/ppermute | solution.py:17
  35.2 0.1 shard_map.108.refs_1_
  35.3 2.2 %collective-permute-done.13.refs_2_ = bf16[2,2,4096]{2,1,0:T(2,128)(2,1)S(1)} collective-permute-done((bf16[2,2,4096]{2,1,0:T(2,128)(2,1)S(1)}, bf16[2,2,4096]{2,1,0:T(2,128)(2,1)S(1)}, u32[]{:S(2)}, u32[]{:S(2)}) %collective-permute-start.13) | collective-permute-done | bytes 32800 | tf_op jit(solution)/shard_map/ppermute | solution.py:17
  37.5 0.7 %shard_map.109 = bf16[8,4096]{1,0:T(8,128)(2,1)} custom-call(f32[8,8]{1,0:T(8,128)S(1)} %copy-done.8, f32[8,4096]{1,0:T(8,128)S(1)} %shard_map.108.refs_1_, bf16[2,2,4096]{2,1,0:T(2,128)(2,1)S(1)} %collective-permute-done.13.refs_2_), custom_call_target="tpu_custom_call" | custom-call | tf_op jit(solution)/shard_map/pallas_call | solution.py:373
  (36 shorter events, 0.6 us)
Async XLA Ops:
  0.0 12.4 %copy-start = (bf16[1,4096,256]{2,1,0:T(8,128)(2,1)S(1)}, bf16[1,4096,256]{2,1,0:T(8,128)(2,1)}, u32[]{:S(2)}) copy-start(bf16[1,4096,256]{2,1,0:T(8,128)(2,1)} %param.15) | copy-start | bytes 6291460
  2.1 6.5 %collective-permute-start = (bf16[2,2,4224]{2,1,0:T(2,128)(2,1)}, bf16[2,2,4224]{2,1,0:T(2,128)(2,1)S(1)}, u32[]{:S(2)}, u32[]{:S(2)}) collective-permute-start(bf16[2,2,4224]{2,1,0:T(2,128)(2,1)} %get-tuple-element.12), channel_id=1, source_target_pairs={{0,8},{4,12},{8,0},{12,4},{1,9},{5,13},{9,1},{13,5},{2,10},{6,14},... | collective-permute-start | bytes 101384 | tf_op jit(solution)/shard_map/ppermute | solution.py:17
  6.1 6.2 %collective-permute-start.1 = (bf16[96,1024]{1,0:T(8,128)(2,1)}, bf16[96,1024]{1,0:T(8,128)(2,1)S(1)}, u32[]{:S(2)}, u32[]{:S(2)}) collective-permute-start(bf16[96,1024]{1,0:T(8,128)(2,1)} %bitcast.22), channel_id=1, source_target_pairs={{0,1},{1,0},{2,3},{3,2},{4,5},{5,4},{6,7},{7,6},{8,9},{9,8},{10,11... | collective-permute-start | bytes 589832 | tf_op jit(solution)/shard_map/ppermute | solution.py:17
  6.1 6.2 %collective-permute-start.2 = (bf16[1024,1024]{1,0:T(8,128)(2,1)}, bf16[1024,1024]{1,0:T(8,128)(2,1)S(1)}, u32[]{:S(2)}, u32[]{:S(2)}) collective-permute-start(bf16[1024,1024]{1,0:T(8,128)(2,1)} %bitcast.20), channel_id=1, source_target_pairs={{0,1},{1,0},{2,3},{3,2},{4,5},{5,4},{6,7},{7,6},{8,9},{9,8},{10,11... | collective-permute-start | bytes 6291464 | tf_op jit(solution)/shard_map/ppermute | solution.py:17
  8.7 6.1 %collective-permute-start.5 = (bf16[2,2,4224]{2,1,0:T(2,128)(2,1)S(1)}, bf16[2,2,4224]{2,1,0:T(2,128)(2,1)S(1)}, u32[]{:S(2)}, u32[]{:S(2)}) collective-permute-start(bf16[2,2,4224]{2,1,0:T(2,128)(2,1)S(1)} %pad_maximum_fusion.2), channel_id=1, source_target_pairs={{0,6},{1,7},{2,4},{3,5},{4,2},{5,3},{6,0},{7,1},{8,14},{9,15},{10,... | collective-permute-start | bytes 101384 | tf_op jit(solution)/shard_map/ppermute | solution.py:17
  11.2 3.9 %collective-permute-start.3 = (bf16[2,2,4224]{2,1,0:T(2,128)(2,1)S(1)}, bf16[2,2,4224]{2,1,0:T(2,128)(2,1)S(1)}, u32[]{:S(2)}, u32[]{:S(2)}) collective-permute-start(bf16[2,2,4224]{2,1,0:T(2,128)(2,1)S(1)} %pad_maximum_fusion.2), channel_id=1, source_target_pairs={{0,4},{4,0},{8,12},{12,8},{1,5},{5,1},{9,13},{13,9},{2,6},{6,2},{1... | collective-permute-start | bytes 101384 | tf_op jit(solution)/shard_map/ppermute | solution.py:17
  11.9 4.0 %collective-permute-start.4 = (bf16[2,2,4224]{2,1,0:T(2,128)(2,1)S(1)}, bf16[2,2,4224]{2,1,0:T(2,128)(2,1)S(1)}, u32[]{:S(2)}, u32[]{:S(2)}) collective-permute-start(bf16[2,2,4224]{2,1,0:T(2,128)(2,1)S(1)} %pad_maximum_fusion.1.x_ref), channel_id=1, source_target_pairs={{0,2},{1,3},{2,0},{3,1},{4,6},{5,7},{6,4},{7,5},{8,10},{9,11},{10,... | collective-permute-start | bytes 101384 | tf_op jit(solution)/shard_map/ppermute | solution.py:17
  12.3 2.4 %copy-start.3 = (bf16[1024,1024]{1,0:T(8,128)(2,1)}, bf16[1024,1024]{1,0:T(8,128)(2,1)S(1)}, u32[]{:S(2)}) copy-start(bf16[1024,1024]{1,0:T(8,128)(2,1)S(1)} %collective-permute-done.2.refs_1_.refs_3_) | copy-start | bytes 6291460
  12.4 2.3 %copy-start.1 = (bf16[1,4096,256]{2,1,0:T(8,128)(2,1)S(1)}, bf16[1,4096,256]{2,1,0:T(8,128)(2,1)}, u32[]{:S(2)}) copy-start(bf16[1,4096,256]{2,1,0:T(8,128)(2,1)} %param.16) | copy-start | bytes 6291460
  14.7 1.6 %copy-start.5 = (bf16[1,6,16,4096]{3,2,1,0:T(8,128)(2,1)S(1)}, bf16[1,6,16,4096]{3,2,1,0:T(8,128)(2,1)}, u32[]{:S(2)}) copy-start(bf16[1,6,16,4096]{3,2,1,0:T(8,128)(2,1)} %param.18) | copy-start | bytes 2359300
  14.7 1.6 %copy-start.7 = (bf16[1,6,16,1024]{3,2,1,0:T(8,128)(2,1)S(1)}, bf16[1,6,16,1024]{3,2,1,0:T(8,128)(2,1)}, u32[]{:S(2)}) copy-start(bf16[1,6,16,1024]{3,2,1,0:T(8,128)(2,1)} %param.19) | copy-start | bytes 589828
  16.2 1.4 %collective-permute-start.6 = (bf16[16,4224]{1,0:T(8,128)(2,1)S(1)}, bf16[16,4224]{1,0:T(8,128)(2,1)S(1)}, u32[]{:S(2)}, u32[]{:S(2)}) collective-permute-start(bf16[16,4224]{1,0:T(8,128)(2,1)S(1)} %reshape.27.x_ref), channel_id=1, source_target_pairs={{0,1},{1,0},{2,3},{3,2},{4,5},{5,4},{6,7},{7,6},{8,9},{9,8},{10,11... | collective-permute-start | bytes 405512 | tf_op jit(solution)/shard_map/ppermute | solution.py:17
  16.3 2.0 %copy-start.2 = (bf16[1,4096,256]{2,1,0:T(8,128)(2,1)S(1)}, bf16[1,4096,256]{2,1,0:T(8,128)(2,1)}, u32[]{:S(2)}) copy-start(bf16[1,4096,256]{2,1,0:T(8,128)(2,1)} %param.16) | copy-start | bytes 6291460
  18.0 5.6 %copy-start.4 = (bf16[1024,1024]{1,0:T(8,128)(2,1)S(1)}, bf16[1024,1024]{1,0:T(8,128)(2,1)}, u32[]{:S(2)}) copy-start(bf16[1024,1024]{1,0:T(8,128)(2,1)} %copy-done.3) | copy-start | bytes 6291460
  18.0 5.6 %copy-start.6 = (bf16[1,1024,1024]{2,1,0:T(8,128)(2,1)S(1)}, bf16[1,1024,1024]{2,1,0:T(8,128)(2,1)}, u32[]{:S(2)}) copy-start(bf16[1,1024,1024]{2,1,0:T(8,128)(2,1)} %param.17) | copy-start | bytes 6291460
  18.0 1.2 %collective-permute-start.7 = (bf16[32,96]{1,0:T(8,128)(2,1)S(1)}, bf16[32,96]{1,0:T(8,128)(2,1)S(1)}, u32[]{:S(2)}, u32[]{:S(2)}) collective-permute-start(bf16[32,96]{1,0:T(8,128)(2,1)S(1)} %shard_map.104.refs_0_), channel_id=1, source_target_pairs={{0,1},{1,0},{2,3},{3,2},{4,5},{5,4},{6,7},{7,6},{8,9},{9,8},{10,11... | collective-permute-start | bytes 18440 | tf_op jit(solution)/shard_map/ppermute | solution.py:17
  19.4 15.8 %copy-start.8 = (f32[8,8]{1,0:T(8,128)S(1)}, f32[8,8]{1,0:T(8,128)}, u32[]{:S(2)}) copy-start(f32[8,8]{1,0:T(8,128)} %get-tuple-element.10.refs_0_) | copy-start | bytes 772
  19.4 4.2 %collective-permute-start.8 = (bf16[32,768]{1,0:T(8,128)(2,1)S(1)}, bf16[32,768]{1,0:T(8,128)(2,1)S(1)}, u32[]{:S(2)}, u32[]{:S(2)}) collective-permute-start(bf16[32,768]{1,0:T(8,128)(2,1)S(1)} %shard_map.106.refs_0_), channel_id=1, source_target_pairs={{0,2},{1,3},{2,0},{3,1},{4,6},{5,7},{6,4},{7,5},{8,10},{9,11},{10,... | collective-permute-start | bytes 147464 | tf_op jit(solution)/shard_map/ppermute | solution.py:17
  24.1 1.3 %collective-permute-start.9 = (bf16[16,2048]{1,0:T(8,128)(2,1)S(1)}, bf16[16,2048]{1,0:T(8,128)(2,1)S(1)}, u32[]{:S(2)}, u32[]{:S(2)}) collective-permute-start(bf16[16,2048]{1,0:T(8,128)(2,1)S(1)} %get-tuple-element.14), channel_id=1, source_target_pairs={{0,1},{1,0},{2,3},{3,2},{4,5},{5,4},{6,7},{7,6},{8,9},{9,8},{10,11... | collective-permute-start | bytes 196616 | tf_op jit(solution)/shard_map/ppermute | solution.py:17
  25.5 4.7 %collective-permute-start.12 = (bf16[4,2048]{1,0:T(4,128)(2,1)S(1)}, bf16[4,2048]{1,0:T(4,128)(2,1)S(1)}, u32[]{:S(2)}, u32[]{:S(2)}) collective-permute-start(bf16[4,2048]{1,0:T(4,128)(2,1)S(1)} %get-tuple-element.20), channel_id=1, source_target_pairs={{0,6},{1,7},{2,4},{3,5},{4,2},{5,3},{6,0},{7,1},{8,14},{9,15},{10,... | collective-permute-start | bytes 49160 | tf_op jit(solution)/shard_map/ppermute | solution.py:17
  27.1 3.7 %collective-permute-start.11 = (bf16[4,2048]{1,0:T(4,128)(2,1)S(1)}, bf16[4,2048]{1,0:T(4,128)(2,1)S(1)}, u32[]{:S(2)}, u32[]{:S(2)}) collective-permute-start(bf16[4,2048]{1,0:T(4,128)(2,1)S(1)} %get-tuple-element.21), channel_id=1, source_target_pairs={{0,2},{1,3},{2,0},{3,1},{4,6},{5,7},{6,4},{7,5},{8,10},{9,11},{10,... | collective-permute-start | bytes 49160 | tf_op jit(solution)/shard_map/ppermute | solution.py:17
  28.3 3.7 %collective-permute-start.10 = (bf16[4,2048]{1,0:T(4,128)(2,1)S(1)}, bf16[4,2048]{1,0:T(4,128)(2,1)S(1)}, u32[]{:S(2)}, u32[]{:S(2)}) collective-permute-start(bf16[4,2048]{1,0:T(4,128)(2,1)S(1)} %get-tuple-element.22), channel_id=1, source_target_pairs={{0,4},{4,0},{8,12},{12,8},{1,5},{5,1},{9,13},{13,9},{2,6},{6,2},{1... | collective-permute-start | bytes 49160 | tf_op jit(solution)/shard_map/ppermute | solution.py:17
  32.2 5.2 %collective-permute-start.13 = (bf16[2,2,4096]{2,1,0:T(2,128)(2,1)S(1)}, bf16[2,2,4096]{2,1,0:T(2,128)(2,1)S(1)}, u32[]{:S(2)}, u32[]{:S(2)}) collective-permute-start(bf16[2,2,4096]{2,1,0:T(2,128)(2,1)S(1)} %pad_maximum_fusion.4), channel_id=1, source_target_pairs={{0,8},{4,12},{8,0},{12,4},{1,9},{5,13},{9,1},{13,5},{2,10},{6,14},... | collective-permute-start | bytes 98312 | tf_op jit(solution)/shard_map/ppermute | solution.py:17
